TPU v7x, 32 devices: a whole 2x2x4 slice. The times are simulated.
32 devices in a mesh: dp: 4 (over y, core), mp: 8 (over z, x).
Axes of the slice: x: 2, y: 2, z: 4, core: 2. Of those that a mesh axis runs over, the one named last changes fastest.
Arguments:
- patches: bfloat16 [18432, 1024], P(('dp', 'mp')), may hold values from -6 to 6
- grid_sizes: int32 [32], P(('dp', 'mp')), may hold values from 16 to 24, as said below
- w_reduce_a: bfloat16 [1024, 256], P(None, 'mp'), may hold values from -0.1875 to 0.1875
- taps_a: bfloat16 [9, 256], P(None, 'mp'), may hold values from -2 to 2
- w_expand_a: bfloat16 [256, 1024], P('mp'), may hold values from -0.375 to 0.375
- gain_a: bfloat16 [1024], P('mp'), may hold values from 0.099609375 to 1.8984375
- w_reduce_b: bfloat16 [1024, 256], P(None, 'mp'), may hold values from -0.1875 to 0.1875
- taps_b: bfloat16 [9, 256], P(None, 'mp'), may hold values from -2 to 2
- w_expand_b: bfloat16 [256, 1024], P('mp'), may hold values from -0.375 to 0.375
- gain_b: bfloat16 [1024], P('mp'), may hold values from 0.099609375 to 1.8984375
- w_in: bfloat16 [1024, 4096], P(None, 'mp'), may hold values from -0.1875 to 0.1875
- w_out: bfloat16 [4096, 4096], P('mp'), may hold values from -0.09375 to 0.09375
- d_tokens: bfloat16 [4608, 4096], P(('dp', 'mp')), may hold values from -6 to 6
Outputs:
- tokens: bfloat16 [4608, 4096], P(('dp', 'mp'))
- d_patches: float32 [18432, 1024], P(('dp', 'mp'))
- grad_reduce_a: float32 [1024, 256], P(None, 'mp')
- grad_taps_a: float32 [9, 256], P(None, 'mp')
- grad_expand_a: float32 [256, 1024], P('mp')
- grad_gain_a: float32 [1024], P('mp')
- grad_reduce_b: float32 [1024, 256], P(None, 'mp')
- grad_taps_b: float32 [9, 256], P(None, 'mp')
- grad_expand_b: float32 [256, 1024], P('mp')
- grad_gain_b: float32 [1024], P('mp')
- grad_in: float32 [1024, 4096], P(None, 'mp')
- grad_out: float32 [4096, 4096], P('mp')
Inputs may be any that keep to these rules, and one draw needn't show every extreme that they name: `grid_sizes`: each value is 16 or 24; an image of side 16 holds its features in the top-left 16 x 16 cells of its 24 x 24 rows, and its other rows are read by nothing.
All inputs are finite; a program needn't handle non-finite values.
Results may differ from a plain program's by a relative error of at most 0.02.
Values may be sent and summed in bfloat16 or wider, within the bound.
A program may use at most 320 MiB of HBM per device.

v0:
```python
import jax
import jax.numpy as jnp
from jax import lax
from jax.sharding import PartitionSpec as P

GRID = 24
SMALL_GRID = 16
POOL = 12


epsilon = 1e-05
highest = lax.Precision.HIGHEST
root_half = 0.7071067811865476
inv_root_tau = 0.3989422804014327


def silu_slope(values):
    sigmoid = jax.nn.sigmoid(values)
    return sigmoid * (1.0 + values * (1.0 - sigmoid))


def gelu_exact(values):
    return 0.5 * values * (1.0 + lax.erf(values * root_half))


def gelu_slope(values):
    return (
        0.5 * (1.0 + lax.erf(values * root_half))
        + values * jnp.exp(-0.5 * values * values) * inv_root_tau
    )


def outer_rows(left, right):
    return lax.dot_general(
        left, right, (((0,), (0,)), ((), ())), preferred_element_type=jnp.float32
    )


def times_trans(left, right):
    return lax.dot_general(
        left, right, (((1,), (1,)), ((), ())), preferred_element_type=jnp.float32
    )


def map_padding(ndims):
    return [(0, 0)] * (ndims - 3) + [(1, 1), (1, 1), (0, 0)]


def depthwise(feature_map, tap_weights):
    extent = feature_map.shape[-2]
    padded = jnp.pad(feature_map, map_padding(feature_map.ndim))
    result = jnp.zeros_like(feature_map)
    for tap_row in range(3):
        for tap_col in range(3):
            result = (
                result
                + padded[..., tap_row : tap_row + extent, tap_col : tap_col + extent, :]
                * tap_weights[3 * tap_row + tap_col]
            )
    return result


def depthwise_back(upstream, feature_map, tap_weights):
    extent = upstream.shape[-2]
    upstream_pad = jnp.pad(upstream, map_padding(upstream.ndim))
    feature_pad = jnp.pad(feature_map, map_padding(feature_map.ndim))
    d_feature = jnp.zeros_like(upstream)
    tap_grads = []
    leading = tuple(range(upstream.ndim - 1))
    for tap_row in range(3):
        for tap_col in range(3):
            d_feature = (
                d_feature
                + upstream_pad[
                    ..., 2 - tap_row : 2 - tap_row + extent, 2 - tap_col : 2 - tap_col + extent, :
                ]
                * tap_weights[3 * tap_row + tap_col]
            )
            shifted = feature_pad[..., tap_row : tap_row + extent, tap_col : tap_col + extent, :]
            tap_grads.append(jnp.sum(shifted * upstream, axis=leading))
    return (d_feature, jnp.stack(tap_grads))


def block_forward(feature_rows, low_rows, weights_set, extent):
    w_reduce, tap_weights, w_expand, norm_gain = weights_set
    channels = w_reduce.shape[1]
    row_count = feature_rows.shape[0]
    reduced = jnp.dot(low_rows, w_reduce, preferred_element_type=jnp.float32)
    activated = jax.nn.silu(reduced).reshape(-1, extent, extent, channels)
    spatial = depthwise(activated, tap_weights.astype(jnp.float32)).reshape(row_count, channels)
    narrow = jax.nn.silu(spatial).astype(jnp.bfloat16)
    widened = jnp.dot(narrow, w_expand, preferred_element_type=jnp.float32)
    centred = widened - jnp.mean(widened, axis=1, keepdims=True)
    inv_scale = lax.rsqrt(jnp.mean(centred * centred, axis=1, keepdims=True) + epsilon)
    normed = centred * inv_scale
    result = feature_rows + normed * norm_gain.astype(jnp.float32)
    return (result, (reduced, activated, spatial, narrow, normed, inv_scale))


def block_backward(d_result, low_rows, weights_set, saved):
    w_reduce, tap_weights, w_expand, norm_gain = weights_set
    reduced, activated, spatial, narrow, normed, inv_scale = saved
    d_gain = jnp.sum(d_result * normed, axis=0)
    d_normed = d_result * norm_gain.astype(jnp.float32)
    d_widened = inv_scale * (
        d_normed
        - jnp.mean(d_normed, axis=1, keepdims=True)
        - normed * jnp.mean(d_normed * normed, axis=1, keepdims=True)
    )
    d_widened = d_widened.astype(jnp.bfloat16)
    grad_expand = outer_rows(narrow, d_widened)
    d_spatial = times_trans(d_widened, w_expand) * silu_slope(spatial)
    d_activated, grad_taps = depthwise_back(
        d_spatial.reshape(activated.shape), activated, tap_weights.astype(jnp.float32)
    )
    d_reduced = (d_activated.reshape(reduced.shape) * silu_slope(reduced)).astype(jnp.bfloat16)
    grad_reduce = outer_rows(low_rows, d_reduced)
    d_rows = d_result + times_trans(d_reduced, w_reduce)
    return (d_rows, (grad_reduce, grad_taps, grad_expand, d_gain))


def crop_rows(pixels, extent):
    features = pixels.shape[-1]
    return pixels.reshape(GRID, GRID, features)[:extent, :extent].reshape(extent * extent, features)


def widen_grid(values, extent):
    features = values.shape[-1]
    return jnp.pad(
        values.reshape(extent, extent, features), ((0, GRID - extent), (0, GRID - extent), (0, 0))
    )


def first_forward(weights_set, extent):

    def compute(pixels):
        cropped = crop_rows(pixels, extent)
        result, unused = block_forward(cropped.astype(jnp.float32), cropped, weights_set, extent)
        return widen_grid(result, extent)

    return compute


def first_backward(weights_set, extent):

    def compute(pixels, upstream):
        cropped = crop_rows(pixels, extent)
        sliced = crop_rows(upstream, extent)
        unused, saved = block_forward(cropped.astype(jnp.float32), cropped, weights_set, extent)
        d_rows, grads = block_backward(sliced, cropped, weights_set, saved)
        return (widen_grid(d_rows, extent).reshape(GRID * GRID, -1), grads)

    return compute


def pool_table(grid_side):
    bin_index = lax.iota(jnp.int32, POOL)
    bin_lower = bin_index * grid_side // POOL
    bin_upper = ((bin_index + 1) * grid_side + POOL - 1) // POOL
    cell_index = lax.iota(jnp.int32, GRID)
    inside = (cell_index[None, :] >= bin_lower[:, None]) & (
        cell_index[None, :] < bin_upper[:, None]
    )
    weights = jnp.where(inside, 1.0, 0.0) / (bin_upper - bin_lower)[:, None]
    return weights.astype(jnp.float32)


def body(
    patches,
    grid_sizes,
    w_reduce_a,
    taps_a,
    w_expand_a,
    gain_a,
    w_reduce_b,
    taps_b,
    w_expand_b,
    gain_b,
    w_in,
    w_out,
    d_tokens,
):
    gathered = (
        lax.all_gather(w_reduce_a, "mp", axis=1, tiled=True),
        lax.all_gather(taps_a, "mp", axis=1, tiled=True),
        lax.all_gather(w_expand_a, "mp", axis=0, tiled=True),
        lax.all_gather(gain_a, "mp", axis=0, tiled=True),
        lax.all_gather(w_reduce_b, "mp", axis=1, tiled=True),
        lax.all_gather(taps_b, "mp", axis=1, tiled=True),
        lax.all_gather(w_expand_b, "mp", axis=0, tiled=True),
        lax.all_gather(gain_b, "mp", axis=0, tiled=True),
    )
    first_set = gathered[0:4]
    second_set = gathered[4:8]
    features = patches.shape[1]
    pictures = patches.reshape(-1, GRID * GRID, features)
    picture_count = pictures.shape[0]
    tables = jax.vmap(pool_table)(grid_sizes)

    def forward_one(element):
        pixels, grid_side, pool_weights = element
        result = lax.cond(
            grid_side == GRID,
            first_forward(first_set, GRID),
            first_forward(first_set, SMALL_GRID),
            pixels,
        )
        return jnp.einsum("ia,jb,abd->ijd", pool_weights, pool_weights, result, precision=highest)

    pooled = lax.map(forward_one, (pictures, grid_sizes, tables))
    pooled_rows = pooled.reshape(picture_count * POOL * POOL, features)
    pooled_low = pooled_rows.astype(jnp.bfloat16)
    mixed_rows, second_saved = block_forward(pooled_rows, pooled_low, second_set, POOL)
    queries = mixed_rows.astype(jnp.bfloat16)
    hidden = jnp.dot(
        lax.all_gather(queries, "mp", axis=0, tiled=True), w_in, preferred_element_type=jnp.float32
    )
    active = gelu_exact(hidden).astype(jnp.bfloat16)
    tokens = lax.psum_scatter(
        jnp.dot(active, w_out, preferred_element_type=jnp.float32).astype(jnp.bfloat16),
        "mp",
        scatter_dimension=0,
        tiled=True,
    )
    piece = lax.all_gather(d_tokens, "mp", axis=0, tiled=True)
    d_part = (times_trans(piece, w_out) * gelu_slope(hidden)).astype(jnp.bfloat16)
    grad_out_sum = outer_rows(active, piece)
    d_hidden = d_part
    d_part = d_hidden
    grad_in_part = outer_rows(lax.all_gather(queries, "mp", axis=0, tiled=True), d_part)
    d_part = d_hidden
    d_mixed = lax.psum_scatter(times_trans(d_part, w_in), "mp", scatter_dimension=0, tiled=True)
    d_pooled, second_grads = block_backward(d_mixed, pooled_low, second_set, second_saved)
    d_pooled = d_pooled.reshape(picture_count, POOL, POOL, features)

    def backward_one(totals, element):
        pixels, grid_side, pool_weights, upstream = element
        d_grid = jnp.einsum(
            "ia,jb,ijd->abd", pool_weights, pool_weights, upstream, precision=highest
        )
        d_pixels, grads = lax.cond(
            grid_side == GRID,
            first_backward(first_set, GRID),
            first_backward(first_set, SMALL_GRID),
            pixels,
            d_grid,
        )
        return (
            tuple((total_part + grad_part for total_part, grad_part in zip(totals, grads))),
            d_pixels,
        )

    zero_grads = tuple((jnp.zeros(weight.shape, jnp.float32) for weight in first_set))
    first_grads, d_pictures = lax.scan(
        backward_one, zero_grads, (pictures, grid_sizes, tables, d_pooled)
    )
    d_patches = d_pictures.reshape(-1, features)
    shards = (
        lax.psum_scatter(
            first_grads[0].astype(jnp.bfloat16), "mp", scatter_dimension=1, tiled=True
        ).astype(jnp.float32),
        lax.psum_scatter(
            first_grads[1].astype(jnp.bfloat16), "mp", scatter_dimension=1, tiled=True
        ).astype(jnp.float32),
        lax.psum_scatter(
            first_grads[2].astype(jnp.bfloat16), "mp", scatter_dimension=0, tiled=True
        ).astype(jnp.float32),
        lax.psum_scatter(
            first_grads[3].astype(jnp.bfloat16), "mp", scatter_dimension=0, tiled=True
        ).astype(jnp.float32),
        lax.psum_scatter(
            second_grads[0].astype(jnp.bfloat16), "mp", scatter_dimension=1, tiled=True
        ).astype(jnp.float32),
        lax.psum_scatter(
            second_grads[1].astype(jnp.bfloat16), "mp", scatter_dimension=1, tiled=True
        ).astype(jnp.float32),
        lax.psum_scatter(
            second_grads[2].astype(jnp.bfloat16), "mp", scatter_dimension=0, tiled=True
        ).astype(jnp.float32),
        lax.psum_scatter(
            second_grads[3].astype(jnp.bfloat16), "mp", scatter_dimension=0, tiled=True
        ).astype(jnp.float32),
    )
    summed = (
        lax.psum(shards[0].astype(jnp.bfloat16), "dp").astype(jnp.float32),
        lax.psum(shards[1].astype(jnp.bfloat16), "dp").astype(jnp.float32),
        lax.psum(shards[2].astype(jnp.bfloat16), "dp").astype(jnp.float32),
        lax.psum(shards[3].astype(jnp.bfloat16), "dp").astype(jnp.float32),
        lax.psum(shards[4].astype(jnp.bfloat16), "dp").astype(jnp.float32),
        lax.psum(shards[5].astype(jnp.bfloat16), "dp").astype(jnp.float32),
        lax.psum(shards[6].astype(jnp.bfloat16), "dp").astype(jnp.float32),
        lax.psum(shards[7].astype(jnp.bfloat16), "dp").astype(jnp.float32),
        lax.psum(grad_in_part.astype(jnp.bfloat16), "dp").astype(jnp.float32),
        lax.psum(grad_out_sum.astype(jnp.bfloat16), "dp").astype(jnp.float32),
    )
    return (
        tokens,
        d_patches,
        summed[0],
        summed[1],
        summed[2],
        summed[3],
        summed[4],
        summed[5],
        summed[6],
        summed[7],
        summed[8],
        summed[9],
    )


def solution(mesh):
    in_specs = (
        P(("dp", "mp"), None),
        P(("dp", "mp")),
        P(None, "mp"),
        P(None, "mp"),
        P("mp", None),
        P("mp"),
        P(None, "mp"),
        P(None, "mp"),
        P("mp", None),
        P("mp"),
        P(None, "mp"),
        P("mp", None),
        P(("dp", "mp"), None),
    )
    out_specs = (
        P(("dp", "mp"), None),
        P(("dp", "mp"), None),
        P(None, "mp"),
        P(None, "mp"),
        P("mp", None),
        P("mp"),
        P(None, "mp"),
        P(None, "mp"),
        P("mp", None),
        P("mp"),
        P(None, "mp"),
        P("mp", None),
    )
    return jax.shard_map(body, mesh=mesh, in_specs=in_specs, out_specs=out_specs, check_vma=False)
```

profile of v0, /device:TPU:0, one launch (start us, length us, event | category | flops | bytes accessed | tf_op | source)
XLA Modules:
  0.0 1229.8 jit_solution(17337222660484581777)
XLA Ops:
  8.0 22.3 %all-gather.1 = bf16[8,1,128]{2,1,0:T(2,128)(2,1)S(1)} all-gather(bf16[1,1,128]{2,1,0:T(2,128)(2,1)} %bitcast.388), channel_id=1, replica_groups=mesh['dp'=4,'mp'=8] {'mp'}, dimensions={0}, use_global_device_ids=true | all-gather | bytes 2304 | tf_op jit(solution)/shard_map/all_gather | solution.py:187
  30.3 16.4 %all-gather.3 = bf16[8,1,128]{2,1,0:T(2,128)(2,1)S(1)} all-gather(bf16[1,1,128]{2,1,0:T(2,128)(2,1)} %bitcast.389), channel_id=1, replica_groups=mesh['dp'=4,'mp'=8] {'mp'}, dimensions={0}, use_global_device_ids=true | all-gather | bytes 2304 | tf_op jit(solution)/shard_map/all_gather | solution.py:191
  46.7 30.5 %all-gather = bf16[8,32,9]{1,2,0:T(8,128)(2,1)S(1)} all-gather(bf16[1,32,9]{1,2,0:T(8,128)(2,1)} %bitcast.368), channel_id=1, replica_groups=mesh['dp'=4,'mp'=8] {'mp'}, dimensions={0}, use_global_device_ids=true | all-gather | bytes 5184 | tf_op jit(solution)/shard_map/all_gather | solution.py:185
  78.0 30.5 %all-gather.2 = bf16[8,32,9]{1,2,0:T(8,128)(2,1)S(1)} all-gather(bf16[1,32,9]{1,2,0:T(8,128)(2,1)} %bitcast.369), channel_id=1, replica_groups=mesh['dp'=4,'mp'=8] {'mp'}, dimensions={0}, use_global_device_ids=true | all-gather | bytes 5184 | tf_op jit(solution)/shard_map/all_gather | solution.py:189
  108.6 33.8 %all_gather.31 = bf16[1024,256]{0,1:T(8,128)(2,1)} all-gather(bf16[1024,32]{0,1:T(8,128)(2,1)} %param.19), channel_id=1, replica_groups=mesh['dp'=4,'mp'=8] {'mp'}, dimensions={1}, use_global_device_ids=true | all-gather | bytes 589824 | tf_op jit(solution)/shard_map/all_gather | solution.py:184
  142.4 31.5 %all_gather.33 = bf16[256,1024]{1,0:T(8,128)(2,1)S(1)} all-gather(bf16[32,1024]{1,0:T(8,128)(2,1)} %param.21), channel_id=1, replica_groups=mesh['dp'=4,'mp'=8] {'mp'}, dimensions={0}, use_global_device_ids=true | all-gather | bytes 589824 | tf_op jit(solution)/shard_map/all_gather | solution.py:186
  173.9 31.8 %all_gather.35 = bf16[1024,256]{0,1:T(8,128)(2,1)S(1)} all-gather(bf16[1024,32]{0,1:T(8,128)(2,1)} %param.23), channel_id=1, replica_groups=mesh['dp'=4,'mp'=8] {'mp'}, dimensions={1}, use_global_device_ids=true | all-gather | bytes 589824 | tf_op jit(solution)/shard_map/all_gather | solution.py:188
  205.7 33.4 %all_gather.37 = bf16[256,1024]{1,0:T(8,128)(2,1)} all-gather(bf16[32,1024]{1,0:T(8,128)(2,1)} %param.25), channel_id=1, replica_groups=mesh['dp'=4,'mp'=8] {'mp'}, dimensions={0}, use_global_device_ids=true | all-gather | bytes 589824 | tf_op jit(solution)/shard_map/all_gather | solution.py:190
  258.8 49.5 %all-gather.7.cloned.1.call-done = bf16[1152,1024]{1,0:T(8,128)(2,1)} async-done(((bf16[144,1024]{1,0:T(8,128)(2,1)}), bf16[1152,1024]{1,0:T(8,128)(2,1)}) %all-gather.7.cloned.1.call-update) | async-done | bytes 2359312 | tf_op jit(solution)/shard_map/all_gather | solution.py:216
  312.7 134.4 %all-gather.9.cloned.1.call-done = bf16[1152,4096]{1,0:T(8,128)(2,1)} async-done(((bf16[144,4096]{1,0:T(8,128)(2,1)}), bf16[1152,4096]{1,0:T(8,128)(2,1)}) %all-gather.9.cloned.1.call-update) | async-done | bytes 9437200 | tf_op jit(solution)/shard_map/all_gather | solution.py:225
  447.1 10.6 fusion.90
  462.4 93.7 %reduce-scatter.15.cloned.1.call-done = f32[144,1024]{1,0:T(8,128)} async-done(((f32[1152,1024]{1,0:T(8,128)}), f32[144,1024]{1,0:T(8,128)}) %reduce-scatter.15.cloned.1.call-update) | async-done | bytes 589840 | tf_op jit(solution)/shard_map/reduce_scatter | solution.py:232
  571.8 14.7 %conditional.3 = (f32[576,1024]{1,0:T(8,128)}, bf16[1024,256]{0,1:T(8,128)(2,1)S(1)}, bf16[9,256]{1,0:T(8,128)(2,1)S(1)}, bf16[256,1024]{1,0:T(8,128)(2,1)S(1)}, bf16[1024]{0:T(1024)(128)(2,1)S(1)}) conditional(s32[]{:T(128)} %convert_element_type.193, (f32[24,24,1024]{2,1,0:T(8,128)S(1)}, bf16[576,1024]{1,0:T(8,128)(2,1)}, ...), branch_computations={%region_12.27_spmd, %region_27.0_spmd} | conditional | flops 1836120320 | bytes 47511336 | solution.py:241
  589.4 10.6 convolution_convert_fusion.1
  604.7 18.5 %reduce-scatter.23.cloned.1.call-done = bf16[32,1024]{1,0:T(8,128)(2,1)} async-done(((bf16[256,1024]{1,0:T(8,128)(2,1)}), bf16[32,1024]{1,0:T(8,128)(2,1)}) %reduce-scatter.23.cloned.1.call-update) | async-done | bytes 65552 | tf_op jit(solution)/shard_map/reduce_scatter | solution.py:277
  623.2 64.5 %reduce-scatter.21.cloned.1.call-done = bf16[1024,32]{0,1:T(8,128)(2,1)} async-done(((bf16[1024,256]{0,1:T(8,128)(2,1)}), bf16[1024,32]{0,1:T(8,128)(2,1)}) %reduce-scatter.21.cloned.1.call-update) | async-done | bytes 65552 | tf_op jit(solution)/shard_map/reduce_scatter | solution.py:271
  687.7 64.2 %reduce-scatter.17.cloned.1.call-done = bf16[1024,32]{0,1:T(8,128)(2,1)} async-done(((bf16[1024,256]{0,1:T(8,128)(2,1)}), bf16[1024,32]{0,1:T(8,128)(2,1)}) %reduce-scatter.17.cloned.1.call-update) | async-done | bytes 65552 | tf_op jit(solution)/shard_map/reduce_scatter | solution.py:259
  751.8 64.6 %reduce-scatter.19.cloned.1.call-done = bf16[32,1024]{1,0:T(8,128)(2,1)} async-done(((bf16[256,1024]{1,0:T(8,128)(2,1)}), bf16[32,1024]{1,0:T(8,128)(2,1)}) %reduce-scatter.19.cloned.1.call-update) | async-done | bytes 65552 | tf_op jit(solution)/shard_map/reduce_scatter | solution.py:265
  818.2 9.6 convolution_convert_fusion
  829.7 19.5 %all-reduce.12 = (bf16[1024]{0:T(1024)(128)(2,1)S(1)}, bf16[1024]{0:T(1024)(128)(2,1)S(1)}) all-reduce(bf16[1024]{0:T(1024)(128)(2,1)S(1)} %get-tuple-element.160, bf16[1024]{0:T(1024)(128)(2,1)S(1)} %copy-done.10), channel_id=7, replica_groups=mesh['dp'=4,'mp'=8] {'mp'}, use_global_device_ids=true, to_apply=%region_48.49.clone | all-reduce | flops 2048 | bytes 8192
  849.3 31.4 %reduce-scatter.27.cloned.1.call-done = bf16[32,9]{1,0:T(8,128)(2,1)} async-done(((bf16[256,9]{1,0:T(8,128)(2,1)}), bf16[32,9]{1,0:T(8,128)(2,1)}) %reduce-scatter.27.cloned.1.call-update) | async-done | bytes 592
  881.5 63.5 %reduce-scatter.25.cloned.1.call-done = bf16[32,9]{1,0:T(8,128)(2,1)} async-done(((bf16[256,9]{1,0:T(8,128)(2,1)}), bf16[32,9]{1,0:T(8,128)(2,1)}) %reduce-scatter.25.cloned.1.call-update) | async-done | bytes 592
  953.9 101.0 %all-reduce.17.cloned.1.call-done = (bf16[1024,32]{0,1:T(8,128)(2,1)}, bf16[32,1024]{1,0:T(8,128)(2,1)}, bf16[1024,32]{0,1:T(8,128)(2,1)}, bf16[32,1024]{1,0:T(8...) async-done(((bf16[1024,32]{0,1:T(8,128)(2,1)}, bf16[32,1024]{1,0:T(8,128)(2,1)}, bf16[1024,32]{0,1:T(8,128)(2,1)}, bf16[32,1024]{1,0:T(8,128)(2,1)}, ...) | async-done | bytes 5505040 | tf_op jit(solution)/shard_map/psum | solution.py:285
  1070.5 152.3 %reduce-scatter.13.cloned.1.call-done = bf16[144,4096]{1,0:T(8,128)(2,1)} async-done(((bf16[1152,4096]{1,0:T(8,128)(2,1)}), bf16[144,4096]{1,0:T(8,128)(2,1)}) %reduce-scatter.13.cloned.1.call-update) | async-done | bytes 1179664 | tf_op jit(solution)/shard_map/reduce_scatter | solution.py:219
  (176 shorter events, 103.3 us)
Async XLA Ops:
  7.2 301.1 %copy-start = (bf16[1024,512]{1,0:T(8,128)(2,1)S(1)}, bf16[1024,512]{1,0:T(8,128)(2,1)}, u32[]{:S(2)}) copy-start(bf16[1024,512]{1,0:T(8,128)(2,1)} %param.27) | copy-start | bytes 3145732
  7.2 301.1 %all-gather.7.cloned.1.call-start = ((), (), s32[]{:S(2)}) async-start(), calls=%async_computation.8 | async-start | bytes 2654208 | tf_op jit(solution)/shard_map/all_gather | solution.py:216
  8.0 558.1 %copy-start.11 = (f32[12]{0:T(128)}, f32[12]{0:T(128)S(1)}, u32[]{:S(2)}) copy-start(f32[12]{0:T(128)S(1)} %subtract_convert_fusion) | copy-start | bytes 148
  8.0 558.0 %copy-start.12 = (s32[12]{0:T(128)}, s32[12]{0:T(128)S(1)}, u32[]{:S(2)}) copy-start(s32[12]{0:T(128)S(1)} %get-tuple-element.347) | copy-start | bytes 148
  8.0 558.0 %copy-start.13 = (s32[12]{0:T(128)}, s32[12]{0:T(128)S(1)}, u32[]{:S(2)}) copy-start(s32[12]{0:T(128)S(1)} %get-tuple-element.348) | copy-start | bytes 148
  257.8 189.3 %all-gather.9.cloned.1.call-start = ((), (), s32[]{:S(2)}) async-start(), calls=%async_computation.10 | async-start | bytes 10616832 | tf_op jit(solution)/shard_map/all_gather | solution.py:225
  258.6 297.6 %reduce-scatter.15.cloned.1.call-start = ((), (), s32[]{:S(2)}) async-start(), calls=%async_computation.11 | async-start | bytes 5308416 | tf_op jit(solution)/shard_map/reduce_scatter | solution.py:232
  462.3 97.8 %copy-start.8 = (f32[144,256]{1,0:T(8,128)S(1)}, f32[144,256]{1,0:T(8,128)}, u32[]{:S(2)}) copy-start(f32[144,256]{1,0:T(8,128)} %reshape.661) | copy-start | bytes 442372
  462.4 160.8 %reduce-scatter.23.cloned.1.call-start = ((), (), s32[]{:S(2)}) async-start(), calls=%async_computation.15 | async-start | bytes 589824 | tf_op jit(solution)/shard_map/reduce_scatter | solution.py:277
  561.4 126.3 %reduce-scatter.21.cloned.1.call-start = ((), (), s32[]{:S(2)}) async-start(), calls=%async_computation.14 | async-start | bytes 589824 | tf_op jit(solution)/shard_map/reduce_scatter | solution.py:271
  565.7 186.2 %reduce-scatter.17.cloned.1.call-start = ((), (), s32[]{:S(2)}) async-start(), calls=%async_computation.12 | async-start | bytes 589824 | tf_op jit(solution)/shard_map/reduce_scatter | solution.py:259
  571.7 16.4 %copy-start.19 = (bf16[256]{0:T(256)(128)(2,1)S(1)}, bf16[256]{0:T(256)(128)(2,1)}, u32[]{:S(2)}) copy-start(bf16[256]{0:T(256)(128)(2,1)} %get-tuple-element.253) | copy-start | bytes 1540
  571.7 16.4 %copy-start.18 = (bf16[256]{0:T(256)(128)(2,1)S(1)}, bf16[256]{0:T(256)(128)(2,1)}, u32[]{:S(2)}) copy-start(bf16[256]{0:T(256)(128)(2,1)} %get-tuple-element.254) | copy-start | bytes 1540
  571.7 16.5 %copy-start.17 = (bf16[256]{0:T(256)(128)(2,1)S(1)}, bf16[256]{0:T(256)(128)(2,1)}, u32[]{:S(2)}) copy-start(bf16[256]{0:T(256)(128)(2,1)} %get-tuple-element.255) | copy-start | bytes 1540
  571.8 16.5 %copy-start.16 = (bf16[256]{0:T(256)(128)(2,1)S(1)}, bf16[256]{0:T(256)(128)(2,1)}, u32[]{:S(2)}) copy-start(bf16[256]{0:T(256)(128)(2,1)} %get-tuple-element.256) | copy-start | bytes 1540
  571.8 16.5 %copy-start.15 = (bf16[256]{0:T(256)(128)(2,1)S(1)}, bf16[256]{0:T(256)(128)(2,1)}, u32[]{:S(2)}) copy-start(bf16[256]{0:T(256)(128)(2,1)} %get-tuple-element.257) | copy-start | bytes 1540
  571.8 16.5 %copy-start.14 = (bf16[256]{0:T(256)(128)(2,1)S(1)}, bf16[256]{0:T(256)(128)(2,1)}, u32[]{:S(2)}) copy-start(bf16[256]{0:T(256)(128)(2,1)} %get-tuple-element.258) | copy-start | bytes 1540
  571.8 16.5 %copy-start.22 = (bf16[256]{0:T(256)(128)(2,1)S(1)}, bf16[256]{0:T(256)(128)(2,1)}, u32[]{:S(2)}) copy-start(bf16[256]{0:T(256)(128)(2,1)} %get-tuple-element.332) | copy-start | bytes 1540
  587.3 229.2 %reduce-scatter.19.cloned.1.call-start = ((), (), s32[]{:S(2)}) async-start(), calls=%async_computation.13 | async-start | bytes 589824 | tf_op jit(solution)/shard_map/reduce_scatter | solution.py:265
  588.1 292.7 %reduce-scatter.27.cloned.1.call-start = ((), (), s32[]{:S(2)}) async-start(), calls=%async_computation.17 | async-start | bytes 73728
  589.1 355.9 %reduce-scatter.25.cloned.1.call-start = ((), (), s32[]{:S(2)}) async-start(), calls=%async_computation.16 | async-start | bytes 73728
  600.8 454.1 %all-reduce.17.cloned.1.call-start = ((), (), s32[]{:S(2)}) async-start(), calls=%async_computation.18 | async-start | bytes 11010048 | tf_op jit(solution)/shard_map/psum | solution.py:285
  816.5 406.3 %reduce-scatter.13.cloned.1.call-start = ((), (), s32[]{:S(2)}) async-start(), calls=%async_computation.9 | async-start | bytes 10616832 | tf_op jit(solution)/shard_map/reduce_scatter | solution.py:219
  1063.8 159.0 %copy-start.1 = (bf16[1024,512]{1,0:T(8,128)(2,1)S(1)}, bf16[1024,512]{1,0:T(8,128)(2,1)}, u32[]{:S(2)}) copy-start(bf16[1024,512]{1,0:T(8,128)(2,1)} %param.27) | copy-start | bytes 3145732
  (13 other events, 62.2 us)
Sparse Core Ops, SparseCore 0:
  257.9 50.3 all-gather.6
  310.5 136.5 all-gather.8
  462.5 93.5 reduce-scatter.14
  561.5 61.6 reduce-scatter.22
  626.7 60.8 reduce-scatter.20
  690.9 60.9 reduce-scatter.16
  755.5 60.8 reduce-scatter.18
  820.4 60.2 reduce-scatter.26
  884.7 60.2 reduce-scatter.24
  948.2 106.7 all-reduce.16
  1059.1 163.6 reduce-scatter.12
where the time goes:
time: 1240 us; the launch traced here: 1230 us
  waiting for transfers between devices  839 us (68%)
  blocking collectives  256 us (21%)
  matrix products  69.2 us (6%)
  other arithmetic  32.9 us (3%)
  between operations  16.2 us (1%)
  local copies, waits for them, and re-layouts  15.6 us (1%)
    reduce_scatter x1, waiting for transfers between devices, body(): lax.psum_scatter(jnp.dot(active, w_out, preferred_element_type=jnp.float3...  152 us
    all_gather x1, waiting for transfers between devices, body(): piece = lax.all_gather(d_tokens, 'mp', axis=0, tiled=True)  134 us
    psum x1, waiting for transfers between devices, body(): lax.psum(shards[0].astype(jnp.bfloat16), 'dp').astype(jnp.float32)  101 us
    unnamed x13, waiting for transfers between devices  96.3 us
    reduce_scatter x1, waiting for transfers between devices, body(): lax.psum_scatter(times_trans(d_part, w_in), 'mp', scatter_dimension=0, ti...  93.7 us
    reduce_scatter x1, waiting for transfers between devices, body(): lax.psum_scatter(first_grads[2].astype(jnp.bfloat16), 'mp', scatter_dimen...  64.6 us
    reduce_scatter x1, waiting for transfers between devices, body(): lax.psum_scatter(second_grads[0].astype(jnp.bfloat16), 'mp', scatter_dime...  64.5 us
    reduce_scatter x1, waiting for transfers between devices, body(): lax.psum_scatter(first_grads[0].astype(jnp.bfloat16), 'mp', scatter_dimen...  64.2 us
  transfers between devices with their start and end apart: 11, of which 11 were waited for; matrix products, arithmetic and copies ran while one was open for 6% of the time, Pallas kernels for 0%

commit v1 on v0

--- a/solution.py
+++ b/solution.py
@@ -1,6 +1,8 @@
 import jax
 import jax.numpy as jnp
 from jax import lax
+from jax.experimental import pallas as pl
+from jax.experimental.pallas import tpu as pltpu
 from jax.sharding import PartitionSpec as P
 
 GRID = 24
@@ -309,6 +311,1021 @@
     )
 
 
+bf16 = jnp.bfloat16
+f32 = jnp.float32
+MESH = pl.DeviceIdType.MESH
+CELLS = GRID * GRID
+POOLED = POOL * POOL
+TILE = 96
+PIECES = 4
+CHUNKS = 8
+
+
+def dot(left, right, left_dim, right_dim):
+    return lax.dot_general(
+        left, right, (((left_dim,), (right_dim,)), ((), ())), preferred_element_type=f32
+    )
+
+
+def split_low(values):
+    high = values.astype(bf16)
+    return high, (values - high.astype(f32)).astype(bf16)
+
+
+def edge_masks(extent, channels):
+    cells = extent * extent
+    index = lax.broadcasted_iota(jnp.int32, (cells, channels), 0).astype(f32)
+    row = jnp.floor((index + 0.5) * (1.0 / extent))
+    col = index - row * extent
+    one = jnp.ones_like(index)
+    zero = jnp.zeros_like(index)
+    return (
+        jnp.where(row >= 0.5, one, zero),
+        jnp.where(row <= extent - 1.5, one, zero),
+        jnp.where(col >= 0.5, one, zero),
+        jnp.where(col <= extent - 1.5, one, zero),
+    )
+
+
+def conv_forward(act, taps, extent, masks):
+    above, below, left, right = masks
+    cells = extent * extent
+    up = pltpu.roll(act, extent, 0) * above
+    down = pltpu.roll(act, cells - extent, 0) * below
+    sums = [up * taps[q] + act * taps[3 + q] + down * taps[6 + q] for q in range(3)]
+    return (
+        sums[1]
+        + pltpu.roll(sums[0], 1, 0) * left
+        + pltpu.roll(sums[2], cells - 1, 0) * right
+    )
+
+
+def conv_backward(upstream, act, taps, extent, masks):
+    above, below, left, right = masks
+    cells = extent * extent
+    sides = [pltpu.roll(upstream, cells - 1, 0) * right, upstream, pltpu.roll(upstream, 1, 0) * left]
+    sums = [
+        sides[0] * taps[3 * r] + sides[1] * taps[3 * r + 1] + sides[2] * taps[3 * r + 2]
+        for r in range(3)
+    ]
+    d_act = (
+        sums[1]
+        + pltpu.roll(sums[0], cells - extent, 0) * below
+        + pltpu.roll(sums[2], extent, 0) * above
+    )
+    acts = [pltpu.roll(act, extent, 0) * above, act, pltpu.roll(act, cells - extent, 0) * below]
+    d_taps = [
+        jnp.sum(acts[r] * sides[q], axis=0, keepdims=True) for r in range(3) for q in range(3)
+    ]
+    return d_act, d_taps
+
+
+def slot_rows(ref):
+    slots, rows, columns = ref.shape
+    return ref[...].reshape(slots * rows, columns)
+
+
+def layer_kernel(
+    patches_in, side_in, pack_in, w_in_in, w_out_in, cot_in,
+    tok_out, dpat_out, gout_out, gin_out, gblk_out, gsml_out, cot_all, gx_land, gi_land,
+    xp, gw, red_a, spa_a, nar_a, norm_a, inv_a, yhi, ylo, dy, dlow, pp,
+    tw, poolv, red_b, spa_b, nar_b, norm_b, inv_b,
+    wi, wo, qs, actv, slope, dpre, dtv, tp, cr, ps, rl, tstage,
+    dr, dz, gos, gis, land,
+    wgs, wgc, xs, xr, zs, zr, ys, yr, sm, smc, smx, smz, smy, gfin,
+    loc, w_s, w_rz, w_rx, w_rc, sw_s, sw_r, q_s, q_rz, q_rc,
+    dt_s, dt_r, dt_cs, dt_cr, t_cs, t_cr, t_s, t_r, credit,
+    d_cs, d_cr, d_zs, d_zr, gx_s, gx_r, gy_s, gy_r, gc_s, gc_r, gl,
+    gr_s, gr_r,
+):
+    dp_at = lax.axis_index("dp")
+    mp_at = lax.axis_index("mp")
+    y = lax.div(dp_at, 2)
+    c = lax.rem(dp_at, 2)
+    z = lax.div(mp_at, 2)
+    x = lax.rem(mp_at, 2)
+    zn = 4
+
+    def device(x_at, y_at, z_at, c_at):
+        return (2 * y_at + c_at, 2 * z_at + x_at)
+
+    twin = device(x, y, z, 1 - c)
+    x_peer = device(1 - x, y, z, c)
+    cross = device(1 - x, y, z, 1 - c)
+    y_peer = device(x, 1 - y, z, c)
+
+    def z_at(step):
+        return lax.rem(z + step + zn, zn)
+
+    def z_dev(z_of):
+        return device(x, y, z_of, c)
+
+    def remote(src, dst, send, recv, to):
+        return pltpu.make_async_remote_copy(
+            src_ref=src, dst_ref=dst, send_sem=send, recv_sem=recv, device_id=to, device_id_type=MESH
+        )
+
+    def start(src, dst, send, recv, to):
+        remote(src, dst, send, recv, to).start()
+
+    def arrived(dst, recv):
+        pltpu.make_async_copy(dst, dst, recv).wait()
+
+    def left_here(src, send):
+        pltpu.make_async_copy(src, src, send).wait()
+
+    own = x == c
+
+    load_patches = pltpu.make_async_copy(patches_in, xp, loc.at[0])
+    load_pack = pltpu.make_async_copy(pack_in.at[c], gw.at[c, mp_at], loc.at[1])
+    me = 2 * z + c
+    load_cot = pltpu.make_async_copy(cot_in, cot_all.at[z, c], loc.at[2])
+    load_patches.start()
+    load_pack.start()
+    load_cot.start()
+
+    barrier = pltpu.get_barrier_semaphore()
+    peers = [twin, x_peer, cross, y_peer] + [z_dev(z_at(k)) for k in range(1, zn)]
+    for peer in peers:
+        pl.semaphore_signal(barrier, inc=1, device_id=peer, device_id_type=MESH)
+    pl.semaphore_wait(barrier, len(peers))
+
+    load_pack.wait()
+    spans = ((0, 48), (48, 32))
+
+    def w_part(b, core, i):
+        return gw.at[core, i, pl.ds(spans[b][0], spans[b][1])]
+
+    def w_own(b):
+        part = w_part(b, c, mp_at)
+        for k in range(1, zn):
+            start(part, part, w_s.at[b, k - 1], w_rz.at[b, k], z_dev(z_at(k)))
+        start(part, part, w_s.at[b, 3], w_rx.at[b, z], x_peer)
+        start(part, part, w_s.at[b, 7], w_rc.at[b, mp_at], twin)
+
+    def w_forward(b):
+        for k in range(1, zn):
+            z_of = z_at(-k)
+            i = 2 * z_of + x
+            part = w_part(b, c, i)
+            arrived(part, w_rz.at[b, k])
+            start(part, part, w_s.at[b, 3 + k], w_rx.at[b, z_of], x_peer)
+            start(part, part, w_s.at[b, 7 + k], w_rc.at[b, i], twin)
+        for k in range(zn):
+            z_of = z_at(-k)
+            i = 2 * z_of + 1 - x
+            part = w_part(b, c, i)
+            arrived(part, w_rx.at[b, z_of])
+            start(part, part, w_s.at[b, 11 + k], w_rc.at[b, i], twin)
+
+    def w_finish(b):
+        for i in range(8):
+            arrived(w_part(b, 1 - c, i), w_rc.at[b, i])
+
+    w_own(0)
+    w_own(1)
+
+    width = cot_in.shape[1] // PIECES
+
+    def cot(z_of, c_of, p):
+        return cot_all.at[z_of, c_of, :, pl.ds(pl.multiple_of(p * width, width), width)]
+
+    def cot_right(z_of, p, hop):
+        @pl.when(z < zn - 1)
+        def _():
+            part = cot(z_of, c, p)
+            start(part, part, dt_s.at[p, 0, hop], dt_r.at[p, 0, hop], z_dev(z + 1))
+
+    def cot_left(z_of, p, hop):
+        @pl.when(z > 0)
+        def _():
+            part = cot(z_of, c, p)
+            start(part, part, dt_s.at[p, 1, hop], dt_r.at[p, 1, hop], z_dev(z - 1))
+
+    def cot_twin(z_of, p):
+        part = cot(z_of, c, p)
+        start(part, part, dt_cs.at[p, z_of], dt_cr.at[p, z_of], twin)
+
+    def cot_own(p):
+        cot_right(z, p, 0)
+        cot_left(z, p, 0)
+        cot_twin(z, p)
+
+    def cot_hop(p, hop):
+        @pl.when(z >= hop)
+        def _():
+            arrived(cot(z - hop, c, p), dt_r.at[p, 0, hop - 1])
+            if hop < zn - 1:
+                cot_right(z - hop, p, hop)
+            cot_twin(z - hop, p)
+
+        @pl.when(z + hop <= zn - 1)
+        def _():
+            arrived(cot(z + hop, c, p), dt_r.at[p, 1, hop - 1])
+            if hop < zn - 1:
+                cot_left(z + hop, p, hop)
+            cot_twin(z + hop, p)
+
+    w_forward(0)
+    chunk = w_out_in.shape[1] // CHUNKS
+
+    def columns(ref, j, span):
+        return ref.at[:, pl.ds(j * span, span)]
+
+    @pl.when(own)
+    def _():
+        pltpu.make_async_copy(w_in_in, wi, sw_r.at[0]).start()
+        for j in range(CHUNKS):
+            pltpu.make_async_copy(
+                columns(w_out_in, j, chunk), columns(wo, j, chunk), sw_r.at[1 + j]
+            ).start()
+
+    @pl.when(jnp.logical_not(own))
+    def _():
+        start(w_in_in, wi, sw_s.at[0], sw_r.at[0], cross)
+        for j in range(CHUNKS):
+            start(
+                columns(w_out_in, j, chunk), columns(wo, j, chunk),
+                sw_s.at[1 + j], sw_r.at[1 + j], cross,
+            )
+
+    load_cot.wait()
+    for p in range(2):
+        cot_own(p)
+    w_finish(0)
+
+    def block_weights(b):
+        rows = pl.ds(spans[b][0], 32)
+        return (
+            gw[0, :, rows, :].reshape(256, 1024),
+            gw[1, :, rows, :].reshape(256, 1024),
+        )
+
+    def small_weights(b):
+        total = gw[b, 0, 32:48, :].astype(f32)
+        for i in range(1, 8):
+            total = total + gw[b, i, 32:48, :].astype(f32)
+        tw[b] = total
+        return total[9:10, :]
+
+    def lanes_of(h):
+        return pl.ds(pl.multiple_of(h * 128, 128), 128)
+
+    def tap_rows(b, lanes):
+        return [tw[b, k : k + 1, lanes] for k in range(9)]
+
+    gain_a = small_weights(0)
+    side = side_in[0].astype(f32)
+    def cell_mask():
+        index = lax.broadcasted_iota(jnp.int32, (CELLS, 128), 0).astype(f32)
+        row = jnp.floor((index + 0.5) * (1.0 / GRID))
+        col = index - row * GRID
+        return jnp.where((row < side - 0.5) & (col < side - 0.5), 1.0, 0.0).astype(f32)
+
+    load_patches.wait()
+    wr_a, we_a = block_weights(0)
+    red_a[...] = dot(xp[...], wr_a, 1, 1)
+
+    def conv_half_a(h, carry):
+        lanes = lanes_of(h)
+        reduced = red_a[:, lanes]
+        activated = reduced * jax.nn.sigmoid(reduced) * cell_mask()
+        spatial = conv_forward(activated, tap_rows(0, lanes), GRID, edge_masks(GRID, 128))
+        spa_a[:, lanes] = spatial
+        nar_a[:, lanes] = (spatial * jax.nn.sigmoid(spatial)).astype(bf16)
+        return carry
+
+    lax.fori_loop(0, 2, conv_half_a, 0)
+    dy[...] = dot(nar_a[...], we_a, 1, 0)
+
+    def normalise(wide_ref, ref, inv_ref, rows):
+        widened = wide_ref[rows, :]
+        centred = widened - jnp.mean(widened, axis=1, keepdims=True)
+        inv = lax.rsqrt(jnp.mean(centred * centred, axis=1, keepdims=True) + epsilon)
+        normed = centred * inv
+        ref[rows, :] = normed.astype(ref.dtype)
+        inv_ref[rows, :] = jnp.broadcast_to(inv, (normed.shape[0], 128))
+        return normed
+
+    def norm_tile(t, carry):
+        rows = pl.ds(pl.multiple_of(t * TILE, TILE), TILE)
+        normed = normalise(dy, norm_a, inv_a, rows)
+        result = xp[rows, :].astype(f32) + normed * gain_a
+        high, low = split_low(result)
+        yhi[rows, :] = high
+        ylo[rows, :] = low
+        return carry
+
+    lax.fori_loop(0, CELLS // TILE, norm_tile, 0)
+
+    cell = lax.broadcasted_iota(jnp.int32, (POOLED, CELLS), 1).astype(f32)
+    bin_of = lax.broadcasted_iota(jnp.int32, (POOLED, CELLS), 0).astype(f32)
+    cell_row = jnp.floor((cell + 0.5) * (1.0 / GRID))
+    cell_col = cell - cell_row * GRID
+    bin_row = jnp.floor((bin_of + 0.5) * (1.0 / POOL))
+    bin_col = bin_of - bin_row * POOL
+
+    def table(bins, at):
+        lower = jnp.floor((bins * side + 0.5) * (1.0 / POOL))
+        upper = jnp.floor(((bins + 1.0) * side + (POOL - 0.5)) * (1.0 / POOL))
+        return jnp.where((at > lower - 0.5) & (at < upper - 0.5), 1.0 / (upper - lower), 0.0)
+
+    pp[...] = (table(bin_row, cell_row) * table(bin_col, cell_col)).astype(bf16)
+    pooled = dot(pp[...], yhi[...], 1, 0) + dot(pp[...], ylo[...], 1, 0)
+    poolv[...] = pooled
+
+    w_forward(1)
+    w_finish(1)
+
+    gain_b = small_weights(1)
+    wr_b, we_b = block_weights(1)
+    reduced_b = dot(pooled.astype(bf16), wr_b, 1, 1)
+    red_b[...] = reduced_b
+    activated_b = reduced_b * jax.nn.sigmoid(reduced_b)
+    spatial_b = conv_forward(activated_b, tap_rows(1, pl.ds(0, 256)), POOL, edge_masks(POOL, 256))
+    spa_b[...] = spatial_b
+    nar_b[...] = (spatial_b * jax.nn.sigmoid(spatial_b)).astype(bf16)
+    norm_b[...] = dot(nar_b[...], we_b, 1, 0)
+    normed_b = normalise(norm_b, norm_b, inv_b, pl.ds(0, POOLED))
+    qs[me] = (pooled + normed_b * gain_b).astype(bf16)
+
+    for k in range(1, zn):
+        start(qs.at[me], qs.at[me], q_s.at[k - 1], q_rz.at[k], z_dev(z_at(k)))
+    start(qs.at[me], qs.at[me], q_s.at[3], q_rc.at[z], twin)
+    for p in range(2, PIECES):
+        cot_own(p)
+    for k in range(1, zn):
+        z_of = z_at(-k)
+        slot = qs.at[2 * z_of + c]
+        arrived(slot, q_rz.at[k])
+        start(slot, slot, q_s.at[3 + k], q_rc.at[z_of], twin)
+    for p in range(PIECES):
+        cot_hop(p, 1)
+    for z_of in range(zn):
+        arrived(qs.at[2 * z_of + 1 - c], q_rc.at[z_of])
+    arrived(wi, sw_r.at[0])
+
+    dpre[...] = dot(slot_rows(qs), wi[...], 1, 0)
+
+    def gelu_tile(t, carry):
+        rows = pl.ds(pl.multiple_of(t * POOLED, POOLED), POOLED)
+        hidden = dpre[rows, :]
+        phi = 0.5 * (1.0 + lax.erf(hidden * root_half))
+        actv[rows, :] = (hidden * phi).astype(bf16)
+        slope[rows, :] = (
+            phi + hidden * jnp.exp(-0.5 * hidden * hidden) * inv_root_tau
+        ).astype(bf16)
+        return carry
+
+    lax.fori_loop(0, 8, gelu_tile, 0)
+    dpre[...] = jnp.zeros_like(dpre)
+
+    def item_part(i):
+        b = lax.rem(i, 2)
+
+        @pl.when(i >= 2)
+        def _():
+            left_here(tp.at[b, :, 1 - c], t_cs.at[b])
+            pl.semaphore_wait(credit, 1)
+
+        weights = wo[:, pl.ds(pl.multiple_of(i * chunk, chunk), chunk)]
+        partial = dot(actv[...], weights, 1, 0).astype(bf16)
+        tp[b] = partial.reshape(zn, 2, POOLED, chunk)
+        start(tp.at[b, :, 1 - c], cr.at[b], t_cs.at[b], t_cr.at[b], twin)
+
+    def send_right(i, d):
+        start(ps.at[i, d], rl.at[i, d + 1], t_s.at[i, d], t_r.at[i, d + 1], z_dev(z + 1))
+
+    def send_left(i, d):
+        start(ps.at[i, d], rl.at[i, d], t_s.at[i, d], t_r.at[i, d], z_dev(z - 1))
+
+    def item_pair(i):
+        b = lax.rem(i, 2)
+        arrived(cr.at[b], t_cr.at[b])
+
+        def add(d, carry):
+            ps[i, d] = (tp[b, d, c].astype(f32) + cr[b, d].astype(f32)).astype(bf16)
+            return carry
+
+        lax.fori_loop(0, zn, add, 0)
+
+        @pl.when(i < CHUNKS - 2)
+        def _():
+            pl.semaphore_signal(credit, inc=1, device_id=twin, device_id_type=MESH)
+
+        @pl.when(z == 0)
+        def _():
+            for d in range(zn - 1, 0, -1):
+                send_right(i, d)
+
+        @pl.when(z == zn - 1)
+        def _():
+            for d in range(zn - 1):
+                send_left(i, d)
+
+    def item_right(i):
+        def pass_on(step, carry):
+            d = zn - 1 - step
+            arrived(rl.at[i, d + 1], t_r.at[i, d + 1])
+            ps[i, d] = (ps[i, d].astype(f32) + rl[i, d + 1].astype(f32)).astype(bf16)
+            send_right(i, d)
+            return carry
+
+        lax.fori_loop(0, zn - 1 - z, pass_on, 0)
+        arrived(rl.at[i, z + 1], t_r.at[i, z + 1])
+
+    def item_left(i):
+        def pass_on(d, carry):
+            arrived(rl.at[i, d], t_r.at[i, d])
+            ps[i, d] = (ps[i, d].astype(f32) + rl[i, d].astype(f32)).astype(bf16)
+            send_left(i, d)
+            return carry
+
+        lax.fori_loop(0, z, pass_on, 0)
+        arrived(rl.at[i, z], t_r.at[i, z])
+
+    def tok_slice(i):
+        return tok_out.at[:, pl.ds(pl.multiple_of(i * chunk, chunk), chunk)]
+
+    def item_final(i):
+        b = lax.rem(i, 2)
+
+        @pl.when(i >= 2)
+        def _():
+            left_here(tstage.at[b], gl.at[8 + b])
+
+        tstage[b] = ps[i, z]
+
+        @pl.when(z > 0)
+        def _():
+            tstage[b] = (tstage[b].astype(f32) + rl[i, z + 1].astype(f32)).astype(bf16)
+
+        @pl.when(z < zn - 1)
+        def _():
+            tstage[b] = (tstage[b].astype(f32) + rl[i, z].astype(f32)).astype(bf16)
+
+        pltpu.make_async_copy(tstage.at[b], tok_slice(i), gl.at[8 + b]).start()
+
+    def item_step(s):
+        @pl.when(s < CHUNKS)
+        def _():
+            item_part(s)
+
+        @pl.when((s >= 1) & (s < CHUNKS + 1))
+        def _():
+            item_pair(s - 1)
+
+        right_at = s - 1 - z
+
+        @pl.when((z > 0) & (right_at >= 0) & (right_at < CHUNKS))
+        def _():
+            item_right(right_at)
+
+        left_at = s - zn + z
+
+        @pl.when((z < zn - 1) & (left_at >= 0) & (left_at < CHUNKS))
+        def _():
+            item_left(left_at)
+
+        @pl.when((s >= zn) & (s < CHUNKS + zn))
+        def _():
+            item_final(s - zn)
+
+    def gx_part(p):
+        return gx_land.at[p]
+
+    def piece_work(p):
+        for z_of in range(zn):
+            arrived(cot(z_of, 1 - c, p), dt_cr.at[p, z_of])
+        load = pltpu.make_async_copy(
+            cot_all.at[:, :, :, pl.ds(pl.multiple_of(p * width, width), width)], dtv, loc.at[3]
+        )
+        load.start()
+
+        @pl.when(p >= 1)
+        def _():
+            grad_pair(p - 1)
+
+        load.wait()
+
+        def out_half(h, carry):
+            lanes = pl.ds(pl.multiple_of(h * chunk, chunk), chunk)
+            rows = dtv[:, :, :, lanes].reshape(8 * POOLED, chunk)
+            gos[p, :, lanes] = dot(actv[...], rows, 0, 0).astype(bf16)
+            return carry
+
+        def hidden_half(h, carry):
+            lanes = pl.ds(pl.multiple_of(h * chunk, chunk), chunk)
+            rows = dtv[:, :, :, lanes].reshape(8 * POOLED, chunk)
+            weights = wo[:, pl.ds(pl.multiple_of(p * width + h * chunk, chunk), chunk)]
+            dpre[...] += dot(rows, weights, 1, 1)
+            return carry
+
+        lax.fori_loop(0, 2, out_half, 0)
+
+        @pl.when(jnp.logical_not(own))
+        def _():
+            start(gos.at[p], gx_land.at[p], gx_s.at[p], gx_r.at[p], x_peer)
+
+        lax.fori_loop(0, 2, hidden_half, 0)
+
+    def gout_slice(half, p):
+        return gout_out.at[half, :, pl.ds(pl.multiple_of(p * width, width), width)]
+
+    def grad_pair(p):
+        @pl.when(own)
+        def _():
+            arrived(gx_land.at[p], gx_r.at[p])
+            for h in range(2):
+                half = pl.ds(h * width // 2, width // 2)
+                load = pltpu.make_async_copy(gx_land.at[p, :, half], land, loc.at[4])
+                load.start()
+                load.wait()
+                gos[p, :, half] = (gos[p, :, half].astype(f32) + land[...].astype(f32)).astype(bf16)
+            mine = gout_slice(y, p)
+            start(gos.at[p], mine, gy_s.at[p], gy_r.at[p], y_peer)
+            start(gos.at[p], mine, gc_s.at[p, 0], gc_r.at[p, 0], twin)
+            pltpu.make_async_copy(gos.at[p], mine, gl.at[p]).start()
+
+    def grad_last(p):
+        other = gout_slice(1 - y, p)
+        mine = gout_slice(y, p)
+
+        @pl.when(own)
+        def _():
+            arrived(other, gy_r.at[p])
+            start(other, other, gc_s.at[p, 1], gc_r.at[p, 1], twin)
+
+    def grad_done(p):
+        other = gout_slice(1 - y, p)
+        mine = gout_slice(y, p)
+
+        @pl.when(own)
+        def _():
+            left_here(gos.at[p], gy_s.at[p])
+            left_here(gos.at[p], gc_s.at[p, 0])
+            left_here(other, gc_s.at[p, 1])
+            pltpu.make_async_copy(gos.at[p], mine, gl.at[p]).wait()
+
+        @pl.when(jnp.logical_not(own))
+        def _():
+            left_here(gos.at[p], gx_s.at[p])
+            arrived(mine, gc_r.at[p, 0])
+            arrived(other, gc_r.at[p, 1])
+
+    def main_step(s, carry):
+        @pl.when(s < CHUNKS // 2)
+        def _():
+            for half in range(2):
+                j = 2 * s + half
+                arrived(wo.at[:, pl.ds(pl.multiple_of(j * chunk, chunk), chunk)], sw_r.at[1 + j])
+
+        item_step(s)
+
+        @pl.when(s < PIECES)
+        def _():
+            cot_hop(s, 2)
+
+        @pl.when((s >= 1) & (s < PIECES + 1))
+        def _():
+            cot_hop(s - 1, 3)
+
+        @pl.when((s >= 2) & (s < PIECES + 2))
+        def _():
+            piece_work(s - 2)
+
+        return carry
+
+    main_steps = PIECES + 2
+    lax.fori_loop(0, main_steps, main_step, 0)
+
+    def dh_tile(t, carry):
+        rows = pl.ds(pl.multiple_of(t * POOLED, POOLED), POOLED)
+        half = lax.div(t, 4)
+        place = pl.ds(pl.multiple_of((t - 4 * half) * POOLED, POOLED), POOLED)
+        ylo[place, pl.ds(pl.multiple_of(half * 512, 512), 512)] = (
+            dpre[rows, :] * slope[rows, :].astype(f32)
+        ).astype(bf16)
+        return carry
+
+    lax.fori_loop(0, 8, dh_tile, 0)
+    for h in range(2):
+        d_part = dot(ylo[:, 512 * h : 512 * h + 512], wi[...], 1, 1).astype(bf16)
+        dtv[2 * h : 2 * h + 2] = d_part.reshape(2, 2, POOLED, 1024)
+    start(dtv.at[:, 1 - c], dr, d_cs.at[0], d_cr.at[0], twin)
+    grad_pair(PIECES - 1)
+    gis[...] = (
+        dot(qs[0:4].reshape(4 * POOLED, 1024), ylo[:, 0:512], 0, 0)
+        + dot(qs[4:8].reshape(4 * POOLED, 1024), ylo[:, 512:1024], 0, 0)
+    ).astype(bf16)
+
+    @pl.when(jnp.logical_not(own))
+    def _():
+        start(gis, gi_land, gx_s.at[PIECES], gx_r.at[PIECES], x_peer)
+
+    arrived(dr, d_cr.at[0])
+
+    def pair_rows(d, carry):
+        dtv[d, c] = (dtv[d, c].astype(f32) + dr[d].astype(f32)).astype(bf16)
+        return carry
+
+    lax.fori_loop(0, zn, pair_rows, 0)
+    for k in range(1, zn):
+        d = z_at(k)
+        start(dtv.at[d, c], dz.at[k - 1], d_zs.at[k - 1], d_zr.at[k - 1], z_dev(d))
+
+    for p in range(PIECES):
+        grad_last(p)
+    total = dtv[z, c].astype(f32)
+    for k in range(1, zn):
+        arrived(dz.at[k - 1], d_zr.at[k - 1])
+        total = total + dz[k - 1].astype(f32)
+
+    def widened_back(d_rows, normed, gain, inv):
+        dn = d_rows * gain
+        return (
+            inv
+            * (
+                dn
+                - jnp.mean(dn, axis=1, keepdims=True)
+                - normed * jnp.mean(dn * normed, axis=1, keepdims=True)
+            )
+        ).astype(bf16)
+
+    def pack_small(t, d_gain):
+        for k in range(4):
+            sm[t, 9 + k : 10 + k, :] = d_gain[:, 256 * k : 256 * k + 256]
+        sm[t, 13:16, :] = jnp.zeros((3, 256), f32)
+
+    normed_b = norm_b[...]
+    d_gain_b = jnp.sum(total * normed_b, axis=0, keepdims=True)
+    gain_b = tw[1, 9:10, :]
+    wr_b, we_b = block_weights(1)
+    dw_b = widened_back(total, normed_b, gain_b, inv_b[:, 0:1])
+    wgs[1, 1] = dot(nar_b[...], dw_b, 0, 0).astype(bf16)
+    spatial_b = spa_b[...]
+    d_spatial_b = dot(dw_b, we_b, 1, 1) * silu_slope(spatial_b)
+    reduced_b = red_b[...]
+    sig_b = jax.nn.sigmoid(reduced_b)
+    d_act_b, d_taps_b = conv_backward(
+        d_spatial_b, reduced_b * sig_b, tap_rows(1, pl.ds(0, 256)), POOL, edge_masks(POOL, 256)
+    )
+    d_red_b = (d_act_b * (sig_b * (1.0 + reduced_b * (1.0 - sig_b)))).astype(bf16)
+    wgs[1, 0] = dot(d_red_b, poolv[...].astype(bf16), 0, 0).astype(bf16)
+    for k in range(9):
+        sm[1, k : k + 1, :] = d_taps_b[k]
+    pack_small(1, d_gain_b)
+    d_pool = total + dot(d_red_b, wr_b, 1, 0)
+
+    def share_core(t):
+        start(wgs.at[t, 1 - c], wgc.at[t], gr_s.at[t, 0], gr_r.at[t, 0], twin)
+        start(sm.at[t], smc.at[t], gr_s.at[t, 1], gr_r.at[t, 1], twin)
+
+    def share_x(t):
+        arrived(wgc.at[t], gr_r.at[t, 0])
+        arrived(smc.at[t], gr_r.at[t, 1])
+        for i in range(8):
+            rows = pl.ds(32 * i, 32)
+            xs[t, i % 2, i // 2] = (
+                wgs[t, c, rows, :].astype(f32) + wgc[t, rows, :].astype(f32)
+            ).astype(bf16)
+        left_here(sm.at[t], gr_s.at[t, 1])
+        sm[t] = sm[t] + smc[t]
+        start(xs.at[t, 1 - x], xr.at[t], gr_s.at[t, 2], gr_r.at[t, 2], x_peer)
+        start(sm.at[t], smx.at[t], gr_s.at[t, 3], gr_r.at[t, 3], x_peer)
+
+    def share_z(t):
+        arrived(xr.at[t], gr_r.at[t, 2])
+        arrived(smx.at[t], gr_r.at[t, 3])
+        zs[t] = (xs[t, x].astype(f32) + xr[t].astype(f32)).astype(bf16)
+        left_here(sm.at[t], gr_s.at[t, 3])
+        smz[t, z] = sm[t] + smx[t]
+        for k in range(1, zn):
+            d = z_at(k)
+            start(zs.at[t, d], zr.at[t, k - 1], gr_s.at[t, 3 + k], gr_r.at[t, 3 + k], z_dev(d))
+            start(
+                smz.at[t, z], smz.at[t, z], gr_s.at[t, 6 + k], gr_r.at[t, 6 + k], z_dev(d)
+            )
+
+    def share_y(t):
+        total_rows = zs[t, z].astype(f32)
+        for k in range(1, zn):
+            arrived(zr.at[t, k - 1], gr_r.at[t, 3 + k])
+            total_rows = total_rows + zr[t, k - 1].astype(f32)
+            arrived(smz.at[t, z_at(-k)], gr_r.at[t, 6 + k])
+        ys[t] = total_rows.astype(bf16)
+        sm[t] = (smz[t, 0] + smz[t, 1]) + (smz[t, 2] + smz[t, 3])
+        start(ys.at[t], yr.at[t], gr_s.at[t, 10], gr_r.at[t, 10], y_peer)
+        start(sm.at[t], smy.at[t], gr_s.at[t, 11], gr_r.at[t, 11], y_peer)
+
+    def share_twin(t):
+        arrived(yr.at[t], gr_r.at[t, 10])
+        arrived(smy.at[t], gr_r.at[t, 11])
+        gfin[t, c] = ys[t].astype(f32) + yr[t].astype(f32)
+        gsml_out[t] = sm[t] + smy[t]
+        start(gfin.at[t, c], gfin.at[t, c], gr_s.at[t, 12], gr_r.at[t, 12], twin)
+
+    def share_done(t):
+        arrived(gfin.at[t, 1 - c], gr_r.at[t, 12])
+        gblk_out[t] = gfin[t]
+        left_here(wgs.at[t, 1 - c], gr_s.at[t, 0])
+        left_here(xs.at[t, 1 - x], gr_s.at[t, 2])
+        for k in range(1, zn):
+            left_here(zs.at[t, 0], gr_s.at[t, 3 + k])
+            left_here(smz.at[t, z], gr_s.at[t, 6 + k])
+        left_here(ys.at[t], gr_s.at[t, 10])
+        left_here(sm.at[t], gr_s.at[t, 11])
+        left_here(gfin.at[t, c], gr_s.at[t, 12])
+
+    share_core(1)
+
+    high, low = split_low(d_pool)
+    dy[...] = dot(pp[...], high, 0, 0) + dot(pp[...], low, 0, 0)
+    gain_a = tw[0, 9:10, :]
+    wr_a, we_a = block_weights(0)
+
+    def back_tile(t, d_gain):
+        rows = pl.ds(pl.multiple_of(t * TILE, TILE), TILE)
+        d_rows = dy[rows, :]
+        normed = norm_a[rows, :].astype(f32)
+        yhi[rows, :] = widened_back(d_rows, normed, gain_a, inv_a[rows, 0:1])
+        return d_gain + jnp.sum(d_rows * normed, axis=0, keepdims=True)
+
+    d_gain_a = lax.fori_loop(0, CELLS // TILE, back_tile, jnp.zeros((1, 1024), f32))
+    wgs[0, 1] = dot(nar_a[...], yhi[...], 0, 0).astype(bf16)
+    share_x(1)
+    spa_a[...] = dot(yhi[...], we_a, 1, 1) * silu_slope(spa_a[...])
+
+    def conv_back_half_a(h, carry):
+        lanes = lanes_of(h)
+        reduced = red_a[:, lanes]
+        sig = jax.nn.sigmoid(reduced)
+        mask = cell_mask()
+        d_act, d_taps = conv_backward(
+            spa_a[:, lanes], reduced * sig * mask, tap_rows(0, lanes), GRID, edge_masks(GRID, 128)
+        )
+        dlow[:, lanes] = (d_act * mask * (sig * (1.0 + reduced * (1.0 - sig)))).astype(bf16)
+        for k in range(9):
+            sm[0, k : k + 1, lanes] = d_taps[k]
+        return carry
+
+    lax.fori_loop(0, 2, conv_back_half_a, 0)
+    wgs[0, 0] = dot(dlow[...], xp[...], 0, 0).astype(bf16)
+    pack_small(0, d_gain_a)
+    share_core(0)
+    share_z(1)
+    dy[...] += dot(dlow[...], wr_a, 1, 0)
+    store_dpat = pltpu.make_async_copy(dy, dpat_out, loc.at[5])
+    store_dpat.start()
+    share_x(0)
+    share_y(1)
+
+    def gin_slice(half):
+        return gin_out.at[half]
+
+    @pl.when(own)
+    def _():
+        arrived(gi_land, gx_r.at[PIECES])
+        for h in range(2):
+            rows = pl.ds(512 * h, 512)
+            load = pltpu.make_async_copy(gi_land.at[rows], land, loc.at[4])
+            load.start()
+            load.wait()
+            gis[rows, :] = (gis[rows, :].astype(f32) + land[...].astype(f32)).astype(bf16)
+        start(gis, gin_slice(y), gy_s.at[PIECES], gy_r.at[PIECES], y_peer)
+        start(gis, gin_slice(y), gc_s.at[PIECES, 0], gc_r.at[PIECES, 0], twin)
+        pltpu.make_async_copy(gis, gin_slice(y), gl.at[PIECES]).start()
+
+    share_z(0)
+    share_twin(1)
+
+    def tail_step(s, carry):
+        item_step(s)
+        return carry
+
+    lax.fori_loop(main_steps, CHUNKS + zn, tail_step, 0)
+    share_y(0)
+    share_twin(0)
+
+    @pl.when(own)
+    def _():
+        arrived(gin_slice(1 - y), gy_r.at[PIECES])
+        start(gin_slice(1 - y), gin_slice(1 - y), gc_s.at[PIECES, 1], gc_r.at[PIECES, 1], twin)
+
+    share_done(1)
+    share_done(0)
+    for p in range(PIECES):
+        grad_done(p)
+
+    @pl.when(own)
+    def _():
+        left_here(gis, gy_s.at[PIECES])
+        left_here(gis, gc_s.at[PIECES, 0])
+        left_here(gin_slice(1 - y), gc_s.at[PIECES, 1])
+        pltpu.make_async_copy(gis, gin_slice(y), gl.at[PIECES]).wait()
+
+    @pl.when(jnp.logical_not(own))
+    def _():
+        left_here(gis, gx_s.at[PIECES])
+        arrived(gin_slice(y), gc_r.at[PIECES, 0])
+        arrived(gin_slice(1 - y), gc_r.at[PIECES, 1])
+        left_here(wi, sw_s.at[0])
+        for j in range(CHUNKS):
+            left_here(columns(wo, j, chunk), sw_s.at[1 + j])
+
+    store_dpat.wait()
+    for b in range(2):
+        pltpu.make_async_copy(tstage.at[b], tok_slice(b), gl.at[8 + b]).wait()
+        left_here(tp.at[b, :, 1 - c], t_cs.at[b])
+        for k in range(15):
+            left_here(w_part(b, c, 0), w_s.at[b, k])
+    for k in range(7):
+        left_here(qs.at[0], q_s.at[k])
+    left_here(dtv.at[:, 0], d_cs.at[0])
+    for k in range(zn - 1):
+        left_here(dtv.at[0, 0], d_zs.at[k])
+    for p in range(PIECES):
+        for z_of in range(zn):
+            left_here(cot(0, 0, p), dt_cs.at[p, z_of])
+        for hop in range(zn - 1):
+            @pl.when((z < zn - 1) & (z >= hop))
+            def _():
+                left_here(cot(0, 0, p), dt_s.at[p, 0, hop])
+
+            @pl.when((z > 0) & (z + hop <= zn - 1))
+            def _():
+                left_here(cot(0, 0, p), dt_s.at[p, 1, hop])
+
+    def drain_items(i, carry):
+        for d in range(zn):
+            @pl.when(z != d)
+            def _():
+                left_here(ps.at[0, 0], t_s.at[i, d])
+        return carry
+
+    lax.fori_loop(0, CHUNKS, drain_items, 0)
+
+
+def layer_call(patches, grid_sizes, pack, w_in, w_out, d_tokens):
+    any_space = pl.BlockSpec(memory_space=pl.ANY)
+    vmem = pl.BlockSpec(memory_space=pltpu.VMEM)
+    smem = pl.BlockSpec(memory_space=pltpu.SMEM)
+    shape = jax.ShapeDtypeStruct
+    width = w_out.shape[1] // PIECES
+    chunk = w_out.shape[1] // CHUNKS
+    out_shape = (
+        shape((POOLED, 4096), bf16),
+        shape((CELLS, 1024), f32),
+        shape((2, 512, 4096), bf16),
+        shape((2, 1024, 512), bf16),
+        shape((2, 2, 32, 1024), f32),
+        shape((2, 16, 256), f32),
+        shape((4, 2, POOLED, 4096), bf16),
+        shape((PIECES, 512, width), bf16),
+        shape((1024, 512), bf16),
+    )
+    dma = pltpu.SemaphoreType.DMA
+    scratch = [
+        pltpu.VMEM((CELLS, 1024), bf16),
+        pltpu.VMEM((2, 8, 80, 1024), bf16),
+        pltpu.VMEM((CELLS, 256), f32),
+        pltpu.VMEM((CELLS, 256), f32),
+        pltpu.VMEM((CELLS, 256), bf16),
+        pltpu.VMEM((CELLS, 1024), bf16),
+        pltpu.VMEM((CELLS, 128), f32),
+        pltpu.VMEM((CELLS, 1024), bf16),
+        pltpu.VMEM((CELLS, 1024), bf16),
+        pltpu.VMEM((CELLS, 1024), f32),
+        pltpu.VMEM((CELLS, 256), bf16),
+        pltpu.VMEM((POOLED, CELLS), bf16),
+        pltpu.VMEM((2, 16, 1024), f32),
+        pltpu.VMEM((POOLED, 1024), f32),
+        pltpu.VMEM((POOLED, 256), f32),
+        pltpu.VMEM((POOLED, 256), f32),
+        pltpu.VMEM((POOLED, 256), bf16),
+        pltpu.VMEM((POOLED, 1024), f32),
+        pltpu.VMEM((POOLED, 128), f32),
+        pltpu.VMEM((1024, 512), bf16),
+        pltpu.VMEM((512, 4096), bf16),
+        pltpu.VMEM((8, POOLED, 1024), bf16),
+        pltpu.VMEM((8 * POOLED, 512), bf16),
+        pltpu.VMEM((8 * POOLED, 512), bf16),
+        pltpu.VMEM((8 * POOLED, 512), f32),
+        pltpu.VMEM((4, 2, POOLED, width), bf16),
+        pltpu.VMEM((2, 4, 2, POOLED, chunk), bf16),
+        pltpu.VMEM((2, 4, POOLED, chunk), bf16),
+        pltpu.VMEM((CHUNKS, 4, POOLED, chunk), bf16),
+        pltpu.VMEM((CHUNKS, 5, POOLED, chunk), bf16),
+        pltpu.VMEM((2, POOLED, chunk), bf16),
+        pltpu.VMEM((4, POOLED, 1024), bf16),
+        pltpu.VMEM((3, POOLED, 1024), bf16),
+        pltpu.VMEM((PIECES, 512, width), bf16),
+        pltpu.VMEM((1024, 512), bf16),
+        pltpu.VMEM((512, width // 2), bf16),
+        pltpu.VMEM((2, 2, 256, 1024), bf16),
+        pltpu.VMEM((2, 256, 1024), bf16),
+        pltpu.VMEM((2, 2, 4, 32, 1024), bf16),
+        pltpu.VMEM((2, 4, 32, 1024), bf16),
+        pltpu.VMEM((2, 4, 32, 1024), bf16),
+        pltpu.VMEM((2, 3, 32, 1024), bf16),
+        pltpu.VMEM((2, 32, 1024), bf16),
+        pltpu.VMEM((2, 32, 1024), bf16),
+        pltpu.VMEM((2, 16, 256), f32),
+        pltpu.VMEM((2, 16, 256), f32),
+        pltpu.VMEM((2, 16, 256), f32),
+        pltpu.VMEM((2, 4, 16, 256), f32),
+        pltpu.VMEM((2, 16, 256), f32),
+        pltpu.VMEM((2, 2, 32, 1024), f32),
+        dma((6,)),
+        dma((2, 15)),
+        dma((2, 4)),
+        dma((2, 4)),
+        dma((2, 8)),
+        dma((1 + CHUNKS,)),
+        dma((1 + CHUNKS,)),
+        dma((7,)),
+        dma((4,)),
+        dma((4,)),
+        dma((PIECES, 2, 3)),
+        dma((PIECES, 2, 3)),
+        dma((PIECES, 4)),
+        dma((PIECES, 4)),
+        dma((2,)),
+        dma((2,)),
+        dma((CHUNKS, 4)),
+        dma((CHUNKS, 5)),
+        pltpu.SemaphoreType.REGULAR,
+        dma((1,)),
+        dma((1,)),
+        dma((3,)),
+        dma((3,)),
+        dma((PIECES + 1,)),
+        dma((PIECES + 1,)),
+        dma((PIECES + 1,)),
+        dma((PIECES + 1,)),
+        dma((PIECES + 1, 2)),
+        dma((PIECES + 1, 2)),
+        dma((10,)),
+        dma((2, 13)),
+        dma((2, 13)),
+    ]
+    return pl.pallas_call(
+        layer_kernel,
+        out_shape=out_shape,
+        in_specs=[any_space, smem, any_space, any_space, any_space, any_space],
+        out_specs=(any_space, any_space, any_space, any_space, vmem, vmem, any_space, any_space, any_space),
+        scratch_shapes=scratch,
+        compiler_params=pltpu.CompilerParams(
+            collective_id=0, has_side_effects=True, vmem_limit_bytes=VMEM_BYTES
+        ),
+    )(patches, grid_sizes, pack, w_in, w_out, d_tokens)
+
+
+VMEM_BYTES = 64 * 1024 * 1024
+
+
+def small_pack(taps, gain, mp_at):
+    shards = 8
+    lane = lax.broadcasted_iota(jnp.int32, (9, 1024), 1)
+    spread = jnp.tile(taps, (1, 1024 // taps.shape[1]))
+    rows = jnp.where((lane // taps.shape[1]) == mp_at, spread, jnp.zeros_like(spread))
+    lane = lax.broadcasted_iota(jnp.int32, (1, 1024), 1)
+    spread = jnp.tile(gain[None, :], (1, shards))
+    gain_row = jnp.where((lane // gain.shape[0]) == mp_at, spread, jnp.zeros_like(spread))
+    return jnp.concatenate([rows, gain_row, jnp.zeros((6, 1024), taps.dtype)], axis=0)
+
+
+def fast_body(
+    patches, grid_sizes, w_reduce_a, taps_a, w_expand_a, gain_a,
+    w_reduce_b, taps_b, w_expand_b, gain_b, w_in, w_out, d_tokens,
+):
+    mp_at = lax.axis_index("mp")
+    pack = jnp.stack(
+        [
+            jnp.concatenate([w_reduce_a.T, small_pack(taps_a, gain_a, mp_at), w_reduce_b.T], axis=0),
+            jnp.concatenate([w_expand_a, small_pack(taps_b, gain_b, mp_at), w_expand_b], axis=0),
+        ]
+    )
+    results = layer_call(patches, grid_sizes, pack, w_in, w_out, d_tokens)
+    tokens, d_patches, gout, gin, gblk, gsml = results[:6]
+    taps_grads = lax.dynamic_slice(gsml, (0, 0, 32 * mp_at), (2, 9, 32))
+    gain_grads = lax.dynamic_slice(gsml[:, 9:13].reshape(2, 1024), (0, 128 * mp_at), (2, 128))
+    return (
+        tokens,
+        d_patches,
+        gblk[0, 0].T,
+        taps_grads[0],
+        gblk[0, 1],
+        gain_grads[0],
+        gblk[1, 0].T,
+        taps_grads[1],
+        gblk[1, 1],
+        gain_grads[1],
+        gin[0].astype(f32) + gin[1].astype(f32),
+        gout[0].astype(f32) + gout[1].astype(f32),
+    )
+
+
 def solution(mesh):
     in_specs = (
         P(("dp", "mp"), None),
@@ -339,4 +1356,5 @@
         P(None, "mp"),
         P("mp", None),
     )
-    return jax.shard_map(body, mesh=mesh, in_specs=in_specs, out_specs=out_specs, check_vma=False)
+    fits = mesh.shape["dp"] == 4 and mesh.shape["mp"] == 8
+    return jax.shard_map(fast_body if fits else body, mesh=mesh, in_specs=in_specs, out_specs=out_specs, check_vma=False)

time: 1240 us -> 329 us (0.27)
  waiting for transfers between devices: 839 us -> 0 us
  Pallas kernels: 0 us -> 302 us
  blocking collectives: 256 us -> 0 us
  matrix products: 69.2 us -> 0 us
  other arithmetic: 32.9 us -> 11 us
  between operations: 16.2 us -> 1.36 us
    reduce_scatter x6 -> x0, waiting for transfers between devices: 458 us -> none  [the longest x1 152 us: body(): lax.psum_scatter(jnp.dot(active, w_out, preferred_element_type=jnp.float3...]
    pallas_call x0 -> x1, Pallas kernels: none -> 302 us  [layer_call(): pl.pallas_call(layer_kernel, out_shape=out_shape, in_specs=[any_space, sm...]
    all_gather x8 -> x0, blocking collectives: 230 us -> none  [the longest x1 33.8 us: body(): lax.all_gather(w_reduce_a, 'mp', axis=1, tiled=True)]
    all_gather x2 -> x0, waiting for transfers between devices: 184 us -> none  [the longest x1 134 us: body(): piece = lax.all_gather(d_tokens, 'mp', axis=0, tiled=True)]
    psum x1 -> x0, waiting for transfers between devices: 101 us -> none  [body(): lax.psum(shards[0].astype(jnp.bfloat16), 'dp').astype(jnp.float32)]
    unnamed x13 -> x0, waiting for transfers between devices: 96.3 us -> none
    dot_general x24 -> x0, matrix products: 69.2 us -> none  [the longest x6 19.4 us: times_trans(): lax.dot_general(left, right, (((1,), (1,)), ((), ())), preferred_element_...]
    convert_element_type x20 -> x0, other arithmetic: 22.5 us -> none  [the longest x1 6.76 us: body(): lax.psum(grad_out_sum.astype(jnp.bfloat16), 'dp').astype(jnp.float32)]
  transfers between devices with their start and end apart: 11 -> 0, of which waited for: 11 -> 0; matrix products, arithmetic and copies ran while one was open for 6% -> 0% of each run, Pallas kernels for 0% -> 0%
where the time goes in v1:
time: 329 us; the launch traced here: 328 us
  Pallas kernels  302 us (92%)
  local copies, waits for them, and re-layouts  14 us (4%)
  other arithmetic  11 us (3%)
    pallas_call x1, Pallas kernels, layer_call(): pl.pallas_call(layer_kernel, out_shape=out_shape, in_specs=[any_space, sm...  302 us
    add x1, other arithmetic, fast_body(): gout[0].astype(f32) + gout[1].astype(f32)  8.59 us

profile of v1, /device:TPU:0, one launch (start us, length us, event | category | flops | bytes accessed | tf_op | source)
XLA Modules:
  0.0 327.9 jit_solution(4011238907142725989)
XLA Ops:
  0.7 0.7 tile.16
  1.4 0.1 tile.17
  1.5 0.7 tile.38
  2.2 0.1 tile.39
  2.4 0.7 broadcast_bitcast_fusion
  3.0 0.7 broadcast_bitcast_fusion.1
  3.7 1.7 concatenate.6
  5.4 1.7 concatenate.7
  7.2 0.8 pad_maximum_fusion.pack_in
  8.6 301.5 %shard_map.220 = (bf16[144,4096]{1,0:T(8,128)(2,1)}, f32[576,1024]{1,0:T(8,128)}, bf16[2,512,4096]{2,1,0:T(8,128)(2,1)}, bf16[2,1024,512]{2,1,0:T(8,128)(2,1)}, ...) custom-call(bf16[576,1024]{1,0:T(8,128)(2,1)} %patches_in.1, ...), custom_call_target="tpu_custom_call" | custom-call | tf_op jit(solution)/shard_map/pallas_call | solution.py:1272
  310.1 0.7 slice_bitcast_fusion.4
  310.8 0.5 slice_bitcast_fusion.5
  311.4 1.4 dynamic-slice_bitcast_fusion
  312.7 1.9 slice_bitcast_fusion
  314.6 0.0 copy-start.1
  314.6 8.6 %add_bitcast_fusion = f32[512,4096]{1,0:T(8,128)} fusion(bf16[2,512,4096]{2,1,0:T(8,128)(2,1)} %get-tuple-element.23), kind=kLoop, calls=%fused_computation | loop fusion | flops 6291456 | bytes 16777216 | tf_op jit(solution)/shard_map/add | solution.py:1325
  323.2 0.0 copy-start.2
  323.2 0.0 copy-done.1
  323.2 0.0 copy-start
  323.2 1.6 add_bitcast_fusion.1
  324.9 0.0 copy-done.2
  324.9 1.0 copy.33
  325.9 0.6 copy-done
  326.4 1.4 copy.34
  (7 shorter events, 0.1 us)
Async XLA Ops:
  314.6 8.6 %copy-start.1 = (bf16[2,1024,512]{2,1,0:T(8,128)(2,1)S(1)}, bf16[2,1024,512]{2,1,0:T(8,128)(2,1)}, u32[]{:S(2)}) copy-start(bf16[2,1024,512]{2,1,0:T(8,128)(2,1)} %get-tuple-element.22) | copy-start | bytes 6291460
  323.2 1.6 copy-start.2
  323.2 3.2 copy-start

commit v2 on v1

--- a/solution.py
+++ b/solution.py
@@ -386,12 +386,13 @@
 
 
 def layer_kernel(
-    patches_in, side_in, pack_in, w_in_in, w_out_in, cot_in,
+    patches_in, side_in, wr_a_in, taps_a_in, we_a_in, gain_a_in, wr_b_in, taps_b_in, we_b_in, gain_b_in,
+    w_in_in, w_out_in, cot_in,
     tok_out, dpat_out, gout_out, gin_out, gblk_out, gsml_out, cot_all, gx_land, gi_land,
-    xp, gw, red_a, spa_a, nar_a, norm_a, inv_a, yhi, ylo, dy, dlow, pp,
+    xp, gw, gws, red_a, spa_a, nar_a, norm_a, inv_a, yhi, ylo, dy, dlow, pp,
     tw, poolv, red_b, spa_b, nar_b, norm_b, inv_b,
     wi, wo, qs, actv, slope, dpre, dtv, tp, cr, ps, rl, tstage,
-    dr, dz, gos, gis, land,
+    dps, dr, dz, gos, gis, land,
     wgs, wgc, xs, xr, zs, zr, ys, yr, sm, smc, smx, smz, smy, gfin,
     loc, w_s, w_rz, w_rx, w_rc, sw_s, sw_r, q_s, q_rz, q_rc,
     dt_s, dt_r, dt_cs, dt_cr, t_cs, t_cr, t_s, t_r, credit,
@@ -437,12 +438,29 @@
     own = x == c
 
     load_patches = pltpu.make_async_copy(patches_in, xp, loc.at[0])
-    load_pack = pltpu.make_async_copy(pack_in.at[c], gw.at[c, mp_at], loc.at[1])
     me = 2 * z + c
-    load_cot = pltpu.make_async_copy(cot_in, cot_all.at[z, c], loc.at[2])
     load_patches.start()
-    load_pack.start()
-    load_cot.start()
+
+    own_rows = pl.ds(pl.multiple_of(16 * c, 16), 16)
+    gw[c, mp_at, 0:16, :] = wr_a_in[own_rows, :]
+    gw[c, mp_at, 32:48, :] = wr_b_in[own_rows, :]
+    gw[c, mp_at, 16:32, :] = we_a_in[own_rows, :]
+    gw[c, mp_at, 48:64, :] = we_b_in[own_rows, :]
+    unit = lax.broadcasted_iota(jnp.int32, (32, 256), 0)
+    lane = lax.broadcasted_iota(jnp.int32, (32, 256), 1)
+    place = 16 * mp_at + jnp.where(unit >= 16, unit + 112, unit)
+    spread = jnp.where(lane == place, 1.0, 0.0).astype(bf16)
+    gws[c, mp_at] = jnp.zeros((16, 256), f32)
+
+    @pl.when(c == 0)
+    def _():
+        gws[0, mp_at, 0:9, :] = dot(taps_a_in[...], spread, 1, 0)
+        gws[0, mp_at, 9:10, 0:128] = gain_a_in[...].astype(f32).reshape(1, 128)
+
+    @pl.when(c == 1)
+    def _():
+        gws[1, mp_at, 0:9, :] = dot(taps_b_in[...], spread, 1, 0)
+        gws[1, mp_at, 9:10, 0:128] = gain_b_in[...].astype(f32).reshape(1, 128)
 
     barrier = pltpu.get_barrier_semaphore()
     peers = [twin, x_peer, cross, y_peer] + [z_dev(z_at(k)) for k in range(1, zn)]
@@ -450,10 +468,11 @@
         pl.semaphore_signal(barrier, inc=1, device_id=peer, device_id_type=MESH)
     pl.semaphore_wait(barrier, len(peers))
 
-    load_pack.wait()
-    spans = ((0, 48), (48, 32))
+    spans = ((0, 16), (16, 16), (32, 32))
 
     def w_part(b, core, i):
+        if b == 3:
+            return gws.at[core, i]
         return gw.at[core, i, pl.ds(spans[b][0], spans[b][1])]
 
     def w_own(b):
@@ -471,6 +490,8 @@
             arrived(part, w_rz.at[b, k])
             start(part, part, w_s.at[b, 3 + k], w_rx.at[b, z_of], x_peer)
             start(part, part, w_s.at[b, 7 + k], w_rc.at[b, i], twin)
+
+    def w_over(b):
         for k in range(zn):
             z_of = z_at(-k)
             i = 2 * z_of + 1 - x
@@ -483,24 +504,33 @@
             arrived(w_part(b, 1 - c, i), w_rc.at[b, i])
 
     w_own(0)
+    w_own(3)
     w_own(1)
+    w_own(2)
 
     width = cot_in.shape[1] // PIECES
 
     def cot(z_of, c_of, p):
         return cot_all.at[z_of, c_of, :, pl.ds(pl.multiple_of(p * width, width), width)]
 
+    def cot_mine(p):
+        return cot_in.at[:, pl.ds(pl.multiple_of(p * width, width), width)]
+
     def cot_right(z_of, p, hop):
+        mine = cot_mine(p)
+
         @pl.when(z < zn - 1)
         def _():
             part = cot(z_of, c, p)
-            start(part, part, dt_s.at[p, 0, hop], dt_r.at[p, 0, hop], z_dev(z + 1))
+            start(mine if hop == 0 else part, part, dt_s.at[p, 0, hop], dt_r.at[p, 0, hop], z_dev(z + 1))
 
     def cot_left(z_of, p, hop):
+        mine = cot_mine(p)
+
         @pl.when(z > 0)
         def _():
             part = cot(z_of, c, p)
-            start(part, part, dt_s.at[p, 1, hop], dt_r.at[p, 1, hop], z_dev(z - 1))
+            start(mine if hop == 0 else part, part, dt_s.at[p, 1, hop], dt_r.at[p, 1, hop], z_dev(z - 1))
 
     def cot_twin(z_of, p):
         part = cot(z_of, c, p)
@@ -509,7 +539,7 @@
     def cot_own(p):
         cot_right(z, p, 0)
         cot_left(z, p, 0)
-        cot_twin(z, p)
+        start(cot_mine(p), cot(z, c, p), dt_cs.at[p, z], dt_cr.at[p, z], twin)
 
     def cot_hop(p, hop):
         @pl.when(z >= hop)
@@ -526,47 +556,55 @@
                 cot_left(z + hop, p, hop)
             cot_twin(z + hop, p)
 
-    w_forward(0)
     chunk = w_out_in.shape[1] // CHUNKS
 
     def columns(ref, j, span):
         return ref.at[:, pl.ds(j * span, span)]
 
-    @pl.when(own)
-    def _():
-        pltpu.make_async_copy(w_in_in, wi, sw_r.at[0]).start()
-        for j in range(CHUNKS):
-            pltpu.make_async_copy(
-                columns(w_out_in, j, chunk), columns(wo, j, chunk), sw_r.at[1 + j]
-            ).start()
-
-    @pl.when(jnp.logical_not(own))
-    def _():
-        start(w_in_in, wi, sw_s.at[0], sw_r.at[0], cross)
-        for j in range(CHUNKS):
-            start(
-                columns(w_out_in, j, chunk), columns(wo, j, chunk),
-                sw_s.at[1 + j], sw_r.at[1 + j], cross,
-            )
-
-    load_cot.wait()
-    for p in range(2):
+    def swap_weights():
+        @pl.when(own)
+        def _():
+            pltpu.make_async_copy(w_in_in, wi, sw_r.at[0]).start()
+            for j in range(CHUNKS):
+                pltpu.make_async_copy(
+                    columns(w_out_in, j, chunk), columns(wo, j, chunk), sw_r.at[1 + j]
+                ).start()
+
+        @pl.when(jnp.logical_not(own))
+        def _():
+            start(w_in_in, wi, sw_s.at[0], sw_r.at[0], cross)
+            for j in range(CHUNKS):
+                start(
+                    columns(w_out_in, j, chunk), columns(wo, j, chunk),
+                    sw_s.at[1 + j], sw_r.at[1 + j], cross,
+                )
+
+    w_forward(0)
+    w_forward(3)
+    w_forward(1)
+    w_over(0)
+    w_over(3)
+    for p in range(3):
         cot_own(p)
+    w_forward(2)
+    w_over(1)
     w_finish(0)
-
-    def block_weights(b):
-        rows = pl.ds(spans[b][0], 32)
-        return (
-            gw[0, :, rows, :].reshape(256, 1024),
-            gw[1, :, rows, :].reshape(256, 1024),
-        )
+    w_finish(3)
+
+    def reduce_weights(b):
+        return gw[:, :, 32 * b : 32 * b + 16, :].reshape(256, 1024)
+
+    def expand_weights(b):
+        return gw[:, :, 32 * b + 16 : 32 * b + 32, :].reshape(256, 1024)
 
     def small_weights(b):
-        total = gw[b, 0, 32:48, :].astype(f32)
+        total = gws[b, 0, 0:9, :]
         for i in range(1, 8):
-            total = total + gw[b, i, 32:48, :].astype(f32)
-        tw[b] = total
-        return total[9:10, :]
+            total = total + gws[b, i, 0:9, :]
+        tw[b, 0:9, 0:256] = total
+        for i in range(8):
+            tw[b, 9:10, 128 * i : 128 * i + 128] = gws[b, i, 9:10, 0:128]
+        return tw[b, 9:10, :]
 
     def lanes_of(h):
         return pl.ds(pl.multiple_of(h * 128, 128), 128)
@@ -583,8 +621,7 @@
         return jnp.where((row < side - 0.5) & (col < side - 0.5), 1.0, 0.0).astype(f32)
 
     load_patches.wait()
-    wr_a, we_a = block_weights(0)
-    red_a[...] = dot(xp[...], wr_a, 1, 1)
+    red_a[...] = dot(xp[...], reduce_weights(0), 1, 1)
 
     def conv_half_a(h, carry):
         lanes = lanes_of(h)
@@ -596,7 +633,10 @@
         return carry
 
     lax.fori_loop(0, 2, conv_half_a, 0)
-    dy[...] = dot(nar_a[...], we_a, 1, 0)
+    w_over(2)
+    swap_weights()
+    w_finish(1)
+    dy[...] = dot(nar_a[...], expand_weights(0), 1, 0)
 
     def normalise(wide_ref, ref, inv_ref, rows):
         widened = wide_ref[rows, :]
@@ -617,6 +657,7 @@
         return carry
 
     lax.fori_loop(0, CELLS // TILE, norm_tile, 0)
+    cot_hop(0, 1)
 
     cell = lax.broadcasted_iota(jnp.int32, (POOLED, CELLS), 1).astype(f32)
     bin_of = lax.broadcasted_iota(jnp.int32, (POOLED, CELLS), 0).astype(f32)
@@ -634,33 +675,30 @@
     pooled = dot(pp[...], yhi[...], 1, 0) + dot(pp[...], ylo[...], 1, 0)
     poolv[...] = pooled
 
-    w_forward(1)
-    w_finish(1)
+    w_finish(2)
 
     gain_b = small_weights(1)
-    wr_b, we_b = block_weights(1)
-    reduced_b = dot(pooled.astype(bf16), wr_b, 1, 1)
+    reduced_b = dot(pooled.astype(bf16), reduce_weights(1), 1, 1)
     red_b[...] = reduced_b
     activated_b = reduced_b * jax.nn.sigmoid(reduced_b)
     spatial_b = conv_forward(activated_b, tap_rows(1, pl.ds(0, 256)), POOL, edge_masks(POOL, 256))
     spa_b[...] = spatial_b
     nar_b[...] = (spatial_b * jax.nn.sigmoid(spatial_b)).astype(bf16)
-    norm_b[...] = dot(nar_b[...], we_b, 1, 0)
+    norm_b[...] = dot(nar_b[...], expand_weights(1), 1, 0)
     normed_b = normalise(norm_b, norm_b, inv_b, pl.ds(0, POOLED))
     qs[me] = (pooled + normed_b * gain_b).astype(bf16)
 
     for k in range(1, zn):
         start(qs.at[me], qs.at[me], q_s.at[k - 1], q_rz.at[k], z_dev(z_at(k)))
     start(qs.at[me], qs.at[me], q_s.at[3], q_rc.at[z], twin)
-    for p in range(2, PIECES):
-        cot_own(p)
+    cot_own(3)
+    cot_hop(1, 1)
     for k in range(1, zn):
         z_of = z_at(-k)
         slot = qs.at[2 * z_of + c]
         arrived(slot, q_rz.at[k])
         start(slot, slot, q_s.at[3 + k], q_rc.at[z_of], twin)
-    for p in range(PIECES):
-        cot_hop(p, 1)
+    cot_hop(0, 2)
     for z_of in range(zn):
         arrived(qs.at[2 * z_of + 1 - c], q_rc.at[z_of])
     arrived(wi, sw_r.at[0])
@@ -685,13 +723,24 @@
 
         @pl.when(i >= 2)
         def _():
-            left_here(tp.at[b, :, 1 - c], t_cs.at[b])
+            left_here(tp.at[b], t_cs.at[b])
             pl.semaphore_wait(credit, 1)
 
         weights = wo[:, pl.ds(pl.multiple_of(i * chunk, chunk), chunk)]
         partial = dot(actv[...], weights, 1, 0).astype(bf16)
-        tp[b] = partial.reshape(zn, 2, POOLED, chunk)
-        start(tp.at[b, :, 1 - c], cr.at[b], t_cs.at[b], t_cr.at[b], twin)
+        partial = partial.reshape(zn, 2, POOLED, chunk)
+
+        @pl.when(c == 0)
+        def _():
+            ps[i] = partial[:, 0]
+            tp[b] = partial[:, 1]
+
+        @pl.when(c == 1)
+        def _():
+            ps[i] = partial[:, 1]
+            tp[b] = partial[:, 0]
+
+        start(tp.at[b], cr.at[b], t_cs.at[b], t_cr.at[b], twin)
 
     def send_right(i, d):
         start(ps.at[i, d], rl.at[i, d + 1], t_s.at[i, d], t_r.at[i, d + 1], z_dev(z + 1))
@@ -704,7 +753,7 @@
         arrived(cr.at[b], t_cr.at[b])
 
         def add(d, carry):
-            ps[i, d] = (tp[b, d, c].astype(f32) + cr[b, d].astype(f32)).astype(bf16)
+            ps[i, d] = (ps[i, d].astype(f32) + cr[b, d].astype(f32)).astype(bf16)
             return carry
 
         lax.fori_loop(0, zn, add, 0)
@@ -791,43 +840,93 @@
         def _():
             item_final(s - zn)
 
-    def gx_part(p):
-        return gx_land.at[p]
+    def twin_rows(z_of, p):
+        arrived(cot(z_of, 1 - c, p), dt_cr.at[p, z_of])
+
+    def slot_span(z_of):
+        return pl.ds(pl.multiple_of(z_of * (2 * POOLED), 2 * POOLED), 2 * POOLED)
+
+    def load_rows(z_of, p, at):
+        @pl.when(z_of != z)
+        def _():
+            part = cot_all.at[z_of, :, :, pl.ds(p * width, width)]
+            pltpu.make_async_copy(part, dtv.at[pl.ds(at, 2)], loc.at[3]).start()
+
+        @pl.when(z_of == z)
+        def _():
+            pltpu.make_async_copy(cot(z, 1 - c, p), dtv.at[at + 1 - c], loc.at[3]).start()
+            pltpu.make_async_copy(cot_mine(p), dtv.at[at + c], loc.at[3]).start()
+
+    def piece_rows(p):
+        for z_of in range(zn):
+            twin_rows(z_of, p)
+            load_rows(z_of, p, 2 * z_of)
+        pltpu.make_async_copy(dtv, dtv, loc.at[3]).wait()
 
     def piece_work(p):
-        for z_of in range(zn):
-            arrived(cot(z_of, 1 - c, p), dt_cr.at[p, z_of])
-        load = pltpu.make_async_copy(
-            cot_all.at[:, :, :, pl.ds(pl.multiple_of(p * width, width), width)], dtv, loc.at[3]
-        )
-        load.start()
-
-        @pl.when(p >= 1)
-        def _():
-            grad_pair(p - 1)
-
-        load.wait()
-
-        def out_half(h, carry):
-            lanes = pl.ds(pl.multiple_of(h * chunk, chunk), chunk)
-            rows = dtv[:, :, :, lanes].reshape(8 * POOLED, chunk)
-            gos[p, :, lanes] = dot(actv[...], rows, 0, 0).astype(bf16)
-            return carry
+        piece_rows(p)
+        grad_part(p)
 
         def hidden_half(h, carry):
             lanes = pl.ds(pl.multiple_of(h * chunk, chunk), chunk)
-            rows = dtv[:, :, :, lanes].reshape(8 * POOLED, chunk)
+            rows = dtv[:, :, lanes].reshape(8 * POOLED, chunk)
             weights = wo[:, pl.ds(pl.multiple_of(p * width + h * chunk, chunk), chunk)]
             dpre[...] += dot(rows, weights, 1, 1)
             return carry
 
+        lax.fori_loop(0, 2, hidden_half, 0)
+
+    last = PIECES - 1
+
+    def source_last(z_of):
+        twin_rows(z_of, last)
+        load_rows(z_of, last, 2 * z_of)
+        pair = dtv.at[pl.ds(2 * z_of, 2)]
+        pltpu.make_async_copy(pair, pair, loc.at[3]).wait()
+        rows = slot_span(z_of)
+        left = dtv[pl.ds(2 * z_of, 2)].reshape(2 * POOLED, width)
+        total = dpre[rows, :] + dot(left, wo[:, last * width :], 1, 1)
+        d_hidden = (total * slope[rows, :].astype(f32)).astype(bf16)
+        half = lax.div(z_of, 2)
+        place = pl.ds(pl.multiple_of((z_of - 2 * half) * (2 * POOLED), 2 * POOLED), 2 * POOLED)
+        ylo[place, pl.ds(pl.multiple_of(half * 512, 512), 512)] = d_hidden
+        d_rows = dot(d_hidden, wi[...], 1, 1).astype(bf16)
+        dps[z_of] = d_rows.reshape(2, POOLED, 1024)
+        start(dps.at[z_of, 1 - c], dr.at[z_of], d_cs.at[z_of], d_cr.at[z_of], twin)
+
+    def source_pair(z_of):
+        arrived(dr.at[z_of], d_cr.at[z_of])
+        dps[z_of, c] = (dps[z_of, c].astype(f32) + dr[z_of].astype(f32)).astype(bf16)
+
+        @pl.when(z_of != z)
+        def _():
+            k = lax.rem(z_of - z + zn, zn)
+            start(dps.at[z_of, c], dz.at[k - 1], d_zs.at[k - 1], d_zr.at[k - 1], z_dev(z_of))
+
+    def around(hop, work):
+        def one_side(side, carry):
+            z_of = z + (2 * side - 1) * hop
+
+            @pl.when((z_of >= 0) & (z_of <= zn - 1))
+            def _():
+                work(z_of)
+
+            return carry
+
+        lax.fori_loop(0, 2, one_side, 0)
+
+    def grad_part(p):
+        def out_half(h, carry):
+            lanes = pl.ds(pl.multiple_of(h * chunk, chunk), chunk)
+            rows = dtv[:, :, lanes].reshape(8 * POOLED, chunk)
+            gos[p, :, lanes] = dot(actv[...], rows, 0, 0).astype(bf16)
+            return carry
+
         lax.fori_loop(0, 2, out_half, 0)
 
         @pl.when(jnp.logical_not(own))
         def _():
             start(gos.at[p], gx_land.at[p], gx_s.at[p], gx_r.at[p], x_peer)
-
-        lax.fori_loop(0, 2, hidden_half, 0)
 
     def gout_slice(half, p):
         return gout_out.at[half, :, pl.ds(pl.multiple_of(p * width, width), width)]
@@ -873,73 +972,8 @@
             arrived(mine, gc_r.at[p, 0])
             arrived(other, gc_r.at[p, 1])
 
-    def main_step(s, carry):
-        @pl.when(s < CHUNKS // 2)
-        def _():
-            for half in range(2):
-                j = 2 * s + half
-                arrived(wo.at[:, pl.ds(pl.multiple_of(j * chunk, chunk), chunk)], sw_r.at[1 + j])
-
-        item_step(s)
-
-        @pl.when(s < PIECES)
-        def _():
-            cot_hop(s, 2)
-
-        @pl.when((s >= 1) & (s < PIECES + 1))
-        def _():
-            cot_hop(s - 1, 3)
-
-        @pl.when((s >= 2) & (s < PIECES + 2))
-        def _():
-            piece_work(s - 2)
-
-        return carry
-
-    main_steps = PIECES + 2
-    lax.fori_loop(0, main_steps, main_step, 0)
-
-    def dh_tile(t, carry):
-        rows = pl.ds(pl.multiple_of(t * POOLED, POOLED), POOLED)
-        half = lax.div(t, 4)
-        place = pl.ds(pl.multiple_of((t - 4 * half) * POOLED, POOLED), POOLED)
-        ylo[place, pl.ds(pl.multiple_of(half * 512, 512), 512)] = (
-            dpre[rows, :] * slope[rows, :].astype(f32)
-        ).astype(bf16)
-        return carry
-
-    lax.fori_loop(0, 8, dh_tile, 0)
-    for h in range(2):
-        d_part = dot(ylo[:, 512 * h : 512 * h + 512], wi[...], 1, 1).astype(bf16)
-        dtv[2 * h : 2 * h + 2] = d_part.reshape(2, 2, POOLED, 1024)
-    start(dtv.at[:, 1 - c], dr, d_cs.at[0], d_cr.at[0], twin)
-    grad_pair(PIECES - 1)
-    gis[...] = (
-        dot(qs[0:4].reshape(4 * POOLED, 1024), ylo[:, 0:512], 0, 0)
-        + dot(qs[4:8].reshape(4 * POOLED, 1024), ylo[:, 512:1024], 0, 0)
-    ).astype(bf16)
-
-    @pl.when(jnp.logical_not(own))
-    def _():
-        start(gis, gi_land, gx_s.at[PIECES], gx_r.at[PIECES], x_peer)
-
-    arrived(dr, d_cr.at[0])
-
-    def pair_rows(d, carry):
-        dtv[d, c] = (dtv[d, c].astype(f32) + dr[d].astype(f32)).astype(bf16)
-        return carry
-
-    lax.fori_loop(0, zn, pair_rows, 0)
-    for k in range(1, zn):
-        d = z_at(k)
-        start(dtv.at[d, c], dz.at[k - 1], d_zs.at[k - 1], d_zr.at[k - 1], z_dev(d))
-
-    for p in range(PIECES):
-        grad_last(p)
-    total = dtv[z, c].astype(f32)
-    for k in range(1, zn):
-        arrived(dz.at[k - 1], d_zr.at[k - 1])
-        total = total + dz[k - 1].astype(f32)
+    def gin_slice(half):
+        return gin_out.at[half]
 
     def widened_back(d_rows, normed, gain, inv):
         dn = d_rows * gain
@@ -957,26 +991,6 @@
             sm[t, 9 + k : 10 + k, :] = d_gain[:, 256 * k : 256 * k + 256]
         sm[t, 13:16, :] = jnp.zeros((3, 256), f32)
 
-    normed_b = norm_b[...]
-    d_gain_b = jnp.sum(total * normed_b, axis=0, keepdims=True)
-    gain_b = tw[1, 9:10, :]
-    wr_b, we_b = block_weights(1)
-    dw_b = widened_back(total, normed_b, gain_b, inv_b[:, 0:1])
-    wgs[1, 1] = dot(nar_b[...], dw_b, 0, 0).astype(bf16)
-    spatial_b = spa_b[...]
-    d_spatial_b = dot(dw_b, we_b, 1, 1) * silu_slope(spatial_b)
-    reduced_b = red_b[...]
-    sig_b = jax.nn.sigmoid(reduced_b)
-    d_act_b, d_taps_b = conv_backward(
-        d_spatial_b, reduced_b * sig_b, tap_rows(1, pl.ds(0, 256)), POOL, edge_masks(POOL, 256)
-    )
-    d_red_b = (d_act_b * (sig_b * (1.0 + reduced_b * (1.0 - sig_b)))).astype(bf16)
-    wgs[1, 0] = dot(d_red_b, poolv[...].astype(bf16), 0, 0).astype(bf16)
-    for k in range(9):
-        sm[1, k : k + 1, :] = d_taps_b[k]
-    pack_small(1, d_gain_b)
-    d_pool = total + dot(d_red_b, wr_b, 1, 0)
-
     def share_core(t):
         start(wgs.at[t, 1 - c], wgc.at[t], gr_s.at[t, 0], gr_r.at[t, 0], twin)
         start(sm.at[t], smc.at[t], gr_s.at[t, 1], gr_r.at[t, 1], twin)
@@ -985,10 +999,11 @@
         arrived(wgc.at[t], gr_r.at[t, 0])
         arrived(smc.at[t], gr_r.at[t, 1])
         for i in range(8):
-            rows = pl.ds(32 * i, 32)
-            xs[t, i % 2, i // 2] = (
-                wgs[t, c, rows, :].astype(f32) + wgc[t, rows, :].astype(f32)
-            ).astype(bf16)
+            for h in range(2):
+                rows = pl.ds(128 * h + 16 * i, 16)
+                xs[t, i % 2, i // 2, 16 * h : 16 * h + 16] = (
+                    wgs[t, c, rows, :].astype(f32) + wgc[t, rows, :].astype(f32)
+                ).astype(bf16)
         left_here(sm.at[t], gr_s.at[t, 1])
         sm[t] = sm[t] + smc[t]
         start(xs.at[t, 1 - x], xr.at[t], gr_s.at[t, 2], gr_r.at[t, 2], x_peer)
@@ -1037,80 +1052,212 @@
         left_here(sm.at[t], gr_s.at[t, 11])
         left_here(gfin.at[t, c], gr_s.at[t, 12])
 
-    share_core(1)
-
-    high, low = split_low(d_pool)
-    dy[...] = dot(pp[...], high, 0, 0) + dot(pp[...], low, 0, 0)
-    gain_a = tw[0, 9:10, :]
-    wr_a, we_a = block_weights(0)
-
-    def back_tile(t, d_gain):
-        rows = pl.ds(pl.multiple_of(t * TILE, TILE), TILE)
-        d_rows = dy[rows, :]
-        normed = norm_a[rows, :].astype(f32)
-        yhi[rows, :] = widened_back(d_rows, normed, gain_a, inv_a[rows, 0:1])
-        return d_gain + jnp.sum(d_rows * normed, axis=0, keepdims=True)
-
-    d_gain_a = lax.fori_loop(0, CELLS // TILE, back_tile, jnp.zeros((1, 1024), f32))
-    wgs[0, 1] = dot(nar_a[...], yhi[...], 0, 0).astype(bf16)
-    share_x(1)
-    spa_a[...] = dot(yhi[...], we_a, 1, 1) * silu_slope(spa_a[...])
-
-    def conv_back_half_a(h, carry):
-        lanes = lanes_of(h)
-        reduced = red_a[:, lanes]
-        sig = jax.nn.sigmoid(reduced)
-        mask = cell_mask()
-        d_act, d_taps = conv_backward(
-            spa_a[:, lanes], reduced * sig * mask, tap_rows(0, lanes), GRID, edge_masks(GRID, 128)
+    def back_second():
+        total = dps[z, c].astype(f32)
+        for k in range(1, zn):
+            arrived(dz.at[k - 1], d_zr.at[k - 1])
+            total = total + dz[k - 1].astype(f32)
+        normed_b = norm_b[...]
+        d_gain_b = jnp.sum(total * normed_b, axis=0, keepdims=True)
+        gain_b = tw[1, 9:10, :]
+        dw_b = widened_back(total, normed_b, gain_b, inv_b[:, 0:1])
+        wgs[1, 1] = dot(nar_b[...], dw_b, 0, 0).astype(bf16)
+        spatial_b = spa_b[...]
+        d_spatial_b = dot(dw_b, expand_weights(1), 1, 1) * silu_slope(spatial_b)
+        reduced_b = red_b[...]
+        sig_b = jax.nn.sigmoid(reduced_b)
+        d_act_b, d_taps_b = conv_backward(
+            d_spatial_b, reduced_b * sig_b, tap_rows(1, pl.ds(0, 256)), POOL, edge_masks(POOL, 256)
         )
-        dlow[:, lanes] = (d_act * mask * (sig * (1.0 + reduced * (1.0 - sig)))).astype(bf16)
+        d_red_b = (d_act_b * (sig_b * (1.0 + reduced_b * (1.0 - sig_b)))).astype(bf16)
+        wgs[1, 0] = dot(d_red_b, poolv[...].astype(bf16), 0, 0).astype(bf16)
         for k in range(9):
-            sm[0, k : k + 1, lanes] = d_taps[k]
+            sm[1, k : k + 1, :] = d_taps_b[k]
+        pack_small(1, d_gain_b)
+        d_pool = total + dot(d_red_b, reduce_weights(1), 1, 0)
+        high, low = split_low(d_pool)
+        dy[...] = dot(pp[...], high, 0, 0) + dot(pp[...], low, 0, 0)
+
+    def back_first_norm():
+        gain_a = tw[0, 9:10, :]
+
+        def back_tile(t, d_gain):
+            rows = pl.ds(pl.multiple_of(t * TILE, TILE), TILE)
+            d_rows = dy[rows, :]
+            normed = norm_a[rows, :].astype(f32)
+            yhi[rows, :] = widened_back(d_rows, normed, gain_a, inv_a[rows, 0:1])
+            return d_gain + jnp.sum(d_rows * normed, axis=0, keepdims=True)
+
+        d_gain_a = lax.fori_loop(0, CELLS // TILE, back_tile, jnp.zeros((1, 1024), f32))
+        pack_small(0, d_gain_a)
+        wgs[0, 1] = dot(nar_a[...], yhi[...], 0, 0).astype(bf16)
+
+    def back_first_conv():
+        spa_a[...] = dot(yhi[...], expand_weights(0), 1, 1) * silu_slope(spa_a[...])
+
+        def conv_back_half_a(h, carry):
+            lanes = lanes_of(h)
+            reduced = red_a[:, lanes]
+            sig = jax.nn.sigmoid(reduced)
+            mask = cell_mask()
+            d_act, d_taps = conv_backward(
+                spa_a[:, lanes], reduced * sig * mask, tap_rows(0, lanes), GRID, edge_masks(GRID, 128)
+            )
+            dlow[:, lanes] = (d_act * mask * (sig * (1.0 + reduced * (1.0 - sig)))).astype(bf16)
+            for k in range(9):
+                sm[0, k : k + 1, lanes] = d_taps[k]
+            return carry
+
+        lax.fori_loop(0, 2, conv_back_half_a, 0)
+        wgs[0, 0] = dot(dlow[...], xp[...], 0, 0).astype(bf16)
+
+    store_dpat = pltpu.make_async_copy(dy, dpat_out, loc.at[5])
+
+    def back_first_rows():
+        dy[...] += dot(dlow[...], reduce_weights(0), 1, 0)
+        store_dpat.start()
+
+    def gin_part():
+        gis[...] = (
+            dot(qs[0:4].reshape(4 * POOLED, 1024), ylo[:, 0:512], 0, 0)
+            + dot(qs[4:8].reshape(4 * POOLED, 1024), ylo[:, 512:1024], 0, 0)
+        ).astype(bf16)
+
+        @pl.when(jnp.logical_not(own))
+        def _():
+            start(gis, gi_land, gx_s.at[PIECES], gx_r.at[PIECES], x_peer)
+
+    def gin_pair():
+        @pl.when(own)
+        def _():
+            arrived(gi_land, gx_r.at[PIECES])
+            for h in range(2):
+                rows = pl.ds(512 * h, 512)
+                load = pltpu.make_async_copy(gi_land.at[rows], land, loc.at[4])
+                load.start()
+                load.wait()
+                gis[rows, :] = (gis[rows, :].astype(f32) + land[...].astype(f32)).astype(bf16)
+            start(gis, gin_slice(y), gy_s.at[PIECES], gy_r.at[PIECES], y_peer)
+            start(gis, gin_slice(y), gc_s.at[PIECES, 0], gc_r.at[PIECES, 0], twin)
+            pltpu.make_async_copy(gis, gin_slice(y), gl.at[PIECES]).start()
+
+    def gin_last():
+        @pl.when(own)
+        def _():
+            arrived(gin_slice(1 - y), gy_r.at[PIECES])
+            start(gin_slice(1 - y), gin_slice(1 - y), gc_s.at[PIECES, 1], gc_r.at[PIECES, 1], twin)
+
+    def main_step(s, carry):
+        def at(step):
+            return pl.when(s == step)
+
+        @pl.when(s < CHUNKS // 2)
+        def _():
+            for half in range(2):
+                j = 2 * s + half
+                arrived(wo.at[:, pl.ds(pl.multiple_of(j * chunk, chunk), chunk)], sw_r.at[1 + j])
+
+        @at(0)
+        def _():
+            cot_hop(2, 1)
+            cot_hop(1, 2)
+            cot_hop(0, 3)
+
+        @at(1)
+        def _():
+            cot_hop(3, 1)
+            cot_hop(2, 2)
+            piece_work(0)
+
+        @at(2)
+        def _():
+            cot_hop(1, 3)
+
+        @at(3)
+        def _():
+            cot_hop(3, 2)
+            piece_work(1)
+            grad_pair(0)
+
+        @at(4)
+        def _():
+            cot_hop(2, 3)
+
+        @at(5)
+        def _():
+            piece_work(2)
+            grad_pair(1)
+            grad_last(0)
+            source_last(z)
+            around(1, source_last)
+
+        @at(6)
+        def _():
+            cot_hop(3, 3)
+            source_pair(z)
+            around(1, source_pair)
+            around(2, source_last)
+
+        @at(7)
+        def _():
+            around(3, source_last)
+            around(2, source_pair)
+            grad_part(3)
+            around(3, source_pair)
+            grad_pair(2)
+            grad_last(1)
+
+        @at(8)
+        def _():
+            gin_part()
+
+        @at(9)
+        def _():
+            back_second()
+            share_core(1)
+
+        @at(10)
+        def _():
+            back_first_norm()
+            share_x(1)
+            grad_pair(3)
+            grad_last(2)
+
+        @at(11)
+        def _():
+            back_first_conv()
+            share_core(0)
+            share_z(1)
+            back_first_rows()
+
+        @at(12)
+        def _():
+            share_x(0)
+            share_y(1)
+            gin_pair()
+
+        @at(13)
+        def _():
+            share_z(0)
+            share_twin(1)
+            grad_last(3)
+
+        @at(14)
+        def _():
+            share_y(0)
+
+        @at(15)
+        def _():
+            share_twin(0)
+            gin_last()
+
+        @pl.when((s >= CHUNKS) | (lax.rem(s, 2) == 0))
+        def _():
+            item_step(jnp.where(s < CHUNKS, lax.div(s, 2), s - CHUNKS // 2))
+
         return carry
 
-    lax.fori_loop(0, 2, conv_back_half_a, 0)
-    wgs[0, 0] = dot(dlow[...], xp[...], 0, 0).astype(bf16)
-    pack_small(0, d_gain_a)
-    share_core(0)
-    share_z(1)
-    dy[...] += dot(dlow[...], wr_a, 1, 0)
-    store_dpat = pltpu.make_async_copy(dy, dpat_out, loc.at[5])
-    store_dpat.start()
-    share_x(0)
-    share_y(1)
-
-    def gin_slice(half):
-        return gin_out.at[half]
-
-    @pl.when(own)
-    def _():
-        arrived(gi_land, gx_r.at[PIECES])
-        for h in range(2):
-            rows = pl.ds(512 * h, 512)
-            load = pltpu.make_async_copy(gi_land.at[rows], land, loc.at[4])
-            load.start()
-            load.wait()
-            gis[rows, :] = (gis[rows, :].astype(f32) + land[...].astype(f32)).astype(bf16)
-        start(gis, gin_slice(y), gy_s.at[PIECES], gy_r.at[PIECES], y_peer)
-        start(gis, gin_slice(y), gc_s.at[PIECES, 0], gc_r.at[PIECES, 0], twin)
-        pltpu.make_async_copy(gis, gin_slice(y), gl.at[PIECES]).start()
-
-    share_z(0)
-    share_twin(1)
-
-    def tail_step(s, carry):
-        item_step(s)
-        return carry
-
-    lax.fori_loop(main_steps, CHUNKS + zn, tail_step, 0)
-    share_y(0)
-    share_twin(0)
-
-    @pl.when(own)
-    def _():
-        arrived(gin_slice(1 - y), gy_r.at[PIECES])
-        start(gin_slice(1 - y), gin_slice(1 - y), gc_s.at[PIECES, 1], gc_r.at[PIECES, 1], twin)
+    lax.fori_loop(0, 2 * CHUNKS, main_step, 0)
 
     share_done(1)
     share_done(0)
@@ -1136,14 +1283,16 @@
     store_dpat.wait()
     for b in range(2):
         pltpu.make_async_copy(tstage.at[b], tok_slice(b), gl.at[8 + b]).wait()
-        left_here(tp.at[b, :, 1 - c], t_cs.at[b])
+        left_here(tp.at[b], t_cs.at[b])
+    for b in range(4):
         for k in range(15):
             left_here(w_part(b, c, 0), w_s.at[b, k])
     for k in range(7):
         left_here(qs.at[0], q_s.at[k])
-    left_here(dtv.at[:, 0], d_cs.at[0])
+    for k in range(zn):
+        left_here(dps.at[0, 0], d_cs.at[k])
     for k in range(zn - 1):
-        left_here(dtv.at[0, 0], d_zs.at[k])
+        left_here(dps.at[0, 0], d_zs.at[k])
     for p in range(PIECES):
         for z_of in range(zn):
             left_here(cot(0, 0, p), dt_cs.at[p, z_of])
@@ -1166,7 +1315,9 @@
     lax.fori_loop(0, CHUNKS, drain_items, 0)
 
 
-def layer_call(patches, grid_sizes, pack, w_in, w_out, d_tokens):
+def layer_call(
+    patches, grid_sizes, wr_a, taps_a, we_a, gain_a, wr_b, taps_b, we_b, gain_b, w_in, w_out, d_tokens
+):
     any_space = pl.BlockSpec(memory_space=pl.ANY)
     vmem = pl.BlockSpec(memory_space=pltpu.VMEM)
     smem = pl.BlockSpec(memory_space=pltpu.SMEM)
@@ -1187,7 +1338,8 @@
     dma = pltpu.SemaphoreType.DMA
     scratch = [
         pltpu.VMEM((CELLS, 1024), bf16),
-        pltpu.VMEM((2, 8, 80, 1024), bf16),
+        pltpu.VMEM((2, 8, 64, 1024), bf16),
+        pltpu.VMEM((2, 8, 16, 256), f32),
         pltpu.VMEM((CELLS, 256), f32),
         pltpu.VMEM((CELLS, 256), f32),
         pltpu.VMEM((CELLS, 256), bf16),
@@ -1211,12 +1363,13 @@
         pltpu.VMEM((8 * POOLED, 512), bf16),
         pltpu.VMEM((8 * POOLED, 512), bf16),
         pltpu.VMEM((8 * POOLED, 512), f32),
-        pltpu.VMEM((4, 2, POOLED, width), bf16),
-        pltpu.VMEM((2, 4, 2, POOLED, chunk), bf16),
+        pltpu.VMEM((8, POOLED, width), bf16),
+        pltpu.VMEM((2, 4, POOLED, chunk), bf16),
         pltpu.VMEM((2, 4, POOLED, chunk), bf16),
         pltpu.VMEM((CHUNKS, 4, POOLED, chunk), bf16),
         pltpu.VMEM((CHUNKS, 5, POOLED, chunk), bf16),
         pltpu.VMEM((2, POOLED, chunk), bf16),
+        pltpu.VMEM((4, 2, POOLED, 1024), bf16),
         pltpu.VMEM((4, POOLED, 1024), bf16),
         pltpu.VMEM((3, POOLED, 1024), bf16),
         pltpu.VMEM((PIECES, 512, width), bf16),
@@ -1237,10 +1390,10 @@
         pltpu.VMEM((2, 16, 256), f32),
         pltpu.VMEM((2, 2, 32, 1024), f32),
         dma((6,)),
-        dma((2, 15)),
-        dma((2, 4)),
-        dma((2, 4)),
-        dma((2, 8)),
+        dma((4, 15)),
+        dma((4, 4)),
+        dma((4, 4)),
+        dma((4, 8)),
         dma((1 + CHUNKS,)),
         dma((1 + CHUNKS,)),
         dma((7,)),
@@ -1255,8 +1408,8 @@
         dma((CHUNKS, 4)),
         dma((CHUNKS, 5)),
         pltpu.SemaphoreType.REGULAR,
-        dma((1,)),
-        dma((1,)),
+        dma((4,)),
+        dma((4,)),
         dma((3,)),
         dma((3,)),
         dma((PIECES + 1,)),
@@ -1272,57 +1425,103 @@
     return pl.pallas_call(
         layer_kernel,
         out_shape=out_shape,
-        in_specs=[any_space, smem, any_space, any_space, any_space, any_space],
+        in_specs=[any_space, smem] + [vmem] * 8 + [any_space] * 3,
         out_specs=(any_space, any_space, any_space, any_space, vmem, vmem, any_space, any_space, any_space),
         scratch_shapes=scratch,
         compiler_params=pltpu.CompilerParams(
             collective_id=0, has_side_effects=True, vmem_limit_bytes=VMEM_BYTES
         ),
-    )(patches, grid_sizes, pack, w_in, w_out, d_tokens)
+    )(
+        patches, grid_sizes, wr_a, taps_a, we_a, gain_a, wr_b, taps_b, we_b, gain_b, w_in, w_out, d_tokens
+    )
 
 
 VMEM_BYTES = 64 * 1024 * 1024
 
 
-def small_pack(taps, gain, mp_at):
-    shards = 8
-    lane = lax.broadcasted_iota(jnp.int32, (9, 1024), 1)
-    spread = jnp.tile(taps, (1, 1024 // taps.shape[1]))
-    rows = jnp.where((lane // taps.shape[1]) == mp_at, spread, jnp.zeros_like(spread))
-    lane = lax.broadcasted_iota(jnp.int32, (1, 1024), 1)
-    spread = jnp.tile(gain[None, :], (1, shards))
-    gain_row = jnp.where((lane // gain.shape[0]) == mp_at, spread, jnp.zeros_like(spread))
-    return jnp.concatenate([rows, gain_row, jnp.zeros((6, 1024), taps.dtype)], axis=0)
+FINISH = 8
+
+
+def finish_kernel(
+    tok_in, dpat_in, gout_in, gin_in, gblk_in, gsml_in,
+    tok, dpat, gout, gin, gra, gta, gea, gga, grb, gtb, geb, ggb,
+):
+    tok[...] = tok_in[...]
+    dpat[...] = dpat_in[...]
+    gout[...] = gout_in[0].astype(f32) + gout_in[1].astype(f32)
+    gin[...] = gin_in[0].astype(f32) + gin_in[1].astype(f32)
+
+    @pl.when(pl.program_id(0) == 0)
+    def _():
+        mp_at = lax.axis_index("mp")
+        for t, outs in enumerate(((gra, gta, gea, gga), (grb, gtb, geb, ggb))):
+            reduce, taps, expand, gain = outs
+            reduce[...] = gblk_in[t, 0]
+            expand[...] = gblk_in[t, 1]
+            turned = pltpu.roll(gsml_in[t], lax.rem(256 - 16 * mp_at, 256), 1)
+            taps[:, 0:16] = turned[0:9, 0:16]
+            taps[:, 16:32] = turned[0:9, 128:144]
+            for i in range(8):
+                @pl.when(mp_at == i)
+                def _(t=t, i=i, gain=gain):
+                    lanes = 128 * (i % 2)
+                    gain[...] = gsml_in[t, 9 + i // 2 : 10 + i // 2, lanes : lanes + 128]
+
+
+def finish_call(tokens, d_patches, gout, gin, gblk, gsml):
+    shape = jax.ShapeDtypeStruct
+    columns = tokens.shape[1] // FINISH
+
+    def whole(*dims):
+        return pl.BlockSpec(dims, lambda i: (0,) * len(dims))
+
+    one = [whole(32, 1024), whole(9, 32), whole(32, 1024), whole(1, 128)]
+    one_shape = [shape((32, 1024), f32), shape((9, 32), f32), shape((32, 1024), f32), shape((1, 128), f32)]
+    return pl.pallas_call(
+        finish_kernel,
+        grid=(FINISH,),
+        out_shape=[
+            shape(tokens.shape, bf16),
+            shape(d_patches.shape, f32),
+            shape(gout.shape[1:], f32),
+            shape(gin.shape[1:], f32),
+        ]
+        + one_shape * 2,
+        in_specs=[
+            pl.BlockSpec((POOLED, columns), lambda i: (0, i)),
+            pl.BlockSpec((CELLS // FINISH, 1024), lambda i: (i, 0)),
+            pl.BlockSpec((2, 512 // FINISH, 4096), lambda i: (0, i, 0)),
+            pl.BlockSpec((2, 1024 // FINISH, 512), lambda i: (0, i, 0)),
+            whole(2, 2, 32, 1024),
+            whole(2, 16, 256),
+        ],
+        out_specs=[
+            pl.BlockSpec((POOLED, columns), lambda i: (0, i)),
+            pl.BlockSpec((CELLS // FINISH, 1024), lambda i: (i, 0)),
+            pl.BlockSpec((512 // FINISH, 4096), lambda i: (i, 0)),
+            pl.BlockSpec((1024 // FINISH, 512), lambda i: (i, 0)),
+        ]
+        + one * 2,
+        compiler_params=pltpu.CompilerParams(vmem_limit_bytes=VMEM_BYTES),
+    )(tokens, d_patches, gout, gin, gblk, gsml)
 
 
 def fast_body(
     patches, grid_sizes, w_reduce_a, taps_a, w_expand_a, gain_a,
     w_reduce_b, taps_b, w_expand_b, gain_b, w_in, w_out, d_tokens,
 ):
-    mp_at = lax.axis_index("mp")
-    pack = jnp.stack(
-        [
-            jnp.concatenate([w_reduce_a.T, small_pack(taps_a, gain_a, mp_at), w_reduce_b.T], axis=0),
-            jnp.concatenate([w_expand_a, small_pack(taps_b, gain_b, mp_at), w_expand_b], axis=0),
-        ]
-    )
-    results = layer_call(patches, grid_sizes, pack, w_in, w_out, d_tokens)
-    tokens, d_patches, gout, gin, gblk, gsml = results[:6]
-    taps_grads = lax.dynamic_slice(gsml, (0, 0, 32 * mp_at), (2, 9, 32))
-    gain_grads = lax.dynamic_slice(gsml[:, 9:13].reshape(2, 1024), (0, 128 * mp_at), (2, 128))
+    results = layer_call(
+        patches, grid_sizes, w_reduce_a.T, taps_a, w_expand_a, gain_a,
+        w_reduce_b.T, taps_b, w_expand_b, gain_b, w_in, w_out, d_tokens,
+    )
+    (
+        tokens, d_patches, gout, gin, reduce_a, tap_a, expand_a, scale_a, reduce_b, tap_b, expand_b, scale_b
+    ) = finish_call(*results[:6])
     return (
-        tokens,
-        d_patches,
-        gblk[0, 0].T,
-        taps_grads[0],
-        gblk[0, 1],
-        gain_grads[0],
-        gblk[1, 0].T,
-        taps_grads[1],
-        gblk[1, 1],
-        gain_grads[1],
-        gin[0].astype(f32) + gin[1].astype(f32),
-        gout[0].astype(f32) + gout[1].astype(f32),
+        tokens, d_patches,
+        reduce_a.T, tap_a, expand_a, scale_a.reshape(-1),
+        reduce_b.T, tap_b, expand_b, scale_b.reshape(-1),
+        gin, gout,
     )
 
 

time: 329 us -> 244 us (0.74)
  Pallas kernels: 302 us -> 242 us
  local copies, waits for them, and re-layouts: 14 us -> 0 us
  other arithmetic: 11 us -> 0 us
    pallas_call x1, Pallas kernels: 302 us -> 229 us  [layer_call(): pl.pallas_call(layer_kernel, out_shape=out_shape, in_specs=[any_space, sm...]
    pallas_call x0 -> x1, Pallas kernels: none -> 12.7 us  [finish_call(): pl.pallas_call(finish_kernel, grid=(FINISH,), out_shape=[shape(tokens.sha...]
    add x2 -> x0, other arithmetic: 10.2 us -> none  [the longest x1 8.59 us: fast_body(): gout[0].astype(f32) + gout[1].astype(f32)]
    unnamed x12 -> x0, local copies, waits for them, and re-layouts: 5.04 us -> none
    squeeze x3 -> x0, local copies, waits for them, and re-layouts: 3.79 us -> none  [the longest x1 1.89 us: fast_body(): gblk[1, 1]]
    concatenate x2 -> x0, local copies, waits for them, and re-layouts: 3.44 us -> none  [the longest x1 1.72 us: fast_body(): jnp.concatenate([w_reduce_a.T, small_pack(taps_a, gain_a, mp_at), w_reduc...]
where the time goes in v2:
time: 244 us; the launch traced here: 243 us
  Pallas kernels  242 us (99%)
    pallas_call x1, Pallas kernels, layer_call(): pl.pallas_call(layer_kernel, out_shape=out_shape, in_specs=[any_space, sm...  229 us
    pallas_call x1, Pallas kernels, finish_call(): pl.pallas_call(finish_kernel, grid=(FINISH,), out_shape=[shape(tokens.sha...  12.7 us

profile of v2, /device:TPU:0, one launch (start us, length us, event | category | flops | bytes accessed | tf_op | source)
XLA Modules:
  0.0 243.0 jit_solution(9744362801895741605)
XLA Ops:
  1.3 228.8 %shard_map.220 = (bf16[144,4096]{1,0:T(8,128)(2,1)}, f32[576,1024]{1,0:T(8,128)}, bf16[2,512,4096]{2,1,0:T(8,128)(2,1)}, bf16[2,1024,512]{2,1,0:T(8,128)(2,1)}, ...) custom-call(bf16[576,1024]{1,0:T(8,128)(2,1)} %patches_in.1, ...), custom_call_target="tpu_custom_call" | custom-call | tf_op jit(solution)/shard_map/pallas_call | solution.py:1425
  230.1 12.7 %shard_map.221 = (bf16[144,4096]{1,0:T(8,128)(2,1)}, f32[576,1024]{1,0:T(8,128)}, f32[512,4096]{1,0:T(8,128)}, f32[1024,512]{1,0:T(8,128)}, f32[32,1024]{1,0:T(8...) custom-call(bf16[144,4096]{1,0:T(8,128)(2,1)} %get-tuple-element.30., ...), custom_call_target="tpu_custom_call" | custom-call | tf_op jit(solution)/shard_map/pallas_call | solution.py:1480

commit v3 on v2

--- a/solution.py
+++ b/solution.py
@@ -388,15 +388,15 @@
 def layer_kernel(
     patches_in, side_in, wr_a_in, taps_a_in, we_a_in, gain_a_in, wr_b_in, taps_b_in, we_b_in, gain_b_in,
     w_in_in, w_out_in, cot_in,
-    tok_out, dpat_out, gout_out, gin_out, gblk_out, gsml_out, cot_all, gx_land, gi_land,
+    tok_out, dpat_out, gout_out, gin_out, gblk_out, gsml_out, cot_all, gfl,
     xp, gw, gws, red_a, spa_a, nar_a, norm_a, inv_a, yhi, ylo, dy, dlow, pp,
     tw, poolv, red_b, spa_b, nar_b, norm_b, inv_b,
     wi, wo, qs, actv, slope, dpre, dtv, tp, cr, ps, rl, tstage,
-    dps, dr, dz, gos, gis, land,
+    dps, dr, dz, gos, gis, gyl, land,
     wgs, wgc, xs, xr, zs, zr, ys, yr, sm, smc, smx, smz, smy, gfin,
-    loc, w_s, w_rz, w_rx, w_rc, sw_s, sw_r, q_s, q_rz, q_rc,
+    loc, w_s, w_rz, w_rx, w_rc, sw_s, sw_r, sy_s, sy_r, q_s, q_r, q_cs, q_rc,
     dt_s, dt_r, dt_cs, dt_cr, t_cs, t_cr, t_s, t_r, credit,
-    d_cs, d_cr, d_zs, d_zr, gx_s, gx_r, gy_s, gy_r, gc_s, gc_r, gl,
+    d_cs, d_cr, d_zs, d_zr, gy_s, gy_r, gx_s, gx_r, ga_s, ga_r, gc_s, gc_r, gl,
     gr_s, gr_r,
 ):
     dp_at = lax.axis_index("dp")
@@ -412,8 +412,19 @@
 
     twin = device(x, y, z, 1 - c)
     x_peer = device(1 - x, y, z, c)
-    cross = device(1 - x, y, z, 1 - c)
     y_peer = device(x, 1 - y, z, c)
+    z_high = lax.div(z, 2)
+    z_low = lax.rem(z, 2)
+    z_near = z + 1 - 2 * z_low
+    z_far = z + 2 - 4 * z_high
+    z_peer = device(x, y, z_near, c)
+    far_peer = device(x, y, z_far, c)
+    cross = device(x, y, z_far, 1 - c)
+    corner = device(1 - x, y, z_near, c)
+    slot_own = 2 * z_low + x
+    slot_x = 2 * z_low + 1 - x
+    slot_z = 2 * (1 - z_low) + x
+    slot_corner = 2 * (1 - z_low) + 1 - x
 
     def z_at(step):
         return lax.rem(z + step + zn, zn)
@@ -435,10 +446,10 @@
     def left_here(src, send):
         pltpu.make_async_copy(src, src, send).wait()
 
-    own = x == c
+    own = z_high == c
 
     load_patches = pltpu.make_async_copy(patches_in, xp, loc.at[0])
-    me = 2 * z + c
+    me = 2 * slot_own + c
     load_patches.start()
 
     own_rows = pl.ds(pl.multiple_of(16 * c, 16), 16)
@@ -463,7 +474,7 @@
         gws[1, mp_at, 9:10, 0:128] = gain_b_in[...].astype(f32).reshape(1, 128)
 
     barrier = pltpu.get_barrier_semaphore()
-    peers = [twin, x_peer, cross, y_peer] + [z_dev(z_at(k)) for k in range(1, zn)]
+    peers = [twin, x_peer, cross, y_peer, corner] + [z_dev(z_at(k)) for k in range(1, zn)]
     for peer in peers:
         pl.semaphore_signal(barrier, inc=1, device_id=peer, device_id_type=MESH)
     pl.semaphore_wait(barrier, len(peers))
@@ -503,93 +514,73 @@
         for i in range(8):
             arrived(w_part(b, 1 - c, i), w_rc.at[b, i])
 
-    w_own(0)
-    w_own(3)
-    w_own(1)
-    w_own(2)
-
     width = cot_in.shape[1] // PIECES
 
-    def cot(z_of, c_of, p):
-        return cot_all.at[z_of, c_of, :, pl.ds(pl.multiple_of(p * width, width), width)]
+    def cot(slot, c_of, p):
+        return cot_all.at[slot, c_of, :, pl.ds(pl.multiple_of(p * width, width), width)]
 
     def cot_mine(p):
         return cot_in.at[:, pl.ds(pl.multiple_of(p * width, width), width)]
 
-    def cot_right(z_of, p, hop):
-        mine = cot_mine(p)
-
-        @pl.when(z < zn - 1)
-        def _():
-            part = cot(z_of, c, p)
-            start(mine if hop == 0 else part, part, dt_s.at[p, 0, hop], dt_r.at[p, 0, hop], z_dev(z + 1))
-
-    def cot_left(z_of, p, hop):
-        mine = cot_mine(p)
-
-        @pl.when(z > 0)
-        def _():
-            part = cot(z_of, c, p)
-            start(mine if hop == 0 else part, part, dt_s.at[p, 1, hop], dt_r.at[p, 1, hop], z_dev(z - 1))
-
-    def cot_twin(z_of, p):
-        part = cot(z_of, c, p)
-        start(part, part, dt_cs.at[p, z_of], dt_cr.at[p, z_of], twin)
-
-    def cot_own(p):
-        cot_right(z, p, 0)
-        cot_left(z, p, 0)
-        start(cot_mine(p), cot(z, c, p), dt_cs.at[p, z], dt_cr.at[p, z], twin)
-
-    def cot_hop(p, hop):
-        @pl.when(z >= hop)
-        def _():
-            arrived(cot(z - hop, c, p), dt_r.at[p, 0, hop - 1])
-            if hop < zn - 1:
-                cot_right(z - hop, p, hop)
-            cot_twin(z - hop, p)
-
-        @pl.when(z + hop <= zn - 1)
-        def _():
-            arrived(cot(z + hop, c, p), dt_r.at[p, 1, hop - 1])
-            if hop < zn - 1:
-                cot_left(z + hop, p, hop)
-            cot_twin(z + hop, p)
+    def cot_twin(slot, p):
+        part = cot(slot, c, p)
+        start(part, part, dt_cs.at[p, slot], dt_cr.at[p, slot], twin)
+
+    def cot_own_z(p):
+        start(cot_mine(p), cot(slot_own, c, p), dt_s.at[p, 1], dt_r.at[p, 1], z_peer)
+
+    def cot_own_x(p):
+        start(cot_mine(p), cot(slot_own, c, p), dt_s.at[p, 0], dt_r.at[p, 0], x_peer)
+
+    def cot_own_twin(p):
+        start(cot_mine(p), cot(slot_own, c, p), dt_cs.at[p, slot_own], dt_cr.at[p, slot_own], twin)
+
+    def cot_over_z(p):
+        part = cot(slot_z, c, p)
+        arrived(part, dt_r.at[p, 1])
+        start(part, part, dt_s.at[p, 2], dt_r.at[p, 2], x_peer)
+        cot_twin(slot_z, p)
+
+    def cot_over_x(p):
+        arrived(cot(slot_x, c, p), dt_r.at[p, 0])
+        cot_twin(slot_x, p)
+
+    def cot_corner(p):
+        arrived(cot(slot_corner, c, p), dt_r.at[p, 2])
+        cot_twin(slot_corner, p)
 
     chunk = w_out_in.shape[1] // CHUNKS
 
-    def columns(ref, j, span):
-        return ref.at[:, pl.ds(j * span, span)]
-
-    def swap_weights():
+    def w_half(ref, j, half):
+        if j == 0:
+            return ref.at[pl.ds(pl.multiple_of(512 * half, 512), 512)]
+        return ref.at[:, pl.ds(pl.multiple_of((j - 1) * width + half * chunk, chunk), chunk)]
+
+    def swap_refs(j):
+        return (w_in_in, wi) if j == 0 else (w_out_in, wo)
+
+    def swap_send(j):
+        src, dst = swap_refs(j)
+
         @pl.when(own)
         def _():
-            pltpu.make_async_copy(w_in_in, wi, sw_r.at[0]).start()
-            for j in range(CHUNKS):
-                pltpu.make_async_copy(
-                    columns(w_out_in, j, chunk), columns(wo, j, chunk), sw_r.at[1 + j]
-                ).start()
+            pltpu.make_async_copy(w_half(src, j, y), w_half(dst, j, y), sw_r.at[j]).start()
+            pltpu.make_async_copy(w_half(src, j, 1 - y), w_half(dst, j, 1 - y), sy_r.at[j]).start()
 
         @pl.when(jnp.logical_not(own))
         def _():
-            start(w_in_in, wi, sw_s.at[0], sw_r.at[0], cross)
-            for j in range(CHUNKS):
-                start(
-                    columns(w_out_in, j, chunk), columns(wo, j, chunk),
-                    sw_s.at[1 + j], sw_r.at[1 + j], cross,
-                )
-
-    w_forward(0)
-    w_forward(3)
-    w_forward(1)
-    w_over(0)
-    w_over(3)
-    for p in range(3):
-        cot_own(p)
-    w_forward(2)
-    w_over(1)
-    w_finish(0)
-    w_finish(3)
+            start(w_half(src, j, y), w_half(dst, j, y), sw_s.at[j], sw_r.at[j], cross)
+
+    def swap_forward(j):
+        part = w_half(swap_refs(j)[1], j, y)
+        arrived(part, sw_r.at[j])
+
+        @pl.when(jnp.logical_not(own))
+        def _():
+            start(part, part, sy_s.at[j], sy_r.at[j], y_peer)
+
+    def swap_ready(j):
+        arrived(w_half(swap_refs(j)[1], j, 1 - y), sy_r.at[j])
 
     def reduce_weights(b):
         return gw[:, :, 32 * b : 32 * b + 16, :].reshape(256, 1024)
@@ -612,32 +603,6 @@
     def tap_rows(b, lanes):
         return [tw[b, k : k + 1, lanes] for k in range(9)]
 
-    gain_a = small_weights(0)
-    side = side_in[0].astype(f32)
-    def cell_mask():
-        index = lax.broadcasted_iota(jnp.int32, (CELLS, 128), 0).astype(f32)
-        row = jnp.floor((index + 0.5) * (1.0 / GRID))
-        col = index - row * GRID
-        return jnp.where((row < side - 0.5) & (col < side - 0.5), 1.0, 0.0).astype(f32)
-
-    load_patches.wait()
-    red_a[...] = dot(xp[...], reduce_weights(0), 1, 1)
-
-    def conv_half_a(h, carry):
-        lanes = lanes_of(h)
-        reduced = red_a[:, lanes]
-        activated = reduced * jax.nn.sigmoid(reduced) * cell_mask()
-        spatial = conv_forward(activated, tap_rows(0, lanes), GRID, edge_masks(GRID, 128))
-        spa_a[:, lanes] = spatial
-        nar_a[:, lanes] = (spatial * jax.nn.sigmoid(spatial)).astype(bf16)
-        return carry
-
-    lax.fori_loop(0, 2, conv_half_a, 0)
-    w_over(2)
-    swap_weights()
-    w_finish(1)
-    dy[...] = dot(nar_a[...], expand_weights(0), 1, 0)
-
     def normalise(wide_ref, ref, inv_ref, rows):
         widened = wide_ref[rows, :]
         centred = widened - jnp.mean(widened, axis=1, keepdims=True)
@@ -647,76 +612,106 @@
         inv_ref[rows, :] = jnp.broadcast_to(inv, (normed.shape[0], 128))
         return normed
 
-    def norm_tile(t, carry):
-        rows = pl.ds(pl.multiple_of(t * TILE, TILE), TILE)
-        normed = normalise(dy, norm_a, inv_a, rows)
-        result = xp[rows, :].astype(f32) + normed * gain_a
-        high, low = split_low(result)
-        yhi[rows, :] = high
-        ylo[rows, :] = low
-        return carry
-
-    lax.fori_loop(0, CELLS // TILE, norm_tile, 0)
-    cot_hop(0, 1)
-
-    cell = lax.broadcasted_iota(jnp.int32, (POOLED, CELLS), 1).astype(f32)
-    bin_of = lax.broadcasted_iota(jnp.int32, (POOLED, CELLS), 0).astype(f32)
-    cell_row = jnp.floor((cell + 0.5) * (1.0 / GRID))
-    cell_col = cell - cell_row * GRID
-    bin_row = jnp.floor((bin_of + 0.5) * (1.0 / POOL))
-    bin_col = bin_of - bin_row * POOL
-
-    def table(bins, at):
-        lower = jnp.floor((bins * side + 0.5) * (1.0 / POOL))
-        upper = jnp.floor(((bins + 1.0) * side + (POOL - 0.5)) * (1.0 / POOL))
-        return jnp.where((at > lower - 0.5) & (at < upper - 0.5), 1.0 / (upper - lower), 0.0)
-
-    pp[...] = (table(bin_row, cell_row) * table(bin_col, cell_col)).astype(bf16)
-    pooled = dot(pp[...], yhi[...], 1, 0) + dot(pp[...], ylo[...], 1, 0)
-    poolv[...] = pooled
-
-    w_finish(2)
-
-    gain_b = small_weights(1)
-    reduced_b = dot(pooled.astype(bf16), reduce_weights(1), 1, 1)
-    red_b[...] = reduced_b
-    activated_b = reduced_b * jax.nn.sigmoid(reduced_b)
-    spatial_b = conv_forward(activated_b, tap_rows(1, pl.ds(0, 256)), POOL, edge_masks(POOL, 256))
-    spa_b[...] = spatial_b
-    nar_b[...] = (spatial_b * jax.nn.sigmoid(spatial_b)).astype(bf16)
-    norm_b[...] = dot(nar_b[...], expand_weights(1), 1, 0)
-    normed_b = normalise(norm_b, norm_b, inv_b, pl.ds(0, POOLED))
-    qs[me] = (pooled + normed_b * gain_b).astype(bf16)
-
-    for k in range(1, zn):
-        start(qs.at[me], qs.at[me], q_s.at[k - 1], q_rz.at[k], z_dev(z_at(k)))
-    start(qs.at[me], qs.at[me], q_s.at[3], q_rc.at[z], twin)
-    cot_own(3)
-    cot_hop(1, 1)
-    for k in range(1, zn):
-        z_of = z_at(-k)
-        slot = qs.at[2 * z_of + c]
-        arrived(slot, q_rz.at[k])
-        start(slot, slot, q_s.at[3 + k], q_rc.at[z_of], twin)
-    cot_hop(0, 2)
-    for z_of in range(zn):
-        arrived(qs.at[2 * z_of + 1 - c], q_rc.at[z_of])
-    arrived(wi, sw_r.at[0])
-
-    dpre[...] = dot(slot_rows(qs), wi[...], 1, 0)
-
-    def gelu_tile(t, carry):
-        rows = pl.ds(pl.multiple_of(t * POOLED, POOLED), POOLED)
-        hidden = dpre[rows, :]
-        phi = 0.5 * (1.0 + lax.erf(hidden * root_half))
-        actv[rows, :] = (hidden * phi).astype(bf16)
-        slope[rows, :] = (
-            phi + hidden * jnp.exp(-0.5 * hidden * hidden) * inv_root_tau
-        ).astype(bf16)
-        return carry
-
-    lax.fori_loop(0, 8, gelu_tile, 0)
-    dpre[...] = jnp.zeros_like(dpre)
+    side = side_in[0].astype(f32)
+
+    def cell_mask():
+        index = lax.broadcasted_iota(jnp.int32, (CELLS, 128), 0).astype(f32)
+        row = jnp.floor((index + 0.5) * (1.0 / GRID))
+        col = index - row * GRID
+        return jnp.where((row < side - 0.5) & (col < side - 0.5), 1.0, 0.0).astype(f32)
+
+
+    def first_conv():
+        small_weights(0)
+        load_patches.wait()
+        red_a[...] = dot(xp[...], reduce_weights(0), 1, 1)
+
+        def conv_half_a(h, carry):
+            lanes = lanes_of(h)
+            reduced = red_a[:, lanes]
+            activated = reduced * jax.nn.sigmoid(reduced) * cell_mask()
+            spatial = conv_forward(activated, tap_rows(0, lanes), GRID, edge_masks(GRID, 128))
+            spa_a[:, lanes] = spatial
+            nar_a[:, lanes] = (spatial * jax.nn.sigmoid(spatial)).astype(bf16)
+            return carry
+
+        lax.fori_loop(0, 2, conv_half_a, 0)
+
+    def first_norm():
+        dy[...] = dot(nar_a[...], expand_weights(0), 1, 0)
+        gain_a = tw[0, 9:10, :]
+
+        def norm_tile(t, carry):
+            rows = pl.ds(pl.multiple_of(t * TILE, TILE), TILE)
+            normed = normalise(dy, norm_a, inv_a, rows)
+            result = xp[rows, :].astype(f32) + normed * gain_a
+            high, low = split_low(result)
+            yhi[rows, :] = high
+            ylo[rows, :] = low
+            return carry
+
+        lax.fori_loop(0, CELLS // TILE, norm_tile, 0)
+
+    def first_pool():
+        cell = lax.broadcasted_iota(jnp.int32, (POOLED, CELLS), 1).astype(f32)
+        bin_of = lax.broadcasted_iota(jnp.int32, (POOLED, CELLS), 0).astype(f32)
+        cell_row = jnp.floor((cell + 0.5) * (1.0 / GRID))
+        cell_col = cell - cell_row * GRID
+        bin_row = jnp.floor((bin_of + 0.5) * (1.0 / POOL))
+        bin_col = bin_of - bin_row * POOL
+
+        def table(bins, at):
+            lower = jnp.floor((bins * side + 0.5) * (1.0 / POOL))
+            upper = jnp.floor(((bins + 1.0) * side + (POOL - 0.5)) * (1.0 / POOL))
+            return jnp.where((at > lower - 0.5) & (at < upper - 0.5), 1.0 / (upper - lower), 0.0)
+
+        pp[...] = (table(bin_row, cell_row) * table(bin_col, cell_col)).astype(bf16)
+        poolv[...] = dot(pp[...], yhi[...], 1, 0) + dot(pp[...], ylo[...], 1, 0)
+
+    def second_forward():
+        gain_b = small_weights(1)
+        pooled = poolv[...]
+        reduced_b = dot(pooled.astype(bf16), reduce_weights(1), 1, 1)
+        red_b[...] = reduced_b
+        activated_b = reduced_b * jax.nn.sigmoid(reduced_b)
+        spatial_b = conv_forward(activated_b, tap_rows(1, pl.ds(0, 256)), POOL, edge_masks(POOL, 256))
+        spa_b[...] = spatial_b
+        nar_b[...] = (spatial_b * jax.nn.sigmoid(spatial_b)).astype(bf16)
+        norm_b[...] = dot(nar_b[...], expand_weights(1), 1, 0)
+        normed_b = normalise(norm_b, norm_b, inv_b, pl.ds(0, POOLED))
+        qs[me] = (pooled + normed_b * gain_b).astype(bf16)
+
+    def query_to(k, to):
+        start(qs.at[me], qs.at[me], q_s.at[k], q_r.at[k], to)
+
+    def query_twin():
+        start(qs.at[me], qs.at[me], q_s.at[3], q_rc.at[slot_own], twin)
+
+    def query_from(k):
+        slot = (slot_x, slot_z, slot_corner)[k]
+        part = qs.at[2 * slot + c]
+        arrived(part, q_r.at[k])
+        start(part, part, q_cs.at[k], q_rc.at[slot], twin)
+
+    def query_all():
+        for slot in (slot_own, slot_x, slot_z, slot_corner):
+            arrived(qs.at[2 * slot + 1 - c], q_rc.at[slot])
+
+    def hidden_units():
+        dpre[...] = dot(slot_rows(qs), wi[...], 1, 0)
+
+        def gelu_tile(t, carry):
+            rows = pl.ds(pl.multiple_of(t * POOLED, POOLED), POOLED)
+            hidden = dpre[rows, :]
+            phi = 0.5 * (1.0 + lax.erf(hidden * root_half))
+            actv[rows, :] = (hidden * phi).astype(bf16)
+            slope[rows, :] = (
+                phi + hidden * jnp.exp(-0.5 * hidden * hidden) * inv_root_tau
+            ).astype(bf16)
+            return carry
+
+        lax.fori_loop(0, 8, gelu_tile, 0)
+        dpre[...] = jnp.zeros_like(dpre)
 
     def item_part(i):
         b = lax.rem(i, 2)
@@ -728,7 +723,7 @@
 
         weights = wo[:, pl.ds(pl.multiple_of(i * chunk, chunk), chunk)]
         partial = dot(actv[...], weights, 1, 0).astype(bf16)
-        partial = partial.reshape(zn, 2, POOLED, chunk)
+        partial = partial.reshape(4, 2, POOLED, chunk)
 
         @pl.when(c == 0)
         def _():
@@ -741,12 +736,6 @@
             tp[b] = partial[:, 0]
 
         start(tp.at[b], cr.at[b], t_cs.at[b], t_cr.at[b], twin)
-
-    def send_right(i, d):
-        start(ps.at[i, d], rl.at[i, d + 1], t_s.at[i, d], t_r.at[i, d + 1], z_dev(z + 1))
-
-    def send_left(i, d):
-        start(ps.at[i, d], rl.at[i, d], t_s.at[i, d], t_r.at[i, d], z_dev(z - 1))
 
     def item_pair(i):
         b = lax.rem(i, 2)
@@ -756,42 +745,19 @@
             ps[i, d] = (ps[i, d].astype(f32) + cr[b, d].astype(f32)).astype(bf16)
             return carry
 
-        lax.fori_loop(0, zn, add, 0)
+        lax.fori_loop(0, 4, add, 0)
 
         @pl.when(i < CHUNKS - 2)
         def _():
             pl.semaphore_signal(credit, inc=1, device_id=twin, device_id_type=MESH)
 
-        @pl.when(z == 0)
-        def _():
-            for d in range(zn - 1, 0, -1):
-                send_right(i, d)
-
-        @pl.when(z == zn - 1)
-        def _():
-            for d in range(zn - 1):
-                send_left(i, d)
-
-    def item_right(i):
-        def pass_on(step, carry):
-            d = zn - 1 - step
-            arrived(rl.at[i, d + 1], t_r.at[i, d + 1])
-            ps[i, d] = (ps[i, d].astype(f32) + rl[i, d + 1].astype(f32)).astype(bf16)
-            send_right(i, d)
-            return carry
-
-        lax.fori_loop(0, zn - 1 - z, pass_on, 0)
-        arrived(rl.at[i, z + 1], t_r.at[i, z + 1])
-
-    def item_left(i):
-        def pass_on(d, carry):
-            arrived(rl.at[i, d], t_r.at[i, d])
-            ps[i, d] = (ps[i, d].astype(f32) + rl[i, d].astype(f32)).astype(bf16)
-            send_left(i, d)
-            return carry
-
-        lax.fori_loop(0, z, pass_on, 0)
-        arrived(rl.at[i, z], t_r.at[i, z])
+        start(ps.at[i, slot_corner], rl.at[i, 0], t_s.at[i, 0], t_r.at[i, 0], x_peer)
+        start(ps.at[i, slot_x], rl.at[i, 1], t_s.at[i, 1], t_r.at[i, 1], x_peer)
+
+    def item_pass(i):
+        arrived(rl.at[i, 0], t_r.at[i, 0])
+        ps[i, slot_z] = (ps[i, slot_z].astype(f32) + rl[i, 0].astype(f32)).astype(bf16)
+        start(ps.at[i, slot_z], rl.at[i, 2], t_s.at[i, 2], t_r.at[i, 2], z_peer)
 
     def tok_slice(i):
         return tok_out.at[:, pl.ds(pl.multiple_of(i * chunk, chunk), chunk)]
@@ -803,177 +769,158 @@
         def _():
             left_here(tstage.at[b], gl.at[8 + b])
 
-        tstage[b] = ps[i, z]
-
-        @pl.when(z > 0)
-        def _():
-            tstage[b] = (tstage[b].astype(f32) + rl[i, z + 1].astype(f32)).astype(bf16)
-
-        @pl.when(z < zn - 1)
-        def _():
-            tstage[b] = (tstage[b].astype(f32) + rl[i, z].astype(f32)).astype(bf16)
-
+        arrived(rl.at[i, 1], t_r.at[i, 1])
+        arrived(rl.at[i, 2], t_r.at[i, 2])
+        tstage[b] = (
+            ps[i, slot_own].astype(f32) + rl[i, 1].astype(f32) + rl[i, 2].astype(f32)
+        ).astype(bf16)
         pltpu.make_async_copy(tstage.at[b], tok_slice(i), gl.at[8 + b]).start()
 
-    def item_step(s):
-        @pl.when(s < CHUNKS)
-        def _():
-            item_part(s)
-
-        @pl.when((s >= 1) & (s < CHUNKS + 1))
-        def _():
-            item_pair(s - 1)
-
-        right_at = s - 1 - z
-
-        @pl.when((z > 0) & (right_at >= 0) & (right_at < CHUNKS))
-        def _():
-            item_right(right_at)
-
-        left_at = s - zn + z
-
-        @pl.when((z < zn - 1) & (left_at >= 0) & (left_at < CHUNKS))
-        def _():
-            item_left(left_at)
-
-        @pl.when((s >= zn) & (s < CHUNKS + zn))
-        def _():
-            item_final(s - zn)
-
-    def twin_rows(z_of, p):
-        arrived(cot(z_of, 1 - c, p), dt_cr.at[p, z_of])
-
-    def slot_span(z_of):
-        return pl.ds(pl.multiple_of(z_of * (2 * POOLED), 2 * POOLED), 2 * POOLED)
-
-    def load_rows(z_of, p, at):
-        @pl.when(z_of != z)
-        def _():
-            part = cot_all.at[z_of, :, :, pl.ds(p * width, width)]
-            pltpu.make_async_copy(part, dtv.at[pl.ds(at, 2)], loc.at[3]).start()
-
-        @pl.when(z_of == z)
-        def _():
-            pltpu.make_async_copy(cot(z, 1 - c, p), dtv.at[at + 1 - c], loc.at[3]).start()
-            pltpu.make_async_copy(cot_mine(p), dtv.at[at + c], loc.at[3]).start()
-
     def piece_rows(p):
-        for z_of in range(zn):
-            twin_rows(z_of, p)
-            load_rows(z_of, p, 2 * z_of)
+        for slot in range(4):
+            arrived(cot(slot, 1 - c, p), dt_cr.at[p, slot])
+
+            @pl.when(slot_own != slot)
+            def _():
+                part = cot_all.at[slot, :, :, pl.ds(p * width, width)]
+                pltpu.make_async_copy(part, dtv.at[pl.ds(2 * slot, 2)], loc.at[3]).start()
+
+        pltpu.make_async_copy(cot(slot_own, 1 - c, p), dtv.at[2 * slot_own + 1 - c], loc.at[3]).start()
+        pltpu.make_async_copy(cot_mine(p), dtv.at[2 * slot_own + c], loc.at[3]).start()
         pltpu.make_async_copy(dtv, dtv, loc.at[3]).wait()
 
-    def piece_work(p):
-        piece_rows(p)
-        grad_part(p)
-
+    def half_lanes(half):
+        return pl.ds(pl.multiple_of(half * chunk, chunk), chunk)
+
+    def piece_lanes(h):
+        return dtv[:, :, half_lanes(h)].reshape(8 * POOLED, chunk)
+
+    def hidden_part(p):
         def hidden_half(h, carry):
-            lanes = pl.ds(pl.multiple_of(h * chunk, chunk), chunk)
-            rows = dtv[:, :, lanes].reshape(8 * POOLED, chunk)
             weights = wo[:, pl.ds(pl.multiple_of(p * width + h * chunk, chunk), chunk)]
-            dpre[...] += dot(rows, weights, 1, 1)
+            dpre[...] += dot(piece_lanes(h), weights, 1, 1)
             return carry
 
         lax.fori_loop(0, 2, hidden_half, 0)
 
-    last = PIECES - 1
-
-    def source_last(z_of):
-        twin_rows(z_of, last)
-        load_rows(z_of, last, 2 * z_of)
-        pair = dtv.at[pl.ds(2 * z_of, 2)]
-        pltpu.make_async_copy(pair, pair, loc.at[3]).wait()
-        rows = slot_span(z_of)
-        left = dtv[pl.ds(2 * z_of, 2)].reshape(2 * POOLED, width)
-        total = dpre[rows, :] + dot(left, wo[:, last * width :], 1, 1)
-        d_hidden = (total * slope[rows, :].astype(f32)).astype(bf16)
-        half = lax.div(z_of, 2)
-        place = pl.ds(pl.multiple_of((z_of - 2 * half) * (2 * POOLED), 2 * POOLED), 2 * POOLED)
+    def row_part(slot):
+        rows = pl.ds(pl.multiple_of(slot * (2 * POOLED), 2 * POOLED), 2 * POOLED)
+        d_hidden = (dpre[rows, :] * slope[rows, :].astype(f32)).astype(bf16)
+        half = lax.div(slot, 2)
+        place = pl.ds(pl.multiple_of((slot - 2 * half) * (2 * POOLED), 2 * POOLED), 2 * POOLED)
         ylo[place, pl.ds(pl.multiple_of(half * 512, 512), 512)] = d_hidden
-        d_rows = dot(d_hidden, wi[...], 1, 1).astype(bf16)
-        dps[z_of] = d_rows.reshape(2, POOLED, 1024)
-        start(dps.at[z_of, 1 - c], dr.at[z_of], d_cs.at[z_of], d_cr.at[z_of], twin)
-
-    def source_pair(z_of):
-        arrived(dr.at[z_of], d_cr.at[z_of])
-        dps[z_of, c] = (dps[z_of, c].astype(f32) + dr[z_of].astype(f32)).astype(bf16)
-
-        @pl.when(z_of != z)
-        def _():
-            k = lax.rem(z_of - z + zn, zn)
-            start(dps.at[z_of, c], dz.at[k - 1], d_zs.at[k - 1], d_zr.at[k - 1], z_dev(z_of))
-
-    def around(hop, work):
-        def one_side(side, carry):
-            z_of = z + (2 * side - 1) * hop
-
-            @pl.when((z_of >= 0) & (z_of <= zn - 1))
+        dps[slot] = dot(d_hidden, wi[...], 1, 1).astype(bf16).reshape(2, POOLED, 1024)
+        start(dps.at[slot, 1 - c], dr.at[slot], d_cs.at[slot], d_cr.at[slot], twin)
+
+    def in_turn(k):
+        return jnp.where(k == 0, slot_corner, jnp.where(k == 1, slot_x, jnp.where(k == 2, slot_z, slot_own)))
+
+    def row_gradients():
+        def one(k, carry):
+            @pl.when(k < 4)
             def _():
-                work(z_of)
+                row_part(in_turn(k))
+
+            slot = in_turn(k - 1)
+
+            @pl.when(k >= 1)
+            def _():
+                arrived(dr.at[slot], d_cr.at[slot])
+                dps[slot, c] = (dps[slot, c].astype(f32) + dr[slot].astype(f32)).astype(bf16)
+
+            @pl.when(k == 1)
+            def _():
+                start(dps.at[slot, c], dz.at[2], d_zs.at[2], d_zr.at[2], corner)
+
+            @pl.when(k == 2)
+            def _():
+                start(dps.at[slot, c], dz.at[0], d_zs.at[0], d_zr.at[0], x_peer)
+
+            @pl.when(k == 3)
+            def _():
+                start(dps.at[slot, c], dz.at[1], d_zs.at[1], d_zr.at[1], z_peer)
 
             return carry
 
-        lax.fori_loop(0, 2, one_side, 0)
+        lax.fori_loop(0, 5, one, 0)
+
+    def grad_half(j, half):
+        if j == PIECES:
+            return gis.at[pl.ds(pl.multiple_of(512 * half, 512), 512)]
+        return gos.at[j, :, half_lanes(half)]
+
+    def out_half(j, half):
+        if j == PIECES:
+            return gin_out.at[pl.ds(pl.multiple_of(512 * half, 512), 512)]
+        return gout_out.at[:, pl.ds(pl.multiple_of(j * width + half * chunk, chunk), chunk)]
+
+    def grad_send(j, h):
+        rows = pl.ds(256 * h, 256)
+        if j == PIECES:
+            part = gis.at[pl.ds(pl.multiple_of(512 * (1 - y) + 256 * h, 256), 256)]
+        else:
+            part = gos.at[j, rows, half_lanes(1 - y)]
+        start(part, gyl.at[j, rows], gy_s.at[j, h], gy_r.at[j, h], y_peer)
 
     def grad_part(p):
-        def out_half(h, carry):
-            lanes = pl.ds(pl.multiple_of(h * chunk, chunk), chunk)
-            rows = dtv[:, :, lanes].reshape(8 * POOLED, chunk)
-            gos[p, :, lanes] = dot(actv[...], rows, 0, 0).astype(bf16)
+        def one_half(h, carry):
+            gos[p, :, half_lanes(h)] = dot(actv[...], piece_lanes(h), 0, 0).astype(bf16)
             return carry
 
-        lax.fori_loop(0, 2, out_half, 0)
+        lax.fori_loop(0, 2, one_half, 0)
+
+    def gin_part():
+        gis[...] = (
+            dot(qs[0:4].reshape(4 * POOLED, 1024), ylo[:, 0:512], 0, 0)
+            + dot(qs[4:8].reshape(4 * POOLED, 1024), ylo[:, 512:1024], 0, 0)
+        ).astype(bf16)
+
+    def grad_pair(j):
+        mine = grad_half(j, y)
+        for h in range(2):
+            arrived(gyl.at[j, pl.ds(256 * h, 256)], gy_r.at[j, h])
+        mine[...] = (mine[...].astype(f32) + gyl[j].astype(f32)).astype(bf16)
 
         @pl.when(jnp.logical_not(own))
         def _():
-            start(gos.at[p], gx_land.at[p], gx_s.at[p], gx_r.at[p], x_peer)
-
-    def gout_slice(half, p):
-        return gout_out.at[half, :, pl.ds(pl.multiple_of(p * width, width), width)]
-
-    def grad_pair(p):
+            start(mine, gfl.at[j], gx_s.at[j], gx_r.at[j], far_peer)
+
+    def grad_sum(j):
         @pl.when(own)
         def _():
-            arrived(gx_land.at[p], gx_r.at[p])
-            for h in range(2):
-                half = pl.ds(h * width // 2, width // 2)
-                load = pltpu.make_async_copy(gx_land.at[p, :, half], land, loc.at[4])
-                load.start()
-                load.wait()
-                gos[p, :, half] = (gos[p, :, half].astype(f32) + land[...].astype(f32)).astype(bf16)
-            mine = gout_slice(y, p)
-            start(gos.at[p], mine, gy_s.at[p], gy_r.at[p], y_peer)
-            start(gos.at[p], mine, gc_s.at[p, 0], gc_r.at[p, 0], twin)
-            pltpu.make_async_copy(gos.at[p], mine, gl.at[p]).start()
-
-    def grad_last(p):
-        other = gout_slice(1 - y, p)
-        mine = gout_slice(y, p)
-
+            mine = grad_half(j, y)
+            arrived(gfl.at[j], gx_r.at[j])
+            load = pltpu.make_async_copy(gfl.at[j], land, loc.at[4])
+            load.start()
+            load.wait()
+            mine[...] = (mine[...].astype(f32) + land[...].astype(f32)).astype(bf16)
+            start(mine, out_half(j, y), ga_s.at[j], ga_r.at[j], y_peer)
+            start(mine, out_half(j, y), gc_s.at[j, 0], gc_r.at[j, 0], twin)
+            pltpu.make_async_copy(mine, out_half(j, y), gl.at[j]).start()
+
+    def grad_last(j):
         @pl.when(own)
         def _():
-            arrived(other, gy_r.at[p])
-            start(other, other, gc_s.at[p, 1], gc_r.at[p, 1], twin)
-
-    def grad_done(p):
-        other = gout_slice(1 - y, p)
-        mine = gout_slice(y, p)
+            other = out_half(j, 1 - y)
+            arrived(other, ga_r.at[j])
+            start(other, other, gc_s.at[j, 1], gc_r.at[j, 1], twin)
+
+    def grad_done(j):
+        for h in range(2):
+            left_here(gyl.at[j, pl.ds(256 * h, 256)], gy_s.at[j, h])
 
         @pl.when(own)
         def _():
-            left_here(gos.at[p], gy_s.at[p])
-            left_here(gos.at[p], gc_s.at[p, 0])
-            left_here(other, gc_s.at[p, 1])
-            pltpu.make_async_copy(gos.at[p], mine, gl.at[p]).wait()
+            left_here(grad_half(j, y), ga_s.at[j])
+            left_here(grad_half(j, y), gc_s.at[j, 0])
+            left_here(grad_half(j, y), gc_s.at[j, 1])
+            pltpu.make_async_copy(grad_half(j, y), out_half(j, y), gl.at[j]).wait()
 
         @pl.when(jnp.logical_not(own))
         def _():
-            left_here(gos.at[p], gx_s.at[p])
-            arrived(mine, gc_r.at[p, 0])
-            arrived(other, gc_r.at[p, 1])
-
-    def gin_slice(half):
-        return gin_out.at[half]
+            left_here(grad_half(j, y), gx_s.at[j])
+            arrived(out_half(j, y), gc_r.at[j, 0])
+            arrived(out_half(j, 1 - y), gc_r.at[j, 1])
 
     def widened_back(d_rows, normed, gain, inv):
         dn = d_rows * gain
@@ -991,72 +938,107 @@
             sm[t, 9 + k : 10 + k, :] = d_gain[:, 256 * k : 256 * k + 256]
         sm[t, 13:16, :] = jnp.zeros((3, 256), f32)
 
-    def share_core(t):
-        start(wgs.at[t, 1 - c], wgc.at[t], gr_s.at[t, 0], gr_r.at[t, 0], twin)
-        start(sm.at[t], smc.at[t], gr_s.at[t, 1], gr_r.at[t, 1], twin)
-
-    def share_x(t):
-        arrived(wgc.at[t], gr_r.at[t, 0])
-        arrived(smc.at[t], gr_r.at[t, 1])
-        for i in range(8):
-            for h in range(2):
-                rows = pl.ds(128 * h + 16 * i, 16)
-                xs[t, i % 2, i // 2, 16 * h : 16 * h + 16] = (
-                    wgs[t, c, rows, :].astype(f32) + wgc[t, rows, :].astype(f32)
+    passes = ((1, 0, 2, 1), (0, 1, 1, None), (0, 0, 1, 0))
+
+    def share_core(p):
+        t, k0, n, small = passes[p]
+        kinds = pl.ds(k0, n)
+        start(
+            wgs.at[t, kinds, pl.ds(pl.multiple_of(128 * (1 - c), 128), 128)], wgc.at[t, kinds],
+            gr_s.at[p, 0], gr_r.at[p, 0], twin,
+        )
+        if small is not None:
+            start(sm.at[t], smc.at[t], gr_s.at[p, 1], gr_r.at[p, 1], twin)
+
+    def share_x(p):
+        t, k0, n, small = passes[p]
+        kinds = pl.ds(k0, n)
+        arrived(wgc.at[t, kinds], gr_r.at[p, 0])
+        for kind in range(k0, k0 + n):
+            for i in range(8):
+                rows = pl.ds(pl.multiple_of(128 * c + 16 * i, 16), 16)
+                xs[t, kind, i % 2, i // 2] = (
+                    wgs[t, kind, rows, :].astype(f32) + wgc[t, kind, 16 * i : 16 * i + 16, :].astype(f32)
                 ).astype(bf16)
-        left_here(sm.at[t], gr_s.at[t, 1])
-        sm[t] = sm[t] + smc[t]
-        start(xs.at[t, 1 - x], xr.at[t], gr_s.at[t, 2], gr_r.at[t, 2], x_peer)
-        start(sm.at[t], smx.at[t], gr_s.at[t, 3], gr_r.at[t, 3], x_peer)
-
-    def share_z(t):
-        arrived(xr.at[t], gr_r.at[t, 2])
-        arrived(smx.at[t], gr_r.at[t, 3])
-        zs[t] = (xs[t, x].astype(f32) + xr[t].astype(f32)).astype(bf16)
-        left_here(sm.at[t], gr_s.at[t, 3])
-        smz[t, z] = sm[t] + smx[t]
+        start(xs.at[t, kinds, 1 - x], xr.at[t, kinds], gr_s.at[p, 2], gr_r.at[p, 2], x_peer)
+        if small is not None:
+            arrived(smc.at[t], gr_r.at[p, 1])
+            left_here(sm.at[t], gr_s.at[p, 1])
+            sm[t] = sm[t] + smc[t]
+            start(sm.at[t], smx.at[t], gr_s.at[p, 3], gr_r.at[p, 3], x_peer)
+
+    def share_z(p):
+        t, k0, n, small = passes[p]
+        kinds = pl.ds(k0, n)
+        arrived(xr.at[t, kinds], gr_r.at[p, 2])
+        for kind in range(k0, k0 + n):
+            zs[t, kind] = (xs[t, kind, x].astype(f32) + xr[t, kind].astype(f32)).astype(bf16)
         for k in range(1, zn):
             d = z_at(k)
-            start(zs.at[t, d], zr.at[t, k - 1], gr_s.at[t, 3 + k], gr_r.at[t, 3 + k], z_dev(d))
             start(
-                smz.at[t, z], smz.at[t, z], gr_s.at[t, 6 + k], gr_r.at[t, 6 + k], z_dev(d)
+                zs.at[t, kinds, d], zr.at[t, kinds, k - 1], gr_s.at[p, 3 + k], gr_r.at[p, 3 + k], z_dev(d)
             )
-
-    def share_y(t):
-        total_rows = zs[t, z].astype(f32)
+        if small is not None:
+            arrived(smx.at[t], gr_r.at[p, 3])
+            left_here(sm.at[t], gr_s.at[p, 3])
+            smz[t, z] = sm[t] + smx[t]
+            for k in range(1, zn):
+                start(
+                    smz.at[t, z], smz.at[t, z], gr_s.at[p, 6 + k], gr_r.at[p, 6 + k], z_dev(z_at(k))
+                )
+
+    def share_y(p):
+        t, k0, n, small = passes[p]
+        kinds = pl.ds(k0, n)
         for k in range(1, zn):
-            arrived(zr.at[t, k - 1], gr_r.at[t, 3 + k])
-            total_rows = total_rows + zr[t, k - 1].astype(f32)
-            arrived(smz.at[t, z_at(-k)], gr_r.at[t, 6 + k])
-        ys[t] = total_rows.astype(bf16)
-        sm[t] = (smz[t, 0] + smz[t, 1]) + (smz[t, 2] + smz[t, 3])
-        start(ys.at[t], yr.at[t], gr_s.at[t, 10], gr_r.at[t, 10], y_peer)
-        start(sm.at[t], smy.at[t], gr_s.at[t, 11], gr_r.at[t, 11], y_peer)
-
-    def share_twin(t):
-        arrived(yr.at[t], gr_r.at[t, 10])
-        arrived(smy.at[t], gr_r.at[t, 11])
-        gfin[t, c] = ys[t].astype(f32) + yr[t].astype(f32)
-        gsml_out[t] = sm[t] + smy[t]
-        start(gfin.at[t, c], gfin.at[t, c], gr_s.at[t, 12], gr_r.at[t, 12], twin)
-
-    def share_done(t):
-        arrived(gfin.at[t, 1 - c], gr_r.at[t, 12])
-        gblk_out[t] = gfin[t]
-        left_here(wgs.at[t, 1 - c], gr_s.at[t, 0])
-        left_here(xs.at[t, 1 - x], gr_s.at[t, 2])
+            arrived(zr.at[t, kinds, k - 1], gr_r.at[p, 3 + k])
+        for kind in range(k0, k0 + n):
+            total_rows = zs[t, kind, z].astype(f32)
+            for k in range(1, zn):
+                total_rows = total_rows + zr[t, kind, k - 1].astype(f32)
+            ys[t, kind] = total_rows.astype(bf16)
+        start(ys.at[t, kinds], yr.at[t, kinds], gr_s.at[p, 10], gr_r.at[p, 10], y_peer)
+        if small is not None:
+            for k in range(1, zn):
+                arrived(smz.at[t, z_at(-k)], gr_r.at[p, 6 + k])
+            sm[t] = (smz[t, 0] + smz[t, 1]) + (smz[t, 2] + smz[t, 3])
+            start(sm.at[t], smy.at[t], gr_s.at[p, 11], gr_r.at[p, 11], y_peer)
+
+    def share_twin(p):
+        t, k0, n, small = passes[p]
+        kinds = pl.ds(k0, n)
+        arrived(yr.at[t, kinds], gr_r.at[p, 10])
+        for kind in range(k0, k0 + n):
+            gfin[c, t, kind] = ys[t, kind].astype(f32) + yr[t, kind].astype(f32)
+        part = gfin.at[c, t, kinds]
+        start(part, part, gr_s.at[p, 12], gr_r.at[p, 12], twin)
+        if small is not None:
+            arrived(smy.at[t], gr_r.at[p, 11])
+            gsml_out[t] = sm[t] + smy[t]
+
+    def share_done(p):
+        t, k0, n, small = passes[p]
+        kinds = pl.ds(k0, n)
+        arrived(gfin.at[1 - c, t, kinds], gr_r.at[p, 12])
+        for kind in range(k0, k0 + n):
+            for h in range(2):
+                gblk_out[t, kind, 16 * h : 16 * h + 16, :] = gfin[h, t, kind]
+        left_here(wgc.at[t, kinds], gr_s.at[p, 0])
+        left_here(xr.at[t, kinds], gr_s.at[p, 2])
         for k in range(1, zn):
-            left_here(zs.at[t, 0], gr_s.at[t, 3 + k])
-            left_here(smz.at[t, z], gr_s.at[t, 6 + k])
-        left_here(ys.at[t], gr_s.at[t, 10])
-        left_here(sm.at[t], gr_s.at[t, 11])
-        left_here(gfin.at[t, c], gr_s.at[t, 12])
+            left_here(ys.at[t, kinds], gr_s.at[p, 3 + k])
+        left_here(ys.at[t, kinds], gr_s.at[p, 10])
+        left_here(gfin.at[c, t, kinds], gr_s.at[p, 12])
+        if small is not None:
+            for k in range(1, zn):
+                left_here(sm.at[t], gr_s.at[p, 6 + k])
+            left_here(sm.at[t], gr_s.at[p, 11])
 
     def back_second():
-        total = dps[z, c].astype(f32)
-        for k in range(1, zn):
-            arrived(dz.at[k - 1], d_zr.at[k - 1])
-            total = total + dz[k - 1].astype(f32)
+        total = dps[slot_own, c].astype(f32)
+        for k in range(3):
+            arrived(dz.at[k], d_zr.at[k])
+            total = total + dz[k].astype(f32)
         normed_b = norm_b[...]
         d_gain_b = jnp.sum(total * normed_b, axis=0, keepdims=True)
         gain_b = tw[1, 9:10, :]
@@ -1117,168 +1099,237 @@
         dy[...] += dot(dlow[...], reduce_weights(0), 1, 0)
         store_dpat.start()
 
-    def gin_part():
-        gis[...] = (
-            dot(qs[0:4].reshape(4 * POOLED, 1024), ylo[:, 0:512], 0, 0)
-            + dot(qs[4:8].reshape(4 * POOLED, 1024), ylo[:, 512:1024], 0, 0)
-        ).astype(bf16)
-
-        @pl.when(jnp.logical_not(own))
-        def _():
-            start(gis, gi_land, gx_s.at[PIECES], gx_r.at[PIECES], x_peer)
-
-    def gin_pair():
-        @pl.when(own)
-        def _():
-            arrived(gi_land, gx_r.at[PIECES])
-            for h in range(2):
-                rows = pl.ds(512 * h, 512)
-                load = pltpu.make_async_copy(gi_land.at[rows], land, loc.at[4])
-                load.start()
-                load.wait()
-                gis[rows, :] = (gis[rows, :].astype(f32) + land[...].astype(f32)).astype(bf16)
-            start(gis, gin_slice(y), gy_s.at[PIECES], gy_r.at[PIECES], y_peer)
-            start(gis, gin_slice(y), gc_s.at[PIECES, 0], gc_r.at[PIECES, 0], twin)
-            pltpu.make_async_copy(gis, gin_slice(y), gl.at[PIECES]).start()
-
-    def gin_last():
-        @pl.when(own)
-        def _():
-            arrived(gin_slice(1 - y), gy_r.at[PIECES])
-            start(gin_slice(1 - y), gin_slice(1 - y), gc_s.at[PIECES, 1], gc_r.at[PIECES, 1], twin)
+    w_own(0)
+    w_own(1)
+    cot_own_x(3)
+    w_own(3)
+    w_forward(0)
+    w_own(2)
+    w_forward(1)
+    w_forward(3)
+    w_over(0)
+    cot_own_z(0)
+    cot_own_z(1)
+    w_over(1)
+    cot_own_x(0)
+    w_over(3)
+    w_finish(3)
+    swap_send(0)
+    cot_own_twin(2)
+    cot_over_x(3)
+    w_finish(0)
+    cot_own_twin(0)
+    w_forward(2)
+    first_conv()
+    w_finish(1)
+    first_norm()
+    swap_send(1)
+    w_over(2)
+    cot_over_z(0)
+    w_finish(2)
+    first_pool()
+    second_forward()
+    query_to(1, z_peer)
+    query_to(0, x_peer)
+    query_to(2, corner)
+    swap_forward(0)
+    cot_own_x(2)
+    query_twin()
+    swap_send(2)
+    cot_own_twin(1)
+    query_from(0)
+    cot_corner(0)
+    cot_over_x(0)
+    cot_own_z(2)
+    piece_rows(0)
+    query_from(1)
+    swap_forward(1)
+    swap_send(3)
+    query_from(2)
+    swap_ready(0)
+    cot_own_x(1)
+    query_all()
+    swap_ready(1)
+    cot_own_z(3)
+    swap_forward(2)
+    hidden_units()
+
+    part_at = (0, 2, 3, 6, 8, 9, 13, 20)
+    pair_at = (1, 4, 6, 7, 11, 15, 16, 21)
+    pass_at = (5, 9, 10, 14, 16, 17, 19, 23)
+    final_at = (12, 14, 17, 18, 20, 22, 24, 25)
+
+    def item_of(s, places):
+        number = jnp.int32(-1)
+        for item, place in enumerate(places):
+            number = jnp.where(s == place, item, number)
+        return number
 
     def main_step(s, carry):
         def at(step):
             return pl.when(s == step)
 
-        @pl.when(s < CHUNKS // 2)
-        def _():
-            for half in range(2):
-                j = 2 * s + half
-                arrived(wo.at[:, pl.ds(pl.multiple_of(j * chunk, chunk), chunk)], sw_r.at[1 + j])
-
-        @at(0)
-        def _():
-            cot_hop(2, 1)
-            cot_hop(1, 2)
-            cot_hop(0, 3)
-
         @at(1)
         def _():
-            cot_hop(3, 1)
-            cot_hop(2, 2)
-            piece_work(0)
+            cot_own_twin(3)
+            grad_part(0)
+            cot_over_z(1)
+            hidden_part(0)
+            cot_over_x(2)
+            swap_ready(2)
+            grad_send(0, 1)
+            cot_over_z(2)
+            cot_over_x(1)
 
         @at(2)
         def _():
-            cot_hop(1, 3)
+            grad_send(0, 0)
+            swap_send(4)
+            cot_corner(1)
 
         @at(3)
         def _():
-            cot_hop(3, 2)
-            piece_work(1)
+            swap_forward(3)
+
+        @at(4)
+        def _():
+            piece_rows(1)
+            hidden_part(1)
             grad_pair(0)
-
-        @at(4)
-        def _():
-            cot_hop(2, 3)
+            cot_over_z(3)
+            grad_part(1)
+            cot_corner(2)
+            swap_forward(4)
+            grad_send(1, 1)
+            piece_rows(2)
+            grad_send(1, 0)
 
         @at(5)
         def _():
-            piece_work(2)
+            swap_ready(3)
+            hidden_part(2)
+            grad_part(2)
+            grad_send(2, 0)
+            cot_corner(3)
+
+        @at(6)
+        def _():
+            piece_rows(3)
+            swap_ready(4)
+            hidden_part(3)
+            row_gradients()
+
+        @at(8)
+        def _():
+            grad_send(2, 1)
             grad_pair(1)
+
+        @at(9)
+        def _():
+            gin_part()
+            grad_sum(0)
+            grad_pair(2)
+            grad_part(3)
+            grad_send(3, 1)
+            grad_send(3, 0)
+            back_second()
+
+        @at(12)
+        def _():
+            grad_send(PIECES, 1)
+            grad_send(PIECES, 0)
+            back_first_norm()
+
+        @at(13)
+        def _():
+            share_core(1)
+
+        @at(14)
+        def _():
+            share_core(0)
+
+        @at(15)
+        def _():
+            grad_pair(3)
+
+        @at(16)
+        def _():
+            grad_sum(2)
+
+        @at(17)
+        def _():
+            share_x(0)
+            share_x(1)
+            grad_sum(1)
+            grad_pair(PIECES)
+            grad_sum(3)
+
+        @at(18)
+        def _():
+            back_first_conv()
+
+        @at(19)
+        def _():
             grad_last(0)
-            source_last(z)
-            around(1, source_last)
-
-        @at(6)
-        def _():
-            cot_hop(3, 3)
-            source_pair(z)
-            around(1, source_pair)
-            around(2, source_last)
-
-        @at(7)
-        def _():
-            around(3, source_last)
-            around(2, source_pair)
-            grad_part(3)
-            around(3, source_pair)
-            grad_pair(2)
+
+        @at(20)
+        def _():
+            share_z(0)
+            share_core(2)
+
+        @at(21)
+        def _():
+            share_z(1)
+            share_x(2)
+            grad_last(2)
+
+        @at(22)
+        def _():
+            grad_sum(PIECES)
             grad_last(1)
 
-        @at(8)
-        def _():
-            gin_part()
-
-        @at(9)
-        def _():
-            back_second()
-            share_core(1)
-
-        @at(10)
-        def _():
-            back_first_norm()
-            share_x(1)
-            grad_pair(3)
-            grad_last(2)
-
-        @at(11)
-        def _():
-            back_first_conv()
-            share_core(0)
-            share_z(1)
+        @at(23)
+        def _():
+            share_z(2)
             back_first_rows()
 
-        @at(12)
-        def _():
-            share_x(0)
+        @at(24)
+        def _():
+            share_y(0)
             share_y(1)
-            gin_pair()
-
-        @at(13)
-        def _():
-            share_z(0)
+            grad_last(PIECES)
+            grad_last(3)
+
+        @at(25)
+        def _():
+            share_y(2)
+            share_twin(0)
             share_twin(1)
-            grad_last(3)
-
-        @at(14)
-        def _():
-            share_y(0)
-
-        @at(15)
-        def _():
-            share_twin(0)
-            gin_last()
-
-        @pl.when((s >= CHUNKS) | (lax.rem(s, 2) == 0))
-        def _():
-            item_step(jnp.where(s < CHUNKS, lax.div(s, 2), s - CHUNKS // 2))
+            share_twin(2)
+
+        for places, work in (
+            (part_at, item_part), (pair_at, item_pair), (pass_at, item_pass), (final_at, item_final)
+        ):
+            number = item_of(s, places)
+
+            @pl.when(number >= 0)
+            def _(number=number, work=work):
+                work(number)
 
         return carry
 
-    lax.fori_loop(0, 2 * CHUNKS, main_step, 0)
-
-    share_done(1)
-    share_done(0)
-    for p in range(PIECES):
-        grad_done(p)
-
-    @pl.when(own)
-    def _():
-        left_here(gis, gy_s.at[PIECES])
-        left_here(gis, gc_s.at[PIECES, 0])
-        left_here(gin_slice(1 - y), gc_s.at[PIECES, 1])
-        pltpu.make_async_copy(gis, gin_slice(y), gl.at[PIECES]).wait()
-
-    @pl.when(jnp.logical_not(own))
-    def _():
-        left_here(gis, gx_s.at[PIECES])
-        arrived(gin_slice(y), gc_r.at[PIECES, 0])
-        arrived(gin_slice(1 - y), gc_r.at[PIECES, 1])
-        left_here(wi, sw_s.at[0])
-        for j in range(CHUNKS):
-            left_here(columns(wo, j, chunk), sw_s.at[1 + j])
+    lax.fori_loop(0, 26, main_step, 0)
+
+    for p in range(3):
+        share_done(p)
+    for j in range(1 + PIECES):
+        grad_done(j)
+
+        @pl.when(jnp.logical_not(own))
+        def _():
+            part = w_half(swap_refs(j)[1], j, y)
+            left_here(part, sw_s.at[j])
+            left_here(part, sy_s.at[j])
 
     store_dpat.wait()
     for b in range(2):
@@ -1287,29 +1338,23 @@
     for b in range(4):
         for k in range(15):
             left_here(w_part(b, c, 0), w_s.at[b, k])
-    for k in range(7):
+    for k in range(4):
         left_here(qs.at[0], q_s.at[k])
-    for k in range(zn):
+    for k in range(3):
+        left_here(qs.at[0], q_cs.at[k])
+    for k in range(4):
         left_here(dps.at[0, 0], d_cs.at[k])
-    for k in range(zn - 1):
+    for k in range(3):
         left_here(dps.at[0, 0], d_zs.at[k])
     for p in range(PIECES):
-        for z_of in range(zn):
-            left_here(cot(0, 0, p), dt_cs.at[p, z_of])
-        for hop in range(zn - 1):
-            @pl.when((z < zn - 1) & (z >= hop))
-            def _():
-                left_here(cot(0, 0, p), dt_s.at[p, 0, hop])
-
-            @pl.when((z > 0) & (z + hop <= zn - 1))
-            def _():
-                left_here(cot(0, 0, p), dt_s.at[p, 1, hop])
+        for slot in range(4):
+            left_here(cot(0, 0, p), dt_cs.at[p, slot])
+        for k in range(3):
+            left_here(cot(0, 0, p), dt_s.at[p, k])
 
     def drain_items(i, carry):
-        for d in range(zn):
-            @pl.when(z != d)
-            def _():
-                left_here(ps.at[0, 0], t_s.at[i, d])
+        for k in range(3):
+            left_here(ps.at[0, 0], t_s.at[i, k])
         return carry
 
     lax.fori_loop(0, CHUNKS, drain_items, 0)
@@ -1327,13 +1372,12 @@
     out_shape = (
         shape((POOLED, 4096), bf16),
         shape((CELLS, 1024), f32),
-        shape((2, 512, 4096), bf16),
-        shape((2, 1024, 512), bf16),
+        shape((512, 4096), bf16),
+        shape((1024, 512), bf16),
         shape((2, 2, 32, 1024), f32),
         shape((2, 16, 256), f32),
         shape((4, 2, POOLED, 4096), bf16),
-        shape((PIECES, 512, width), bf16),
-        shape((1024, 512), bf16),
+        shape((1 + PIECES, 512, width // 2), bf16),
     )
     dma = pltpu.SemaphoreType.DMA
     scratch = [
@@ -1367,66 +1411,72 @@
         pltpu.VMEM((2, 4, POOLED, chunk), bf16),
         pltpu.VMEM((2, 4, POOLED, chunk), bf16),
         pltpu.VMEM((CHUNKS, 4, POOLED, chunk), bf16),
-        pltpu.VMEM((CHUNKS, 5, POOLED, chunk), bf16),
+        pltpu.VMEM((CHUNKS, 3, POOLED, chunk), bf16),
         pltpu.VMEM((2, POOLED, chunk), bf16),
         pltpu.VMEM((4, 2, POOLED, 1024), bf16),
         pltpu.VMEM((4, POOLED, 1024), bf16),
         pltpu.VMEM((3, POOLED, 1024), bf16),
         pltpu.VMEM((PIECES, 512, width), bf16),
         pltpu.VMEM((1024, 512), bf16),
+        pltpu.VMEM((1 + PIECES, 512, width // 2), bf16),
         pltpu.VMEM((512, width // 2), bf16),
         pltpu.VMEM((2, 2, 256, 1024), bf16),
-        pltpu.VMEM((2, 256, 1024), bf16),
-        pltpu.VMEM((2, 2, 4, 32, 1024), bf16),
-        pltpu.VMEM((2, 4, 32, 1024), bf16),
-        pltpu.VMEM((2, 4, 32, 1024), bf16),
-        pltpu.VMEM((2, 3, 32, 1024), bf16),
-        pltpu.VMEM((2, 32, 1024), bf16),
-        pltpu.VMEM((2, 32, 1024), bf16),
+        pltpu.VMEM((2, 2, 128, 1024), bf16),
+        pltpu.VMEM((2, 2, 2, 4, 16, 1024), bf16),
+        pltpu.VMEM((2, 2, 4, 16, 1024), bf16),
+        pltpu.VMEM((2, 2, 4, 16, 1024), bf16),
+        pltpu.VMEM((2, 2, 3, 16, 1024), bf16),
+        pltpu.VMEM((2, 2, 16, 1024), bf16),
+        pltpu.VMEM((2, 2, 16, 1024), bf16),
         pltpu.VMEM((2, 16, 256), f32),
         pltpu.VMEM((2, 16, 256), f32),
         pltpu.VMEM((2, 16, 256), f32),
         pltpu.VMEM((2, 4, 16, 256), f32),
         pltpu.VMEM((2, 16, 256), f32),
-        pltpu.VMEM((2, 2, 32, 1024), f32),
+        pltpu.VMEM((2, 2, 2, 16, 1024), f32),
         dma((6,)),
         dma((4, 15)),
         dma((4, 4)),
         dma((4, 4)),
         dma((4, 8)),
-        dma((1 + CHUNKS,)),
-        dma((1 + CHUNKS,)),
-        dma((7,)),
+        dma((1 + PIECES,)),
+        dma((1 + PIECES,)),
+        dma((1 + PIECES,)),
+        dma((1 + PIECES,)),
         dma((4,)),
+        dma((3,)),
+        dma((3,)),
         dma((4,)),
-        dma((PIECES, 2, 3)),
-        dma((PIECES, 2, 3)),
+        dma((PIECES, 3)),
+        dma((PIECES, 3)),
         dma((PIECES, 4)),
         dma((PIECES, 4)),
         dma((2,)),
         dma((2,)),
-        dma((CHUNKS, 4)),
-        dma((CHUNKS, 5)),
+        dma((CHUNKS, 3)),
+        dma((CHUNKS, 3)),
         pltpu.SemaphoreType.REGULAR,
         dma((4,)),
         dma((4,)),
         dma((3,)),
         dma((3,)),
-        dma((PIECES + 1,)),
-        dma((PIECES + 1,)),
-        dma((PIECES + 1,)),
-        dma((PIECES + 1,)),
-        dma((PIECES + 1, 2)),
-        dma((PIECES + 1, 2)),
+        dma((1 + PIECES, 2)),
+        dma((1 + PIECES, 2)),
+        dma((1 + PIECES,)),
+        dma((1 + PIECES,)),
+        dma((1 + PIECES,)),
+        dma((1 + PIECES,)),
+        dma((1 + PIECES, 2)),
+        dma((1 + PIECES, 2)),
         dma((10,)),
-        dma((2, 13)),
-        dma((2, 13)),
+        dma((3, 13)),
+        dma((3, 13)),
     ]
     return pl.pallas_call(
         layer_kernel,
         out_shape=out_shape,
         in_specs=[any_space, smem] + [vmem] * 8 + [any_space] * 3,
-        out_specs=(any_space, any_space, any_space, any_space, vmem, vmem, any_space, any_space, any_space),
+        out_specs=(any_space, any_space, any_space, any_space, vmem, vmem, any_space, any_space),
         scratch_shapes=scratch,
         compiler_params=pltpu.CompilerParams(
             collective_id=0, has_side_effects=True, vmem_limit_bytes=VMEM_BYTES
@@ -1448,8 +1498,8 @@
 ):
     tok[...] = tok_in[...]
     dpat[...] = dpat_in[...]
-    gout[...] = gout_in[0].astype(f32) + gout_in[1].astype(f32)
-    gin[...] = gin_in[0].astype(f32) + gin_in[1].astype(f32)
+    gout[...] = gout_in[...].astype(f32)
+    gin[...] = gin_in[...].astype(f32)
 
     @pl.when(pl.program_id(0) == 0)
     def _():
@@ -1483,15 +1533,15 @@
         out_shape=[
             shape(tokens.shape, bf16),
             shape(d_patches.shape, f32),
-            shape(gout.shape[1:], f32),
-            shape(gin.shape[1:], f32),
+            shape(gout.shape, f32),
+            shape(gin.shape, f32),
         ]
         + one_shape * 2,
         in_specs=[
             pl.BlockSpec((POOLED, columns), lambda i: (0, i)),
             pl.BlockSpec((CELLS // FINISH, 1024), lambda i: (i, 0)),
-            pl.BlockSpec((2, 512 // FINISH, 4096), lambda i: (0, i, 0)),
-            pl.BlockSpec((2, 1024 // FINISH, 512), lambda i: (0, i, 0)),
+            pl.BlockSpec((512 // FINISH, 4096), lambda i: (i, 0)),
+            pl.BlockSpec((1024 // FINISH, 512), lambda i: (i, 0)),
             whole(2, 2, 32, 1024),
             whole(2, 16, 256),
         ],

time: 244 us -> 209 us (0.86)
  Pallas kernels: 242 us -> 207 us
    pallas_call x1, Pallas kernels: 229 us -> 196 us  [layer_call(): pl.pallas_call(layer_kernel, out_shape=out_shape, in_specs=[any_space, sm...]
where the time goes in v3:
time: 209 us; the launch traced here: 208 us
  Pallas kernels  207 us (99%)
    pallas_call x1, Pallas kernels, layer_call(): pl.pallas_call(layer_kernel, out_shape=out_shape, in_specs=[any_space, sm...  196 us
    pallas_call x1, Pallas kernels, finish_call(): pl.pallas_call(finish_kernel, grid=(FINISH,), out_shape=[shape(tokens.sha...  10.8 us

profile of v3, /device:TPU:0, one launch (start us, length us, event | category | flops | bytes accessed | tf_op | source)
XLA Modules:
  0.0 208.2 jit_solution(2288704398169684186)
XLA Ops:
  1.3 196.0 %shard_map.220 = (bf16[144,4096]{1,0:T(8,128)(2,1)}, f32[576,1024]{1,0:T(8,128)}, bf16[512,4096]{1,0:T(8,128)(2,1)}, bf16[1024,512]{1,0:T(8,128)(2,1)}, f32[2,2,...) custom-call(bf16[576,1024]{1,0:T(8,128)(2,1)} %patches_in.1, ...), custom_call_target="tpu_custom_call" | custom-call | tf_op jit(solution)/shard_map/pallas_call | solution.py:1475
  197.3 10.8 %shard_map.221 = (bf16[144,4096]{1,0:T(8,128)(2,1)}, f32[576,1024]{1,0:T(8,128)}, f32[512,4096]{1,0:T(8,128)}, f32[1024,512]{1,0:T(8,128)}, f32[32,1024]{1,0:T(8...) custom-call(bf16[144,4096]{1,0:T(8,128)(2,1)} %get-tuple-element.30., ...), custom_call_target="tpu_custom_call" | custom-call | tf_op jit(solution)/shard_map/pallas_call | solution.py:1530

commit v4 on v3

--- a/solution.py
+++ b/solution.py
@@ -714,14 +714,14 @@
         dpre[...] = jnp.zeros_like(dpre)
 
     def item_part(i):
-        b = lax.rem(i, 2)
-
-        @pl.when(i >= 2)
-        def _():
+        b = i % 2
+
+        if i >= 2:
             left_here(tp.at[b], t_cs.at[b])
             pl.semaphore_wait(credit, 1)
 
-        weights = wo[:, pl.ds(pl.multiple_of(i * chunk, chunk), chunk)]
+
+        weights = wo[:, i * chunk : (i + 1) * chunk]
         partial = dot(actv[...], weights, 1, 0).astype(bf16)
         partial = partial.reshape(4, 2, POOLED, chunk)
 
@@ -738,7 +738,7 @@
         start(tp.at[b], cr.at[b], t_cs.at[b], t_cr.at[b], twin)
 
     def item_pair(i):
-        b = lax.rem(i, 2)
+        b = i % 2
         arrived(cr.at[b], t_cr.at[b])
 
         def add(d, carry):
@@ -747,8 +747,7 @@
 
         lax.fori_loop(0, 4, add, 0)
 
-        @pl.when(i < CHUNKS - 2)
-        def _():
+        if i < CHUNKS - 2:
             pl.semaphore_signal(credit, inc=1, device_id=twin, device_id_type=MESH)
 
         start(ps.at[i, slot_corner], rl.at[i, 0], t_s.at[i, 0], t_r.at[i, 0], x_peer)
@@ -760,13 +759,12 @@
         start(ps.at[i, slot_z], rl.at[i, 2], t_s.at[i, 2], t_r.at[i, 2], z_peer)
 
     def tok_slice(i):
-        return tok_out.at[:, pl.ds(pl.multiple_of(i * chunk, chunk), chunk)]
+        return tok_out.at[:, pl.ds(i * chunk, chunk)]
 
     def item_final(i):
-        b = lax.rem(i, 2)
-
-        @pl.when(i >= 2)
-        def _():
+        b = i % 2
+
+        if i >= 2:
             left_here(tstage.at[b], gl.at[8 + b])
 
         arrived(rl.at[i, 1], t_r.at[i, 1])
@@ -1099,226 +1097,165 @@
         dy[...] += dot(dlow[...], reduce_weights(0), 1, 0)
         store_dpat.start()
 
+    w_own(3)
+    cot_own_x(0)
     w_own(0)
+    w_own(2)
+    cot_own_z(0)
     w_own(1)
+    w_forward(3)
+    cot_own_x(2)
+    cot_own_z(1)
+    w_over(3)
+    w_forward(2)
+    cot_own_twin(1)
+    swap_send(0)
+    swap_send(1)
+    w_forward(0)
+    swap_send(2)
+    w_forward(1)
+    w_over(2)
+    w_finish(3)
+    cot_over_z(0)
     cot_own_x(3)
-    w_own(3)
-    w_forward(0)
-    w_own(2)
-    w_forward(1)
-    w_forward(3)
+    w_over(1)
+    w_finish(1)
     w_over(0)
-    cot_own_z(0)
-    cot_own_z(1)
-    w_over(1)
-    cot_own_x(0)
-    w_over(3)
-    w_finish(3)
-    swap_send(0)
+    w_finish(0)
+    cot_over_x(2)
+    w_finish(2)
+    first_conv()
+    first_norm()
+    first_pool()
     cot_own_twin(2)
+    second_forward()
+    cot_corner(0)
+    swap_forward(0)
+    query_to(0, x_peer)
+    query_twin()
+    query_to(2, corner)
+    swap_ready(0)
+    query_to(1, z_peer)
+    cot_over_x(0)
+    swap_forward(1)
+    cot_own_twin(0)
+    piece_rows(0)
+    swap_ready(1)
+    cot_own_z(2)
+    swap_send(3)
+    swap_forward(2)
+    query_from(1)
+    query_from(2)
+    query_from(0)
+    cot_over_z(1)
+    query_all()
+    hidden_units()
+
+    cot_own_x(1)
+    grad_part(0)
+    grad_send(0, 0)
+    item_part(0)
+    hidden_part(0)
+    grad_send(0, 1)
+    cot_corner(1)
     cot_over_x(3)
-    w_finish(0)
-    cot_own_twin(0)
-    w_forward(2)
-    first_conv()
-    w_finish(1)
-    first_norm()
-    swap_send(1)
-    w_over(2)
-    cot_over_z(0)
-    w_finish(2)
-    first_pool()
-    second_forward()
-    query_to(1, z_peer)
-    query_to(0, x_peer)
-    query_to(2, corner)
-    swap_forward(0)
-    cot_own_x(2)
-    query_twin()
-    swap_send(2)
-    cot_own_twin(1)
-    query_from(0)
-    cot_corner(0)
-    cot_over_x(0)
-    cot_own_z(2)
-    piece_rows(0)
-    query_from(1)
-    swap_forward(1)
-    swap_send(3)
-    query_from(2)
-    swap_ready(0)
-    cot_own_x(1)
-    query_all()
-    swap_ready(1)
     cot_own_z(3)
-    swap_forward(2)
-    hidden_units()
-
-    part_at = (0, 2, 3, 6, 8, 9, 13, 20)
-    pair_at = (1, 4, 6, 7, 11, 15, 16, 21)
-    pass_at = (5, 9, 10, 14, 16, 17, 19, 23)
-    final_at = (12, 14, 17, 18, 20, 22, 24, 25)
-
-    def item_of(s, places):
-        number = jnp.int32(-1)
-        for item, place in enumerate(places):
-            number = jnp.where(s == place, item, number)
-        return number
-
-    def main_step(s, carry):
-        def at(step):
-            return pl.when(s == step)
-
-        @at(1)
-        def _():
-            cot_own_twin(3)
-            grad_part(0)
-            cot_over_z(1)
-            hidden_part(0)
-            cot_over_x(2)
-            swap_ready(2)
-            grad_send(0, 1)
-            cot_over_z(2)
-            cot_over_x(1)
-
-        @at(2)
-        def _():
-            grad_send(0, 0)
-            swap_send(4)
-            cot_corner(1)
-
-        @at(3)
-        def _():
-            swap_forward(3)
-
-        @at(4)
-        def _():
-            piece_rows(1)
-            hidden_part(1)
-            grad_pair(0)
-            cot_over_z(3)
-            grad_part(1)
-            cot_corner(2)
-            swap_forward(4)
-            grad_send(1, 1)
-            piece_rows(2)
-            grad_send(1, 0)
-
-        @at(5)
-        def _():
-            swap_ready(3)
-            hidden_part(2)
-            grad_part(2)
-            grad_send(2, 0)
-            cot_corner(3)
-
-        @at(6)
-        def _():
-            piece_rows(3)
-            swap_ready(4)
-            hidden_part(3)
-            row_gradients()
-
-        @at(8)
-        def _():
-            grad_send(2, 1)
-            grad_pair(1)
-
-        @at(9)
-        def _():
-            gin_part()
-            grad_sum(0)
-            grad_pair(2)
-            grad_part(3)
-            grad_send(3, 1)
-            grad_send(3, 0)
-            back_second()
-
-        @at(12)
-        def _():
-            grad_send(PIECES, 1)
-            grad_send(PIECES, 0)
-            back_first_norm()
-
-        @at(13)
-        def _():
-            share_core(1)
-
-        @at(14)
-        def _():
-            share_core(0)
-
-        @at(15)
-        def _():
-            grad_pair(3)
-
-        @at(16)
-        def _():
-            grad_sum(2)
-
-        @at(17)
-        def _():
-            share_x(0)
-            share_x(1)
-            grad_sum(1)
-            grad_pair(PIECES)
-            grad_sum(3)
-
-        @at(18)
-        def _():
-            back_first_conv()
-
-        @at(19)
-        def _():
-            grad_last(0)
-
-        @at(20)
-        def _():
-            share_z(0)
-            share_core(2)
-
-        @at(21)
-        def _():
-            share_z(1)
-            share_x(2)
-            grad_last(2)
-
-        @at(22)
-        def _():
-            grad_sum(PIECES)
-            grad_last(1)
-
-        @at(23)
-        def _():
-            share_z(2)
-            back_first_rows()
-
-        @at(24)
-        def _():
-            share_y(0)
-            share_y(1)
-            grad_last(PIECES)
-            grad_last(3)
-
-        @at(25)
-        def _():
-            share_y(2)
-            share_twin(0)
-            share_twin(1)
-            share_twin(2)
-
-        for places, work in (
-            (part_at, item_part), (pair_at, item_pair), (pass_at, item_pass), (final_at, item_final)
-        ):
-            number = item_of(s, places)
-
-            @pl.when(number >= 0)
-            def _(number=number, work=work):
-                work(number)
-
-        return carry
-
-    lax.fori_loop(0, 26, main_step, 0)
+    cot_over_z(2)
+    swap_send(4)
+    item_pair(0)
+    cot_over_x(1)
+    cot_own_twin(3)
+    piece_rows(1)
+    item_part(1)
+    swap_forward(3)
+    swap_ready(2)
+    item_part(2)
+    cot_over_z(3)
+    grad_part(1)
+    swap_forward(4)
+    grad_send(1, 0)
+    item_pass(0)
+    hidden_part(1)
+    cot_corner(2)
+    item_pair(1)
+    grad_send(1, 1)
+    grad_pair(0)
+    item_part(3)
+    piece_rows(2)
+    item_pair(2)
+    grad_part(2)
+    swap_ready(3)
+    hidden_part(2)
+    cot_corner(3)
+    piece_rows(3)
+    item_pass(1)
+    grad_send(2, 1)
+    swap_ready(4)
+    grad_send(2, 0)
+    hidden_part(3)
+    row_gradients()
+    grad_pair(1)
+    item_pair(3)
+    grad_part(3)
+    grad_send(3, 1)
+    grad_pair(2)
+    item_pass(2)
+    grad_send(3, 0)
+    item_part(4)
+    item_pair(4)
+    grad_sum(1)
+    gin_part()
+    item_part(5)
+    grad_send(PIECES, 0)
+    item_part(6)
+    grad_send(PIECES, 1)
+    grad_pair(3)
+    back_second()
+    share_core(0)
+    item_pair(5)
+    item_part(7)
+    back_first_norm()
+    item_final(0)
+    item_pass(3)
+    share_x(0)
+    back_first_conv()
+    item_pass(4)
+    share_core(1)
+    grad_sum(0)
+    item_final(1)
+    grad_pair(PIECES)
+    item_pass(5)
+    share_core(2)
+    grad_sum(3)
+    item_final(2)
+    item_final(3)
+    grad_last(1)
+    share_x(1)
+    back_first_rows()
+    grad_last(0)
+    grad_sum(2)
+    share_z(0)
+    item_final(4)
+    item_pair(6)
+    grad_last(3)
+    share_x(2)
+    grad_sum(PIECES)
+    item_pass(6)
+    share_z(2)
+    item_final(5)
+    item_pair(7)
+    share_z(1)
+    grad_last(2)
+    share_y(0)
+    item_pass(7)
+    share_y(2)
+    share_y(1)
+    share_twin(0)
+    item_final(6)
+    grad_last(PIECES)
+    share_twin(2)
+    item_final(7)
+    share_twin(1)
 
     for p in range(3):
         share_done(p)
@@ -1489,7 +1426,7 @@
 VMEM_BYTES = 64 * 1024 * 1024
 
 
-FINISH = 8
+FINISH = 2
 
 
 def finish_kernel(

time: 209 us -> 202 us (0.967)
  Pallas kernels: 207 us -> 200 us
    pallas_call x1, Pallas kernels: 196 us -> 192 us  [layer_call(): pl.pallas_call(layer_kernel, out_shape=out_shape, in_specs=[any_space, sm...]
    pallas_call x1, Pallas kernels: 10.8 us -> 8.67 us  [finish_call(): pl.pallas_call(finish_kernel, grid=(FINISH,), out_shape=[shape(tokens.sha...]
where the time goes in v4:
time: 202 us
  Pallas kernels  200 us (99%)
    pallas_call x1, Pallas kernels, layer_call(): pl.pallas_call(layer_kernel, out_shape=out_shape, in_specs=[any_space, sm...  192 us
    pallas_call x1, Pallas kernels, finish_call(): pl.pallas_call(finish_kernel, grid=(FINISH,), out_shape=[shape(tokens.sha...  8.67 us

profile of v4, /device:TPU:0, one launch (start us, length us, event | category | flops | bytes accessed | tf_op | source)
XLA Modules:
  0.0 201.7 jit_solution(16860751617409178314)
XLA Ops:
  1.3 191.5 %shard_map.220 = (bf16[144,4096]{1,0:T(8,128)(2,1)}, f32[576,1024]{1,0:T(8,128)}, bf16[512,4096]{1,0:T(8,128)(2,1)}, bf16[1024,512]{1,0:T(8,128)(2,1)}, f32[2,2,...) custom-call(bf16[576,1024]{1,0:T(8,128)(2,1)} %patches_in.1, ...), custom_call_target="tpu_custom_call" | custom-call | tf_op jit(solution)/shard_map/pallas_call | solution.py:1412
  192.8 8.7 %shard_map.221 = (bf16[144,4096]{1,0:T(8,128)(2,1)}, f32[576,1024]{1,0:T(8,128)}, f32[512,4096]{1,0:T(8,128)}, f32[1024,512]{1,0:T(8,128)}, f32[32,1024]{1,0:T(8...) custom-call(bf16[144,4096]{1,0:T(8,128)(2,1)} %get-tuple-element.30., ...), custom_call_target="tpu_custom_call" | custom-call | tf_op jit(solution)/shard_map/pallas_call | solution.py:1467

commit v5 on v4

--- a/solution.py
+++ b/solution.py
@@ -769,6 +769,8 @@
 
         arrived(rl.at[i, 1], t_r.at[i, 1])
         arrived(rl.at[i, 2], t_r.at[i, 2])
+        for k in range(3):
+            left_here(ps.at[i, 0], t_s.at[i, k])
         tstage[b] = (
             ps[i, slot_own].astype(f32) + rl[i, 1].astype(f32) + rl[i, 2].astype(f32)
         ).astype(bf16)
@@ -841,6 +843,27 @@
             return carry
 
         lax.fori_loop(0, 5, one, 0)
+
+    def drain_first():
+        for b in range(4):
+            for k in range(15):
+                left_here(w_part(b, c, 0), w_s.at[b, k])
+        for k in range(4):
+            left_here(qs.at[0], q_s.at[k])
+        for k in range(3):
+            left_here(qs.at[0], q_cs.at[k])
+        for p in range(PIECES):
+            for slot in range(4):
+                left_here(cot(0, 0, p), dt_cs.at[p, slot])
+            for k in range(3):
+                left_here(cot(0, 0, p), dt_s.at[p, k])
+
+        for j in range(1 + PIECES):
+            @pl.when(jnp.logical_not(own))
+            def _(j=j):
+                part = w_half(swap_refs(j)[1], j, y)
+                left_here(part, sw_s.at[j])
+                left_here(part, sy_s.at[j])
 
     def grad_half(j, half):
         if j == PIECES:
@@ -1097,204 +1120,183 @@
         dy[...] += dot(dlow[...], reduce_weights(0), 1, 0)
         store_dpat.start()
 
+    w_own(1)
+    cot_own_twin(0)
+    cot_own_x(3)
+    cot_own_x(0)
     w_own(3)
-    cot_own_x(0)
+    cot_own_twin(3)
     w_own(0)
     w_own(2)
     cot_own_z(0)
-    w_own(1)
+    swap_send(0)
+    swap_send(1)
     w_forward(3)
-    cot_own_x(2)
-    cot_own_z(1)
+    w_forward(1)
+    w_forward(0)
     w_over(3)
     w_forward(2)
-    cot_own_twin(1)
-    swap_send(0)
-    swap_send(1)
-    w_forward(0)
+    w_finish(3)
+    cot_own_x(2)
+    w_over(0)
+    cot_own_z(1)
     swap_send(2)
-    w_forward(1)
-    w_over(2)
-    w_finish(3)
-    cot_over_z(0)
-    cot_own_x(3)
     w_over(1)
+    w_finish(0)
     w_finish(1)
-    w_over(0)
-    w_finish(0)
-    cot_over_x(2)
-    w_finish(2)
     first_conv()
     first_norm()
+    cot_over_z(0)
+    cot_own_twin(2)
+    cot_over_x(3)
     first_pool()
-    cot_own_twin(2)
+    w_over(2)
+    swap_forward(0)
+    w_finish(2)
+    swap_forward(1)
     second_forward()
+    query_to(2, corner)
+    query_twin()
+    query_to(1, z_peer)
+    query_to(0, x_peer)
     cot_corner(0)
-    swap_forward(0)
-    query_to(0, x_peer)
-    query_twin()
-    query_to(2, corner)
-    swap_ready(0)
-    query_to(1, z_peer)
+    swap_forward(2)
     cot_over_x(0)
-    swap_forward(1)
-    cot_own_twin(0)
     piece_rows(0)
     swap_ready(1)
+    swap_ready(0)
+    query_from(2)
+    swap_send(3)
     cot_own_z(2)
-    swap_send(3)
-    swap_forward(2)
+    cot_own_x(1)
     query_from(1)
-    query_from(2)
     query_from(0)
+    swap_send(4)
     cot_over_z(1)
     query_all()
     hidden_units()
 
-    cot_own_x(1)
     grad_part(0)
     grad_send(0, 0)
+    grad_send(0, 1)
+    cot_over_x(1)
+    cot_over_z(2)
+    cot_own_twin(1)
     item_part(0)
+    swap_ready(2)
+    cot_own_z(3)
     hidden_part(0)
-    grad_send(0, 1)
     cot_corner(1)
-    cot_over_x(3)
-    cot_own_z(3)
-    cot_over_z(2)
-    swap_send(4)
+    swap_forward(3)
+    piece_rows(1)
     item_pair(0)
-    cot_over_x(1)
-    cot_own_twin(3)
-    piece_rows(1)
     item_part(1)
-    swap_forward(3)
-    swap_ready(2)
+    grad_part(1)
     item_part(2)
+    grad_send(1, 0)
+    grad_pair(0)
+    cot_corner(2)
     cot_over_z(3)
-    grad_part(1)
+    cot_over_x(2)
+    item_pair(1)
+    swap_ready(3)
+    hidden_part(1)
+    item_part(3)
+    grad_send(1, 1)
+    piece_rows(2)
     swap_forward(4)
-    grad_send(1, 0)
-    item_pass(0)
-    hidden_part(1)
-    cot_corner(2)
-    item_pair(1)
-    grad_send(1, 1)
-    grad_pair(0)
-    item_part(3)
-    piece_rows(2)
-    item_pair(2)
     grad_part(2)
-    swap_ready(3)
     hidden_part(2)
     cot_corner(3)
+    item_pair(2)
+    item_pass(0)
+    grad_send(2, 0)
+    grad_send(2, 1)
+    item_pair(3)
+    item_pass(1)
+    grad_pair(1)
     piece_rows(3)
-    item_pass(1)
-    grad_send(2, 1)
+    item_part(4)
     swap_ready(4)
-    grad_send(2, 0)
     hidden_part(3)
     row_gradients()
-    grad_pair(1)
-    item_pair(3)
     grad_part(3)
     grad_send(3, 1)
+    item_pair(4)
+    item_part(5)
+    item_part(6)
     grad_pair(2)
-    item_pass(2)
+    item_final(0)
+    item_pair(5)
     grad_send(3, 0)
-    item_part(4)
-    item_pair(4)
     grad_sum(1)
     gin_part()
-    item_part(5)
-    grad_send(PIECES, 0)
-    item_part(6)
-    grad_send(PIECES, 1)
+    item_final(1)
+    item_pass(2)
     grad_pair(3)
+    item_pair(6)
+    drain_first()
     back_second()
     share_core(0)
-    item_pair(5)
+    grad_send(PIECES, 0)
+    grad_send(PIECES, 1)
+    item_pass(3)
+    grad_sum(0)
+    back_first_norm()
+    item_pass(4)
     item_part(7)
-    back_first_norm()
-    item_final(0)
-    item_pass(3)
-    share_x(0)
     back_first_conv()
-    item_pass(4)
-    share_core(1)
-    grad_sum(0)
-    item_final(1)
-    grad_pair(PIECES)
-    item_pass(5)
     share_core(2)
     grad_sum(3)
+    share_x(0)
+    grad_sum(2)
+    grad_pair(PIECES)
+    share_core(1)
+    share_x(2)
+    item_pass(5)
+    share_z(0)
+    share_x(1)
+    grad_sum(PIECES)
+    item_pass(6)
+    grad_last(1)
+    grad_last(0)
     item_final(2)
     item_final(3)
-    grad_last(1)
-    share_x(1)
+    item_pair(7)
+    item_final(4)
+    item_final(5)
     back_first_rows()
-    grad_last(0)
-    grad_sum(2)
-    share_z(0)
-    item_final(4)
-    item_pair(6)
+    share_z(2)
     grad_last(3)
-    share_x(2)
-    grad_sum(PIECES)
-    item_pass(6)
-    share_z(2)
-    item_final(5)
-    item_pair(7)
+    item_final(6)
     share_z(1)
+    share_y(0)
+    share_y(2)
+    grad_last(PIECES)
+    item_pass(7)
+    share_y(1)
     grad_last(2)
-    share_y(0)
-    item_pass(7)
-    share_y(2)
-    share_y(1)
+    share_twin(2)
     share_twin(0)
-    item_final(6)
-    grad_last(PIECES)
-    share_twin(2)
+    share_twin(1)
+    for j in range(3):
+        grad_done(j)
+    for p in range(2):
+        share_done(p)
     item_final(7)
-    share_twin(1)
-
-    for p in range(3):
-        share_done(p)
-    for j in range(1 + PIECES):
+
+    share_done(2)
+    for j in range(3, 1 + PIECES):
         grad_done(j)
-
-        @pl.when(jnp.logical_not(own))
-        def _():
-            part = w_half(swap_refs(j)[1], j, y)
-            left_here(part, sw_s.at[j])
-            left_here(part, sy_s.at[j])
 
     store_dpat.wait()
     for b in range(2):
         pltpu.make_async_copy(tstage.at[b], tok_slice(b), gl.at[8 + b]).wait()
         left_here(tp.at[b], t_cs.at[b])
-    for b in range(4):
-        for k in range(15):
-            left_here(w_part(b, c, 0), w_s.at[b, k])
-    for k in range(4):
-        left_here(qs.at[0], q_s.at[k])
-    for k in range(3):
-        left_here(qs.at[0], q_cs.at[k])
     for k in range(4):
         left_here(dps.at[0, 0], d_cs.at[k])
     for k in range(3):
         left_here(dps.at[0, 0], d_zs.at[k])
-    for p in range(PIECES):
-        for slot in range(4):
-            left_here(cot(0, 0, p), dt_cs.at[p, slot])
-        for k in range(3):
-            left_here(cot(0, 0, p), dt_s.at[p, k])
-
-    def drain_items(i, carry):
-        for k in range(3):
-            left_here(ps.at[0, 0], t_s.at[i, k])
-        return carry
-
-    lax.fori_loop(0, CHUNKS, drain_items, 0)
 
 
 def layer_call(

time: 202 us -> 196 us (0.970)
  Pallas kernels: 200 us -> 194 us
    pallas_call x1, Pallas kernels: 192 us -> 185 us  [layer_call(): pl.pallas_call(layer_kernel, out_shape=out_shape, in_specs=[any_space, sm...]
where the time goes in v5:
time: 196 us; the launch traced here: 195 us
  Pallas kernels  194 us (99%)
    pallas_call x1, Pallas kernels, layer_call(): pl.pallas_call(layer_kernel, out_shape=out_shape, in_specs=[any_space, sm...  185 us
    pallas_call x1, Pallas kernels, finish_call(): pl.pallas_call(finish_kernel, grid=(FINISH,), out_shape=[shape(tokens.sha...  8.67 us

profile of v5, /device:TPU:0, one launch (start us, length us, event | category | flops | bytes accessed | tf_op | source)
XLA Modules:
  0.0 195.4 jit_solution(17707160688616566889)
XLA Ops:
  1.3 185.2 %shard_map.220 = (bf16[144,4096]{1,0:T(8,128)(2,1)}, f32[576,1024]{1,0:T(8,128)}, bf16[512,4096]{1,0:T(8,128)(2,1)}, bf16[1024,512]{1,0:T(8,128)(2,1)}, f32[2,2,...) custom-call(bf16[576,1024]{1,0:T(8,128)(2,1)} %patches_in.1, ...), custom_call_target="tpu_custom_call" | custom-call | tf_op jit(solution)/shard_map/pallas_call | solution.py:1414
  186.5 8.7 %shard_map.221 = (bf16[144,4096]{1,0:T(8,128)(2,1)}, f32[576,1024]{1,0:T(8,128)}, f32[512,4096]{1,0:T(8,128)}, f32[1024,512]{1,0:T(8,128)}, f32[32,1024]{1,0:T(8...) custom-call(bf16[144,4096]{1,0:T(8,128)(2,1)} %get-tuple-element.30., ...), custom_call_target="tpu_custom_call" | custom-call | tf_op jit(solution)/shard_map/pallas_call | solution.py:1469

commit v6 on v5

--- a/solution.py
+++ b/solution.py
@@ -1120,162 +1120,162 @@
         dy[...] += dot(dlow[...], reduce_weights(0), 1, 0)
         store_dpat.start()
 
-    w_own(1)
-    cot_own_twin(0)
-    cot_own_x(3)
     cot_own_x(0)
     w_own(3)
-    cot_own_twin(3)
+    w_own(1)
     w_own(0)
+    cot_own_z(0)
+    cot_own_x(3)
+    w_forward(3)
     w_own(2)
-    cot_own_z(0)
     swap_send(0)
     swap_send(1)
-    w_forward(3)
     w_forward(1)
+    swap_send(2)
     w_forward(0)
+    cot_own_x(2)
     w_over(3)
-    w_forward(2)
     w_finish(3)
-    cot_own_x(2)
+    cot_own_twin(1)
+    cot_over_x(0)
     w_over(0)
     cot_own_z(1)
-    swap_send(2)
+    w_finish(0)
     w_over(1)
-    w_finish(0)
+    w_forward(2)
+    first_conv()
     w_finish(1)
-    first_conv()
     first_norm()
     cot_over_z(0)
     cot_own_twin(2)
-    cot_over_x(3)
+    w_over(2)
     first_pool()
-    w_over(2)
+    cot_own_twin(0)
+    w_finish(2)
+    second_forward()
     swap_forward(0)
-    w_finish(2)
+    query_to(0, x_peer)
+    query_twin()
+    query_to(2, corner)
     swap_forward(1)
-    second_forward()
-    query_to(2, corner)
-    query_twin()
     query_to(1, z_peer)
-    query_to(0, x_peer)
+    swap_ready(0)
     cot_corner(0)
-    swap_forward(2)
-    cot_over_x(0)
     piece_rows(0)
-    swap_ready(1)
-    swap_ready(0)
+    query_from(0)
     query_from(2)
     swap_send(3)
+    swap_ready(1)
+    swap_forward(2)
     cot_own_z(2)
     cot_own_x(1)
     query_from(1)
-    query_from(0)
+    query_all()
+    cot_over_z(1)
     swap_send(4)
-    cot_over_z(1)
-    query_all()
     hidden_units()
 
     grad_part(0)
+    grad_send(0, 1)
+    item_part(0)
+    hidden_part(0)
     grad_send(0, 0)
-    grad_send(0, 1)
     cot_over_x(1)
+    swap_forward(3)
+    cot_own_z(3)
     cot_over_z(2)
-    cot_own_twin(1)
-    item_part(0)
-    swap_ready(2)
-    cot_own_z(3)
-    hidden_part(0)
+    cot_over_x(3)
     cot_corner(1)
-    swap_forward(3)
     piece_rows(1)
     item_pair(0)
+    grad_part(1)
+    grad_send(1, 1)
+    grad_send(1, 0)
     item_part(1)
-    grad_part(1)
-    item_part(2)
-    grad_send(1, 0)
-    grad_pair(0)
+    cot_over_x(2)
+    swap_ready(3)
+    swap_ready(2)
     cot_corner(2)
     cot_over_z(3)
-    cot_over_x(2)
+    cot_own_twin(3)
+    grad_pair(0)
+    item_part(2)
     item_pair(1)
-    swap_ready(3)
+    item_part(3)
+    swap_forward(4)
+    item_pass(0)
     hidden_part(1)
-    item_part(3)
-    grad_send(1, 1)
     piece_rows(2)
-    swap_forward(4)
     grad_part(2)
-    hidden_part(2)
     cot_corner(3)
     item_pair(2)
-    item_pass(0)
+    item_pair(3)
     grad_send(2, 0)
+    hidden_part(2)
     grad_send(2, 1)
-    item_pair(3)
+    grad_pair(1)
+    item_part(4)
     item_pass(1)
-    grad_pair(1)
     piece_rows(3)
-    item_part(4)
+    grad_part(3)
+    grad_send(3, 1)
     swap_ready(4)
     hidden_part(3)
     row_gradients()
-    grad_part(3)
-    grad_send(3, 1)
+    item_final(0)
     item_pair(4)
+    grad_send(3, 0)
+    gin_part()
+    grad_sum(1)
+    grad_pair(2)
     item_part(5)
     item_part(6)
-    grad_pair(2)
-    item_final(0)
     item_pair(5)
-    grad_send(3, 0)
-    grad_sum(1)
-    gin_part()
-    item_final(1)
-    item_pass(2)
     grad_pair(3)
-    item_pair(6)
     drain_first()
     back_second()
+    item_pass(2)
+    item_pass(3)
+    grad_last(1)
+    grad_send(PIECES, 1)
+    item_pass(4)
     share_core(0)
     grad_send(PIECES, 0)
-    grad_send(PIECES, 1)
-    item_pass(3)
     grad_sum(0)
+    item_pair(6)
     back_first_norm()
-    item_pass(4)
-    item_part(7)
     back_first_conv()
     share_core(2)
+    share_x(0)
+    item_final(1)
     grad_sum(3)
-    share_x(0)
     grad_sum(2)
     grad_pair(PIECES)
+    share_x(2)
     share_core(1)
-    share_x(2)
+    item_part(7)
     item_pass(5)
     share_z(0)
+    item_pass(6)
+    item_final(2)
+    item_final(3)
+    item_final(4)
+    grad_last(0)
+    item_final(5)
     share_x(1)
     grad_sum(PIECES)
-    item_pass(6)
-    grad_last(1)
-    grad_last(0)
-    item_final(2)
-    item_final(3)
-    item_pair(7)
-    item_final(4)
-    item_final(5)
     back_first_rows()
     share_z(2)
-    grad_last(3)
     item_final(6)
+    item_pair(7)
     share_z(1)
     share_y(0)
+    grad_last(2)
     share_y(2)
     grad_last(PIECES)
+    grad_last(3)
     item_pass(7)
     share_y(1)
-    grad_last(2)
     share_twin(2)
     share_twin(0)
     share_twin(1)

time: 196 us -> 209 us (1.066)
  Pallas kernels: 194 us -> 207 us
    pallas_call x1, Pallas kernels: 185 us -> 199 us  [layer_call(): pl.pallas_call(layer_kernel, out_shape=out_shape, in_specs=[any_space, sm...]
where the time goes in v6:
time: 209 us
  Pallas kernels  207 us (99%)
    pallas_call x1, Pallas kernels, layer_call(): pl.pallas_call(layer_kernel, out_shape=out_shape, in_specs=[any_space, sm...  199 us
    pallas_call x1, Pallas kernels, finish_call(): pl.pallas_call(finish_kernel, grid=(FINISH,), out_shape=[shape(tokens.sha...  8.67 us

profile of v6, /device:TPU:0, one launch (start us, length us, event | category | flops | bytes accessed | tf_op | source)
XLA Modules:
  0.0 208.9 jit_solution(18105294204247942551)
XLA Ops:
  1.3 198.8 %shard_map.220 = (bf16[144,4096]{1,0:T(8,128)(2,1)}, f32[576,1024]{1,0:T(8,128)}, bf16[512,4096]{1,0:T(8,128)(2,1)}, bf16[1024,512]{1,0:T(8,128)(2,1)}, f32[2,2,...) custom-call(bf16[576,1024]{1,0:T(8,128)(2,1)} %patches_in.1, ...), custom_call_target="tpu_custom_call" | custom-call | tf_op jit(solution)/shard_map/pallas_call | solution.py:1414
  200.1 8.7 %shard_map.221 = (bf16[144,4096]{1,0:T(8,128)(2,1)}, f32[576,1024]{1,0:T(8,128)}, f32[512,4096]{1,0:T(8,128)}, f32[1024,512]{1,0:T(8,128)}, f32[32,1024]{1,0:T(8...) custom-call(bf16[144,4096]{1,0:T(8,128)(2,1)} %get-tuple-element.30., ...), custom_call_target="tpu_custom_call" | custom-call | tf_op jit(solution)/shard_map/pallas_call | solution.py:1469
